TPU v7x, 128 devices: a whole 4x4x4 slice. The times are simulated.
128 devices in a mesh: ctx: 16 (over x_lo, z, core), wsh: 8 (over x_hi, y).
Axes of the slice: x: 4 (x_hi: 2, x_lo: 2; x = x_hi * 2 + x_lo), y: 4, z: 4, core: 2. Of those that a mesh axis runs over, the one named last changes fastest.
Arguments:
- hidden: bfloat16 [8, 2048, 1152], P('wsh', 'ctx'), may hold values from -36 to 36
- w_qkv: bfloat16 [1536, 1152], P('wsh'), may hold values from -0.1875 to 0.1875
- w_out: bfloat16 [1024, 1152], P('wsh'), may hold values from -0.1875 to 0.1875
- norm_gains: bfloat16 [1152, 4], P('wsh'), may hold values from 0.25 to 1.75
- qk_gains: bfloat16 [256, 2], P('wsh'), may hold values from 0.25 to 1.75
- w_gate_up: bfloat16 [6912, 2, 1152], P('wsh'), may hold values from -0.1875 to 0.1875
- w_down: bfloat16 [6912, 1152], P('wsh'), may hold values from -0.078125 to 0.078125
- cotangent: bfloat16 [8, 2048, 1152], P('wsh', 'ctx'), may hold values from -6 to 6
Outputs:
- out_hidden: bfloat16 [8, 2048, 1152], P('wsh', 'ctx')
- grad_hidden: bfloat16 [8, 2048, 1152], P('wsh', 'ctx')
- grad_qkv: float32 [1536, 1152], P('wsh')
- grad_out: float32 [1024, 1152], P('wsh')
- grad_norm_gains: float32 [1152, 4], P('wsh')
- grad_qk_gains: float32 [256, 2], P('wsh')
- grad_gate_up: float32 [6912, 2, 1152], P('wsh')
- grad_down: float32 [6912, 1152], P('wsh')
All inputs are finite; a program needn't handle non-finite values.
Results may differ from a plain program's by a relative error of at most 0.025.
Values may be sent and summed in bfloat16 or wider, within the bound.
A program may use at most 256 MiB of HBM per device.

v0:
```python
import jax
import jax.numpy as jnp
from jax import lax
from jax.sharding import PartitionSpec as P

HEADS = 4
HD = 256
KB = 512


epsilon = 1e-06
rope_base = 1000000.0
masked_value = -1e30


def rms_scale(values):
    return lax.rsqrt(jnp.mean(values * values, axis=-1, keepdims=True) + epsilon)


def scaled_norm(values, gain):
    return values * rms_scale(values) * gain


def post_add(resid, branch, gain):
    return resid + branch * rms_scale(branch) * gain


def rotate(values, cosine, sine):
    half = values.shape[-1] // 2
    turned = jnp.concatenate([-values[..., half:], values[..., :half]], axis=-1)
    return values * cosine + turned * sine


def rope_tables(positions, head_dim):
    freqs = rope_base ** (-jnp.arange(0, head_dim, 2, dtype=jnp.float32) / head_dim)
    angles = positions.astype(jnp.float32)[:, None] * freqs[None, :]
    angles = jnp.concatenate([angles, angles], axis=-1)
    return (jnp.cos(angles), jnp.sin(angles))


def prepare(mixed_qk, qk_gain, cosine, sine):
    count = mixed_qk.shape[0]
    queries = mixed_qk[:, : HEADS * HD].reshape(count, HEADS, HD)
    keys = mixed_qk[:, HEADS * HD :]
    queries = rotate(
        scaled_norm(queries, qk_gain[:, 0]), cosine[:, None, :], sine[:, None, :]
    ) * HD ** (-0.5)
    keys = rotate(scaled_norm(keys, qk_gain[:, 1]), cosine, sine)
    return (queries, keys)


def gating(gate, up):
    return jax.nn.gelu(gate, approximate=True) * up


def on_device(hidden, w_qkv, w_out, norm_gains, qk_gains, w_gate_up, w_down, cotangent):
    token_count = hidden.shape[1]
    offset = lax.axis_index("ctx") * token_count
    seq_len = token_count * lax.axis_size("ctx")
    inputs = hidden[0].astype(jnp.float32)
    positions = offset + jnp.arange(token_count, dtype=jnp.int32)
    cosine, sine = rope_tables(positions, HD)
    full_qkv, full_out, gains_low, qk_low = (
        lax.all_gather(w_qkv, "wsh", axis=0, tiled=True),
        lax.all_gather(w_out, "wsh", axis=0, tiled=True),
        lax.all_gather(norm_gains, "wsh", axis=0, tiled=True),
        lax.all_gather(qk_gains, "wsh", axis=0, tiled=True),
    )
    gains = gains_low.astype(jnp.float32)
    qk_gain = qk_low.astype(jnp.float32)
    normed_f32, input_pull = jax.vjp(scaled_norm, inputs, gains[:, 0])
    normed = normed_f32.astype(jnp.bfloat16)
    mixed = jnp.dot(normed, full_qkv.T, preferred_element_type=jnp.float32)
    split_at = (HEADS + 1) * HD

    def prepare_local(block_cols, gain):
        return prepare(block_cols, gain, cosine, sine)

    (queries, keys), prep_pull = jax.vjp(prepare_local, mixed[:, :split_at], qk_gain)
    query_low = queries.astype(jnp.bfloat16)
    local_kv = jnp.concatenate(
        [keys.astype(jnp.bfloat16), mixed[:, split_at:].astype(jnp.bfloat16)], axis=1
    )
    whole_kv = lax.all_gather(local_kv, "ctx", axis=0, tiled=True)
    block_count = (offset + token_count - 1) // KB + 1

    def block_scores(index):
        block = lax.dynamic_slice_in_dim(whole_kv, index * KB, KB, 0)
        scores = jnp.einsum(
            "thd,kd->htk", query_low, block[:, :HD], preferred_element_type=jnp.float32
        )
        allowed = (index * KB + jnp.arange(KB, dtype=jnp.int32))[None, :] <= positions[:, None]
        return (jnp.where(allowed[None], scores, masked_value), block)

    def max_step(index, carry):
        running_max, running_sum = carry
        scores, block = block_scores(index)
        new_max = jnp.maximum(running_max, jnp.max(scores, axis=-1))
        running_sum = running_sum * jnp.exp(running_max - new_max) + jnp.sum(
            jnp.exp(scores - new_max[..., None]), axis=-1
        )
        return (new_max, running_sum)

    start_max = jnp.full((HEADS, token_count), masked_value, jnp.float32)
    running_max, running_sum = lax.fori_loop(
        0, block_count, max_step, (start_max, jnp.zeros((HEADS, token_count), jnp.float32))
    )
    log_total = running_max + jnp.log(running_sum)

    def out_step(index, accum):
        scores, block = block_scores(index)
        probs = jnp.exp(scores - log_total[..., None]).astype(jnp.bfloat16)
        return accum + jnp.einsum(
            "htk,kd->thd", probs, block[:, HD:], preferred_element_type=jnp.float32
        )

    attended = lax.fori_loop(
        0, block_count, out_step, jnp.zeros((token_count, HEADS, HD), jnp.float32)
    )
    attended = attended.reshape(token_count, HEADS * HD).astype(jnp.bfloat16)
    branch = jnp.dot(attended, full_out, preferred_element_type=jnp.float32)
    resid, attn_pull = jax.vjp(post_add, inputs, branch, gains[:, 1])
    normed2_f32, pre_pull = jax.vjp(scaled_norm, resid, gains[:, 2])
    normed2 = normed2_f32.astype(jnp.bfloat16)
    gate_up = jnp.einsum(
        "td,fcd->ctf",
        normed2,
        lax.all_gather(w_gate_up, "wsh", axis=0, tiled=True),
        preferred_element_type=jnp.float32,
    )
    inner_f32, gate_pull = jax.vjp(gating, gate_up[0], gate_up[1])
    inner = inner_f32.astype(jnp.bfloat16)
    columns = inner
    branch2 = jnp.dot(
        columns,
        lax.all_gather(w_down, "wsh", axis=0, tiled=True),
        preferred_element_type=jnp.float32,
    )
    output, out_pull = jax.vjp(post_add, resid, branch2, gains[:, 3])
    cot_rows = cotangent[0].astype(jnp.float32)
    d_resid, d_branch2, grad_gain3 = out_pull(cot_rows)
    grad_low = d_branch2.astype(jnp.bfloat16)
    d_inner = jnp.einsum(
        "td,fd->tf",
        grad_low,
        lax.all_gather(w_down, "wsh", axis=0, tiled=True),
        preferred_element_type=jnp.float32,
    )
    d_gate, d_up = gate_pull(d_inner)
    d_gate_up = jnp.stack([d_gate, d_up]).astype(jnp.bfloat16)
    columns = d_gate_up
    d_normed2 = jnp.einsum(
        "ctf,fcd->td",
        columns,
        lax.all_gather(w_gate_up, "wsh", axis=0, tiled=True),
        preferred_element_type=jnp.float32,
    )
    columns = d_gate_up
    term_gate = jnp.einsum("ctf,td->fcd", columns, normed2, preferred_element_type=jnp.float32)
    term_down = jnp.einsum("tf,td->fd", inner, grad_low, preferred_element_type=jnp.float32)
    shares = lax.psum_scatter(
        jnp.concatenate([term_gate, term_down[:, None, :]], axis=1).astype(jnp.bfloat16),
        "wsh",
        scatter_dimension=0,
        tiled=True,
    ).astype(jnp.float32)
    grad_gu_part = shares[:, :2]
    grad_down_part = shares[:, 2]
    d_resid_more, grad_gain2 = pre_pull(d_normed2)
    d_inputs, d_branch, grad_gain1 = attn_pull(d_resid + d_resid_more)
    branch_low = d_branch.astype(jnp.bfloat16)
    grad_out_full = jnp.einsum(
        "tk,td->kd", attended, branch_low, preferred_element_type=jnp.float32
    )
    d_attended = jnp.einsum("td,kd->tk", branch_low, full_out, preferred_element_type=jnp.float32)
    d_attended = d_attended.astype(jnp.bfloat16).reshape(token_count, HEADS, HD)

    def delta_step(index, delta):
        scores, block = block_scores(index)
        probs = jnp.exp(scores - log_total[..., None])
        d_probs = jnp.einsum(
            "thd,kd->htk", d_attended, block[:, HD:], preferred_element_type=jnp.float32
        )
        return delta + jnp.sum(probs * d_probs, axis=-1)

    delta = lax.fori_loop(0, block_count, delta_step, jnp.zeros((HEADS, token_count), jnp.float32))

    def grad_step(index, carry):
        d_queries, d_kv = carry
        scores, block = block_scores(index)
        probs = jnp.exp(scores - log_total[..., None])
        d_probs = jnp.einsum(
            "thd,kd->htk", d_attended, block[:, HD:], preferred_element_type=jnp.float32
        )
        d_scores = (probs * (d_probs - delta[..., None])).astype(jnp.bfloat16)
        d_queries = d_queries + jnp.einsum(
            "htk,kd->thd", d_scores, block[:, :HD], preferred_element_type=jnp.float32
        )
        d_keys = jnp.einsum("htk,thd->kd", d_scores, query_low, preferred_element_type=jnp.float32)
        d_values = jnp.einsum(
            "htk,thd->kd",
            probs.astype(jnp.bfloat16),
            d_attended,
            preferred_element_type=jnp.float32,
        )
        current = lax.dynamic_slice_in_dim(d_kv, index * KB, KB, 0)
        d_kv = lax.dynamic_update_slice_in_dim(
            d_kv, current + jnp.concatenate([d_keys, d_values], axis=1), index * KB, 0
        )
        return (d_queries, d_kv)

    start_grads = (
        jnp.zeros((token_count, HEADS, HD), jnp.float32),
        jnp.zeros((seq_len, 2 * HD), jnp.float32),
    )
    d_queries, d_kv = lax.fori_loop(0, block_count, grad_step, start_grads)
    own_kv = lax.psum_scatter(
        d_kv.astype(jnp.bfloat16), "ctx", scatter_dimension=0, tiled=True
    ).astype(jnp.float32)
    d_qk, grad_qk = prep_pull((d_queries, own_kv[:, :HD]))
    d_mixed = jnp.concatenate([d_qk, own_kv[:, HD:]], axis=1).astype(jnp.bfloat16)
    grad_qkv_full = jnp.einsum("tr,td->rd", d_mixed, normed, preferred_element_type=jnp.float32)
    d_normed = jnp.dot(d_mixed, full_qkv, preferred_element_type=jnp.float32)
    d_input_more, grad_gain0 = input_pull(d_normed)
    grad_inputs = (d_inputs + d_input_more).astype(jnp.bfloat16)
    gain_grads = jnp.stack([grad_gain0, grad_gain1, grad_gain2, grad_gain3], axis=1)
    part_qkv, part_out, part_gains, part_qk = (
        lax.psum_scatter(
            grad_qkv_full.astype(jnp.bfloat16), "wsh", scatter_dimension=0, tiled=True
        ).astype(jnp.float32),
        lax.psum_scatter(
            grad_out_full.astype(jnp.bfloat16), "wsh", scatter_dimension=0, tiled=True
        ).astype(jnp.float32),
        lax.psum_scatter(
            gain_grads.astype(jnp.bfloat16), "wsh", scatter_dimension=0, tiled=True
        ).astype(jnp.float32),
        lax.psum_scatter(
            grad_qk.astype(jnp.bfloat16), "wsh", scatter_dimension=0, tiled=True
        ).astype(jnp.float32),
    )
    summed = (
        lax.psum(part_qkv.astype(jnp.bfloat16), "ctx").astype(jnp.float32),
        lax.psum(part_out.astype(jnp.bfloat16), "ctx").astype(jnp.float32),
        lax.psum(part_gains.astype(jnp.bfloat16), "ctx").astype(jnp.float32),
        lax.psum(part_qk.astype(jnp.bfloat16), "ctx").astype(jnp.float32),
        lax.psum(grad_gu_part.astype(jnp.bfloat16), "ctx").astype(jnp.float32),
        lax.psum(grad_down_part.astype(jnp.bfloat16), "ctx").astype(jnp.float32),
    )
    return (
        output.astype(jnp.bfloat16)[None],
        grad_inputs[None],
        summed[0],
        summed[1],
        summed[2],
        summed[3],
        summed[4],
        summed[5],
    )


def solution(mesh):
    return jax.shard_map(
        on_device,
        mesh=mesh,
        in_specs=(
            P("wsh", "ctx", None),
            P("wsh", None),
            P("wsh", None),
            P("wsh", None),
            P("wsh", None),
            P("wsh", None, None),
            P("wsh", None),
            P("wsh", "ctx", None),
        ),
        out_specs=(
            P("wsh", "ctx", None),
            P("wsh", "ctx", None),
            P("wsh", None),
            P("wsh", None),
            P("wsh", None),
            P("wsh", None),
            P("wsh", None, None),
            P("wsh", None),
        ),
        check_vma=False,
    )
```

profile of v0, /device:TPU:0, one launch (start us, length us, event | category | flops | bytes accessed | tf_op | source)
XLA Modules:
  0.0 1816.7 jit_solution(9382442562186543173)
XLA Ops:
  8.0 23.7 %all-gather.1 = bf16[8,32,2]{1,2,0:T(2,128)(2,1)S(1)} all-gather(bf16[1,32,2]{1,2,0:T(2,128)(2,1)} %bitcast.275), channel_id=1, replica_groups=mesh['ctx'=16,'wsh'=8] {'wsh'}, dimensions={0}, use_global_device_ids=true | all-gather | bytes 1152 | tf_op jit(solution)/shard_map/all_gather | solution.py:67
  31.8 29.8 %all-gather = bf16[8,144,4]{1,2,0:T(4,128)(2,1)S(1)} all-gather(bf16[1,144,4]{1,2,0:T(4,128)(2,1)} %bitcast.274), channel_id=1, replica_groups=mesh['ctx'=16,'wsh'=8] {'wsh'}, dimensions={0}, use_global_device_ids=true | all-gather | bytes 10368 | tf_op jit(solution)/shard_map/all_gather | solution.py:66
  61.8 1.1 fusion.60
  63.0 15.7 all-gather.8.cloned.1.call-done
  78.7 3.4 fusion.76
  84.4 4.6 copy.150
  91.6 24.3 %all-gather.10.cloned.1.call-done = bf16[2048,512]{1,0:T(8,128)(2,1)} async-done(((bf16[128,512]{1,0:T(8,128)(2,1)}), bf16[2048,512]{1,0:T(8,128)(2,1)}) %all-gather.10.cloned.1.call-update) | async-done | bytes 2097168 | tf_op jit(solution)/shard_map/all_gather | solution.py:84
  115.9 1.7 while.48
  116.1 1.3 fusion.138
  117.6 2.0 while.49
  117.8 1.6 fusion.140
  119.8 54.2 %all-gather.12.cloned.1.call-done = bf16[1024,1152]{1,0:T(8,128)(2,1)} async-done(((bf16[128,1152]{1,0:T(8,128)(2,1)}), bf16[1024,1152]{1,0:T(8,128)(2,1)}) %all-gather.12.cloned.1.call-update) | async-done | bytes 2359312 | tf_op jit(solution)/shard_map/all_gather | solution.py:65
  174.0 2.3 multiply_reduce_fusion.6
  176.6 316.7 %all-gather.14.cloned.1.call-done = bf16[6912,2,1152]{2,0,1:T(8,128)(2,1)} async-done(((bf16[864,2,1152]{2,0,1:T(8,128)(2,1)}), bf16[6912,2,1152]{2,0,1:T(8,128)(2,1)}) %all-gather.14.cloned.1.call-update) | async-done | bytes 31850512 | tf_op jit(solution)/shard_map/all_gather | solution.py:128
  493.3 16.5 convolution_bitcast_fusion.10
  509.8 3.0 copy-done
  512.7 2.4 multiply_convert_fusion.1
  515.2 153.2 %all-gather.16.cloned.1.call-done = bf16[6912,1152]{1,0:T(8,128)(2,1)} async-done(((bf16[864,1152]{1,0:T(8,128)(2,1)}), bf16[6912,1152]{1,0:T(8,128)(2,1)}) %all-gather.16.cloned.1.call-update) | async-done | bytes 15925264 | tf_op jit(solution)/shard_map/all_gather | solution.py:136
  668.3 8.7 multiply_reduce_fusion.4
  677.1 0.8 fusion.59
  677.9 1.0 fusion.55
  678.9 10.3 fusion.47
  689.2 16.3 fusion.37
  705.5 15.1 multiply_reduce_fusion
  721.3 1.2 copy-done.10
  722.5 0.9 convolution_convert_fusion.4
  723.6 2.9 while.50
  723.8 1.3 convolution_bitcast_fusion.15
  725.1 1.4 fusion.143
  726.6 2.5 broadcast_in_dim.107.clone
  729.1 8.7 while.51
  729.3 1.3 fusion.151
  730.6 1.3 fusion.152
  732.5 1.3 fusion.153
  733.8 0.8 copy-done.2
  734.6 1.3 constant_dynamic-slice_fusion.2
  736.8 1.0 constant_dynamic-update-slice_fusion.2
  737.9 3.9 convert_element_type.138
  741.9 7.8 fusion.38
  749.7 32.4 %pad_maximum_fusion = bf16[6912,3,1152]{0,2,1:T(8,128)(2,1)} fusion(bf16[6912,1,1152]{0,2,1:T(8,128)(2,1)} %fusion.38, bf16[6912,2,1152]{0,2,1:T(8,128)(2,1)} %fusion.37), kind=kLoop, calls=%fused_computation.66 | loop fusion | flops 23887872 | bytes 95551488 | tf_op jit(solution)/shard_map/concatenate | solution.py:162
  782.1 57.1 %copy.184 = bf16[6912,3456]{1,0:T(8,128)(2,1)} copy(bf16[6912,3456]{0,1:T(8,128)(2,1)} %bitcast.255) | data formatting | bytes 95551488
  840.2 2.1 convolution_convert_fusion.3
  842.5 1.3 convert_multiply_fusion.6
  843.9 1.2 multiply_reduce_fusion.10
  845.1 1.2 add_add_fusion.5
  847.6 2.9 convolution_convert_fusion.2
  850.7 2.8 fusion.53
  854.4 0.9 copy.178
  855.3 488.8 %reduce-scatter.23.cloned.1.call-done = bf16[864,3456]{1,0:T(8,128)(2,1)} async-done(((bf16[6912,3456]{1,0:T(8,128)(2,1)}), bf16[864,3456]{1,0:T(8,128)(2,1)}) %reduce-scatter.23.cloned.1.call-update) | async-done | bytes 5971984
  1344.1 9.2 copy.185
  1353.3 3.1 slice_bitcast_fusion.2
  1356.4 4.4 slice.133
  1360.8 62.7 %reduce-scatter.17.cloned.1.call-done = bf16[128,1152]{1,0:T(8,128)(2,1)} async-done(((bf16[1024,1152]{1,0:T(8,128)(2,1)}), bf16[128,1152]{1,0:T(8,128)(2,1)}) %reduce-scatter.17.cloned.1.call-update) | async-done | bytes 294928 | tf_op jit(solution)/shard_map/reduce_scatter | solution.py:231
  1423.5 84.7 %reduce-scatter.15.cloned.1.call-done = bf16[192,1152]{1,0:T(8,128)(2,1)} async-done(((bf16[1536,1152]{1,0:T(8,128)(2,1)}), bf16[192,1152]{1,0:T(8,128)(2,1)}) %reduce-scatter.15.cloned.1.call-update) | async-done | bytes 442384 | tf_op jit(solution)/shard_map/reduce_scatter | solution.py:228
  1508.2 0.9 fusion.67
  1509.1 70.7 %reduce-scatter.21.cloned.1.call-done = bf16[32,2]{1,0:T(8,128)(2,1)} async-done(((bf16[256,2]{1,0:T(8,128)(2,1)}), bf16[32,2]{1,0:T(8,128)(2,1)}) %reduce-scatter.21.cloned.1.call-update) | async-done | bytes 144
  1580.6 69.2 %reduce-scatter.19.cloned.1.call-done = bf16[144,4]{1,0:T(8,128)(2,1)} async-done(((bf16[1152,4]{1,0:T(8,128)(2,1)}), bf16[144,4]{1,0:T(8,128)(2,1)}) %reduce-scatter.19.cloned.1.call-update) | async-done | bytes 1168
  1649.8 0.8 copy.179
  1650.6 27.9 %all-reduce.8 = (bf16[144,4]{0,1:T(4,128)(2,1)S(1)}, bf16[32,2]{0,1:T(2,128)(2,1)S(1)}) all-reduce(bf16[144,4]{0,1:T(4,128)(2,1)S(1)} %copy.179, bf16[32,2]{0,1:T(2,128)(2,1)S(1)} %copy.181), channel_id=1, replica_groups=mesh['ctx'=16,'wsh'=8] {'ctx'}, use_global_device_ids=true, to_apply=%region_33.34 | all-reduce | flops 640 | bytes 2560 | tf_op jit(solution)/shard_map/psum | solution.py:244
  1679.7 110.8 %all-reduce.12.cloned.1.call-done = (bf16[864,2,1152]{0,2,1:T(8,128)(2,1)}, bf16[864,1152]{0,1:T(8,128)(2,1)}, bf16[192,1152]{1,0:T(8,128)(2,1)}, bf16[128,1152]{1,0:T(8,128)(2,1)}) async-done(((bf16[864,2,1152]{0,2,1:T(8,128)(2,1)}, bf16[864,1152]{0,1:T(8,128)(2,1)}, bf16[192,1152]{1,0:T(8,128)(2,1)}, bf16[128,1152]{1,0:T(8,128)(2,1)}), (bf16[864,2,1152]{0,2,1:T(8,128)(2,1)}, bf16[864,1152]{0,1:T(8,128)(2,1)}, ...) | async-done | bytes 6709264 | tf_op jit(solution)/shard_map/psum | solution.py:246
  1790.4 1.8 convert_element_type.143
  1792.2 2.0 convert_element_type.141
  1794.2 12.8 copy.162
  1807.0 2.8 copy.163
  (214 shorter events, 14.6 us)
Async XLA Ops:
  7.2 71.6 %all-gather.8.cloned.1.call-start = ((), (), s32[]{:S(2)}) async-start(), calls=%async_computation.6 | async-start | bytes 3981312 | tf_op jit(solution)/shard_map/all_gather | solution.py:64
  7.9 108.0 %all-gather.10.cloned.1.call-start = ((), (), s32[]{:S(2)}) async-start(), calls=%async_computation.7 | async-start | bytes 2228224 | tf_op jit(solution)/shard_map/all_gather | solution.py:84
  61.8 20.5 %copy-start.31 = (f32[1152]{0:T(1024)}, f32[1152]{0:T(1024)S(1)}, u32[]{:S(2)}) copy-start(f32[1152]{0:T(1024)S(1)} %get-tuple-element.483) | copy-start | bytes 13828
  62.9 19.4 %copy-start.46 = (f32[128]{0:T(128)}, f32[128]{0:T(128)S(1)}, u32[]{:S(2)}) copy-start(f32[128]{0:T(128)S(1)} %fusion.60) | copy-start | bytes 1540
  62.9 26.0 %copy-start.44 = (f32[128]{0:T(128)}, f32[128]{0:T(128)S(1)}, u32[]{:S(2)}) copy-start(f32[128]{0:T(128)S(1)} %fusion.81) | copy-start | bytes 1540
  62.9 26.0 %copy-start.37 = (f32[256,1]{0,1:T(1,128)}, f32[256,1]{0,1:T(1,128)S(1)}, u32[]{:S(2)}) copy-start(f32[256,1]{0,1:T(1,128)S(1)} %get-tuple-element.579) | copy-start | bytes 3076
  62.9 27.9 %copy-start.35 = (f32[256,1]{0,1:T(1,128)}, f32[256,1]{0,1:T(1,128)S(1)}, u32[]{:S(2)}) copy-start(f32[256,1]{0,1:T(1,128)S(1)} %get-tuple-element.578) | copy-start | bytes 3076
  63.0 25.9 %copy-start.26 = (f32[128,128]{1,0:T(8,128)}, f32[128,128]{1,0:T(8,128)S(1)}, u32[]{:S(2)}) copy-start(f32[128,128]{1,0:T(8,128)S(1)} %broadcast_multiply_fusion.3) | copy-start | bytes 196612
  82.1 7.5 copy-start.17
  82.2 6.7 copy-start.48
  82.3 6.7 copy-start.42
  83.6 90.4 %all-gather.12.cloned.1.call-start = ((), (), s32[]{:S(2)}) async-start(), calls=%async_computation.8 | async-start | bytes 2654208 | tf_op jit(solution)/shard_map/all_gather | solution.py:65
  84.3 408.9 %all-gather.14.cloned.1.call-start = ((), (), s32[]{:S(2)}) async-start(), calls=%async_computation.9 | async-start | bytes 35831808 | tf_op jit(solution)/shard_map/all_gather | solution.py:128
  89.0 579.3 %all-gather.16.cloned.1.call-start = ((), (), s32[]{:S(2)}) async-start(), calls=%async_computation.10 | async-start | bytes 17915904 | tf_op jit(solution)/shard_map/all_gather | solution.py:136
  89.6 752.9 %reduce-scatter.13.cloned.1.call-start = ((), (), s32[]{:S(2)}) async-start(), calls=%async_computation.11 | async-start | bytes 2228224 | tf_op jit(solution)/shard_map/reduce_scatter | solution.py:217
  90.4 25.5 %copy-start.5 = (f32[128,4,256]{0,2,1:T(8,128)}, f32[128,4,256]{0,2,1:T(8,128)S(1)}, u32[]{:S(2)}) copy-start(f32[128,4,256]{0,2,1:T(8,128)S(1)} %copy.145) | copy-start | bytes 1572868
  90.7 0.6 copy-start.39
  90.7 0.6 copy-start.33
  91.4 24.5 %copy-start.7 = (bf16[128,4,256]{0,2,1:T(8,128)(2,1)}, bf16[128,4,256]{0,2,1:T(8,128)(2,1)S(1)}, u32[]{:S(2)}) copy-start(bf16[128,4,256]{0,2,1:T(8,128)(2,1)S(1)} %fusion.64) | copy-start | bytes 786436
  119.7 373.6 %copy-start.11 = (bf16[128,4,256]{2,0,1:T(8,128)(2,1)}, bf16[128,4,256]{2,0,1:T(8,128)(2,1)S(1)}, u32[]{:S(2)}) copy-start(bf16[128,4,256]{2,0,1:T(8,128)(2,1)S(1)} %get-tuple-element.996) | copy-start | bytes 786436
  119.7 56.6 %copy-start.13 = (bf16[1,128,1152]{2,1,0:T(8,128)(2,1)S(1)}, bf16[1,128,1152]{2,1,0:T(8,128)(2,1)}, u32[]{:S(2)}) copy-start(bf16[1,128,1152]{2,1,0:T(8,128)(2,1)} %param.16) | copy-start | bytes 884740
  119.7 373.5 %copy-start.21 = (bf16[128,4,256]{0,2,1:T(8,128)(2,1)}, bf16[128,4,256]{0,2,1:T(8,128)(2,1)S(1)}, u32[]{:S(2)}) copy-start(bf16[128,4,256]{0,2,1:T(8,128)(2,1)S(1)} %convert_element_type.128) | copy-start | bytes 786436
  509.8 3.0 copy-start
  515.2 161.9 %copy-start.18 = (bf16[1,128,1152]{2,1,0:T(8,128)(2,1)S(1)}, bf16[1,128,1152]{2,1,0:T(8,128)(2,1)}, u32[]{:S(2)}) copy-start(bf16[1,128,1152]{2,1,0:T(8,128)(2,1)} %param.23) | copy-start | bytes 884740
  668.3 10.6 copy-start.1
  678.9 10.3 copy-start.28
  689.2 16.3 copy-start.24
  689.2 16.3 copy-start.25
  720.6 1.9 copy-start.10
  720.6 3.0 copy-start.12
  721.1 2.5 copy-start.15
  722.5 1.1 copy-start.19
  726.5 2.6 copy-start.8
  733.8 0.8 copy-start.2
  736.5 1.4 copy-start.3
  736.5 1.4 copy-start.9
  737.9 4.0 copy-start.4
  737.9 4.0 copy-start.29
  741.8 602.3 %reduce-scatter.23.cloned.1.call-start = ((), (), s32[]{:S(2)}) async-start(), calls=%async_computation.16 | async-start | bytes 53747712
  839.2 1.0 copy-start.20
  839.2 1.0 copy-start.22
  839.2 3.3 copy-start.27
  839.2 4.6 copy-start.38
  839.3 4.6 copy-start.43
  839.3 5.9 copy-start.49
  839.3 584.2 %reduce-scatter.17.cloned.1.call-start = ((), (), s32[]{:S(2)}) async-start(), calls=%async_computation.13 | async-start | bytes 2654208 | tf_op jit(solution)/shard_map/reduce_scatter | solution.py:231
  842.4 4.3 copy-start.6
  842.4 4.3 copy-start.34
  842.4 4.3 copy-start.36
  842.4 4.5 copy-start.40
  842.4 665.7 %reduce-scatter.15.cloned.1.call-start = ((), (), s32[]{:S(2)}) async-start(), calls=%async_computation.12 | async-start | bytes 3981312 | tf_op jit(solution)/shard_map/reduce_scatter | solution.py:228
  846.5 0.9 copy-start.30
  846.6 1.0 copy-start.14
  846.6 1.0 copy-start.32
  846.6 1.0 copy-start.45
  847.6 3.0 copy-start.41
  850.6 729.2 %reduce-scatter.21.cloned.1.call-start = ((), (), s32[]{:S(2)}) async-start(), calls=%async_computation.15 | async-start | bytes 73728
  854.3 795.5 %reduce-scatter.19.cloned.1.call-start = ((), (), s32[]{:S(2)}) async-start(), calls=%async_computation.14 | async-start | bytes 331776
  855.3 935.1 %all-reduce.12.cloned.1.call-start = ((), (), s32[]{:S(2)}) async-start(), calls=%async_computation.17 | async-start | bytes 13860864 | tf_op jit(solution)/shard_map/psum | solution.py:246
  1360.8 147.3 %copy-start.47 = (f32[128]{0:T(128)S(1)}, f32[128]{0:T(128)}, u32[]{:S(2)}) copy-start(f32[128]{0:T(128)} %copy-done.46) | copy-start | bytes 1540
  1360.8 147.4 %copy-start.16 = (f32[128,1152]{1,0:T(8,128)S(1)}, f32[128,1152]{1,0:T(8,128)}, u32[]{:S(2)}) copy-start(f32[128,1152]{1,0:T(8,128)} %copy-done.15) | copy-start | bytes 1769476
  1794.2 12.8 copy-start.23
Sparse Core Ops, SparseCore 0:
  10.3 68.3 all-gather.7
  83.7 32.1 all-gather.9
  118.2 55.7 all-gather.11
  176.7 316.5 all-gather.13
  495.4 172.8 all-gather.15
  741.9 96.2 reduce-scatter.12
  842.3 501.7 reduce-scatter.22
  1347.9 75.5 reduce-scatter.16
  1427.9 80.1 reduce-scatter.14
  1511.5 68.2 reduce-scatter.20
  1583.9 65.8 reduce-scatter.18
  1652.4 137.9 all-reduce.11
where the time goes:
time: 1820 us
  waiting for transfers between devices  1450 us (80%)
  local copies, waits for them, and re-layouts  111 us (6%)
  matrix products  99.2 us (5%)
  blocking collectives  81.4 us (4%)
  other arithmetic  55.8 us (3%)
    unnamed x15, waiting for transfers between devices  631 us
    all_gather x1, waiting for transfers between devices, on_device(): lax.all_gather(w_gate_up, 'wsh', axis=0, tiled=True)  317 us
    all_gather x1, waiting for transfers between devices, on_device(): lax.all_gather(w_down, 'wsh', axis=0, tiled=True)  153 us
    psum x1, waiting for transfers between devices, on_device(): lax.psum(grad_gu_part.astype(jnp.bfloat16), 'ctx').astype(jnp.float32)  111 us
    unnamed x105, local copies, waits for them, and re-layouts  95.6 us
    reduce_scatter x1, waiting for transfers between devices, on_device(): lax.psum_scatter(grad_qkv_full.astype(jnp.bfloat16), 'wsh', scatter_dimen...  84.7 us
    reduce_scatter x1, waiting for transfers between devices, on_device(): lax.psum_scatter(grad_out_full.astype(jnp.bfloat16), 'wsh', scatter_dimen...  62.7 us
    all_gather x1, waiting for transfers between devices, on_device(): lax.all_gather(w_out, 'wsh', axis=0, tiled=True)  54.2 us
  transfers between devices with their start and end apart: 12, of which 11 were waited for; matrix products, arithmetic and copies ran while one was open for 9% of the time, Pallas kernels for 0%

commit v1 on v0

v1 whole, which is shorter than its diff:
```python
import functools

import jax
import jax.numpy as jnp
from jax import lax
from jax.experimental import pallas as pl
from jax.experimental.pallas import tpu as pltpu
from jax.sharding import PartitionSpec as P

HEADS = 4
HD = 256
KB = 512
EPS = 1e-06
ROPE_BASE = 1000000.0
MASKED = -1e30
MESH = pl.DeviceIdType.MESH
BF = jnp.bfloat16
F32 = jnp.float32


def params(cid):
    return pltpu.CompilerParams(collective_id=cid, has_side_effects=True)


def cost(us):
    return pl.CostEstimate(flops=0, bytes_accessed=int(us * 3.0e6), transcendentals=0)


def exchange_kernel(axis, n, modes, *refs):
    count = len(modes)
    ins, outs = refs[:count], refs[count : 2 * count]
    send, recv, own = refs[2 * count :]
    me = lax.axis_index(axis)
    barrier = pltpu.get_barrier_semaphore()
    for step in range(1, n):
        pl.semaphore_signal(
            barrier, inc=1, device_id={axis: lax.rem(me + step, n)}, device_id_type=MESH
        )
    pl.semaphore_wait(barrier, n - 1)
    copies = []
    for step in range(1, n):
        peer = lax.rem(me + step, n)
        for i, mode in enumerate(modes):
            copies.append(
                pltpu.make_async_remote_copy(
                    src_ref=ins[i] if mode == "gather" else ins[i].at[peer],
                    dst_ref=outs[i].at[me],
                    send_sem=send.at[i, step - 1],
                    recv_sem=recv.at[i, step - 1],
                    device_id={axis: peer},
                    device_id_type=MESH,
                )
            )
            copies[-1].start()
    for i, mode in enumerate(modes):
        mine = ins[i] if mode == "gather" else ins[i].at[me]
        copies.append(pltpu.make_async_copy(mine, outs[i].at[me], own.at[i]))
        copies[-1].start()
    for copy in copies:
        copy.wait()


def exchange(axis, n, cid, name, us, *pairs):
    modes = [mode for mode, _ in pairs]
    arrays = [array for _, array in pairs]
    shapes = [
        jax.ShapeDtypeStruct(((n,) + a.shape) if m == "gather" else a.shape, a.dtype)
        for m, a in pairs
    ]
    any_spec = pl.BlockSpec(memory_space=pl.ANY)
    return pl.pallas_call(
        functools.partial(exchange_kernel, axis, n, modes),
        out_shape=shapes,
        in_specs=[any_spec] * len(pairs),
        out_specs=[any_spec] * len(pairs),
        scratch_shapes=[
            pltpu.SemaphoreType.DMA((len(pairs), n - 1)),
            pltpu.SemaphoreType.DMA((len(pairs), n - 1)),
            pltpu.SemaphoreType.DMA((len(pairs),)),
        ],
        compiler_params=params(cid),
        cost_estimate=cost(us),
        name=name,
    )(*arrays)


def weights_kernel(w_ref, g_ref, wo_ref, go_ref, send, recv, fsend, frecv, gsend, grecv, own):
    ctx, me = lax.axis_index("ctx"), lax.axis_index("wsh")
    core = lax.rem(ctx, 2)
    other = ctx + 1 - 2 * core
    half = w_ref.shape[0] // 2
    rows = pl.ds(pl.multiple_of(core * half, half), half)
    barrier = pltpu.get_barrier_semaphore()
    for step in range(1, 8):
        pl.semaphore_signal(
            barrier, inc=1, device_id={"wsh": lax.rem(me + step, 8)}, device_id_type=MESH
        )
    pl.semaphore_signal(barrier, inc=1, device_id={"ctx": other}, device_id_type=MESH)
    pl.semaphore_wait(barrier, 8)
    copies, small = [], []
    for step in range(1, 8):
        peer = lax.rem(me + step, 8)
        small.append(
            pltpu.make_async_remote_copy(
                src_ref=g_ref, dst_ref=go_ref.at[me], send_sem=gsend.at[step - 1],
                recv_sem=grecv.at[step - 1], device_id={"wsh": peer}, device_id_type=MESH,
            )
        )
        small[-1].start()
        copies.append(
            pltpu.make_async_remote_copy(
                src_ref=w_ref.at[rows], dst_ref=wo_ref.at[me, rows], send_sem=send.at[step - 1],
                recv_sem=recv.at[step - 1], device_id={"wsh": peer}, device_id_type=MESH,
            )
        )
        copies[-1].start()
    mine = [
        pltpu.make_async_copy(w_ref, wo_ref.at[me], own.at[0]),
        pltpu.make_async_copy(g_ref, go_ref.at[me], own.at[1]),
    ]
    for copy in mine:
        copy.start()
    passed = []
    for step in range(1, 8):
        copies[step - 1].wait_recv()
        source = lax.rem(me + 8 - step, 8)
        passed.append(
            pltpu.make_async_remote_copy(
                src_ref=wo_ref.at[source, rows], dst_ref=wo_ref.at[source, rows],
                send_sem=fsend.at[step - 1], recv_sem=frecv.at[step - 1],
                device_id={"ctx": other}, device_id_type=MESH,
            )
        )
        passed[-1].start()
    for copy in copies:
        copy.wait_send()
    for copy in small + passed + mine:
        copy.wait()


def gather_weights(w, packed):
    any_spec = pl.BlockSpec(memory_space=pl.ANY)
    return pl.pallas_call(
        weights_kernel,
        out_shape=[
            jax.ShapeDtypeStruct((8,) + w.shape, w.dtype),
            jax.ShapeDtypeStruct((8,) + packed.shape, packed.dtype),
        ],
        in_specs=[any_spec] * 2,
        out_specs=[any_spec] * 2,
        scratch_shapes=[pltpu.SemaphoreType.DMA((7,))] * 6 + [pltpu.SemaphoreType.DMA((2,))],
        compiler_params=params(1),
        cost_estimate=cost(27),
        name="gather_weights",
    )(w, packed)


def kv_kernel(x_ref, o_ref, send, recv, fsend, frecv, own):
    me = lax.axis_index("ctx")
    core = lax.rem(me, 2)
    other = me + 1 - 2 * core
    barrier = pltpu.get_barrier_semaphore()
    for step in range(1, 8):
        pl.semaphore_signal(
            barrier, inc=1, device_id={"ctx": lax.rem(me + 2 * step, 16)}, device_id_type=MESH
        )
    pl.semaphore_signal(barrier, inc=1, device_id={"ctx": other}, device_id_type=MESH)
    pl.semaphore_wait(barrier, 8)
    copies = []
    for step in range(1, 8):
        copies.append(
            pltpu.make_async_remote_copy(
                src_ref=x_ref, dst_ref=o_ref.at[me], send_sem=send.at[step - 1],
                recv_sem=recv.at[step - 1], device_id={"ctx": lax.rem(me + 2 * step, 16)},
                device_id_type=MESH,
            )
        )
        copies[-1].start()
    mine = pltpu.make_async_copy(x_ref, o_ref.at[me], own)
    mine.start()
    passed = [
        pltpu.make_async_remote_copy(
            src_ref=x_ref, dst_ref=o_ref.at[me], send_sem=fsend.at[0], recv_sem=frecv.at[0],
            device_id={"ctx": other}, device_id_type=MESH,
        )
    ]
    passed[0].start()
    for step in range(1, 8):
        copies[step - 1].wait_recv()
        source = lax.rem(me + 16 - 2 * step, 16)
        passed.append(
            pltpu.make_async_remote_copy(
                src_ref=o_ref.at[source], dst_ref=o_ref.at[source],
                send_sem=fsend.at[step], recv_sem=frecv.at[step],
                device_id={"ctx": other}, device_id_type=MESH,
            )
        )
        passed[-1].start()
    for copy in copies:
        copy.wait_send()
    for copy in passed + [mine]:
        copy.wait()


def gather_kv(x):
    any_spec = pl.BlockSpec(memory_space=pl.ANY)
    return pl.pallas_call(
        kv_kernel,
        out_shape=jax.ShapeDtypeStruct((16,) + x.shape, x.dtype),
        in_specs=[any_spec],
        out_specs=any_spec,
        scratch_shapes=[
            pltpu.SemaphoreType.DMA((7,)),
            pltpu.SemaphoreType.DMA((7,)),
            pltpu.SemaphoreType.DMA((8,)),
            pltpu.SemaphoreType.DMA((8,)),
            pltpu.SemaphoreType.DMA,
        ],
        compiler_params=params(2),
        cost_estimate=cost(17),
        name="gather_kv",
    )(x)


NT = (((1,), (1,)), ((), ()))
TN = (((0,), (0,)), ((), ()))


def dot(a, b, dims):
    return lax.dot_general(a, b, dims, preferred_element_type=F32)


def masked_scores(q, keys, block, ctx, tokens):
    scores = dot(q, keys, NT)
    row = lax.rem(lax.broadcasted_iota(jnp.int32, scores.shape, 0), tokens) + ctx * tokens
    col = lax.broadcasted_iota(jnp.int32, scores.shape, 1) + block * KB
    return jnp.where(col <= row, scores, MASKED)


def attend_kernel(tokens, q_ref, kv_ref, out_ref, lse_ref, top, total, accum):
    ctx = lax.axis_index("ctx")
    last = (ctx * tokens) // KB
    q = q_ref[...]

    def block_of(index):
        return pl.ds(pl.multiple_of(index * KB, KB), KB)

    scores = masked_scores(q, kv_ref[block_of(last), :HD], last, ctx, tokens)
    start = jnp.max(scores, axis=-1, keepdims=True)
    probs = jnp.exp(scores - start)
    top[...] = jnp.broadcast_to(start, top.shape)
    total[...] = jnp.broadcast_to(jnp.sum(probs, axis=-1, keepdims=True), total.shape)
    accum[...] = jnp.dot(
        probs.astype(BF), kv_ref[block_of(last), HD:], preferred_element_type=F32
    )

    def body(index, carry):
        scores = dot(q, kv_ref[block_of(index), :HD], NT)
        old = top[:, :1]
        new = jnp.maximum(old, jnp.max(scores, axis=-1, keepdims=True))
        probs = jnp.exp(scores - new)
        keep = jnp.exp(old - new)
        top[...] = jnp.broadcast_to(new, top.shape)
        total[...] = total[...] * keep + jnp.sum(probs, axis=-1, keepdims=True)
        accum[...] = accum[...] * keep + jnp.dot(
            probs.astype(BF), kv_ref[block_of(index), HD:], preferred_element_type=F32
        )
        return carry

    lax.fori_loop(0, last, body, 0)
    out_ref[...] = accum[...] / total[:, :1]
    lse_ref[...] = top[...] + jnp.log(total[...])


def attend(q, kv, tokens):
    rows = q.shape[0]
    return pl.pallas_call(
        functools.partial(attend_kernel, tokens),
        out_shape=[
            jax.ShapeDtypeStruct((rows, HD), F32),
            jax.ShapeDtypeStruct((rows, 128), F32),
        ],
        scratch_shapes=[
            pltpu.VMEM((rows, 128), F32),
            pltpu.VMEM((rows, 128), F32),
            pltpu.VMEM((rows, HD), F32),
        ],
        compiler_params=pltpu.CompilerParams(vmem_limit_bytes=40 * 2**20),
        cost_estimate=cost(12),
        name="attend",
    )(q, kv)


def attend_back_kernel(tokens, q_ref, kv_ref, out_ref, lse_ref, d_ref, dq_ref, dkv_ref):
    ctx = lax.axis_index("ctx")
    last = (ctx * tokens) // KB
    q = q_ref[...]
    d_out = d_ref[...]
    lse = lse_ref[:, :1]
    delta = jnp.sum(d_out.astype(F32) * out_ref[...], axis=-1, keepdims=True)

    def block_of(index):
        return pl.ds(pl.multiple_of(index * KB, KB), KB)

    def work(index, scores):
        block = block_of(index)
        probs = jnp.exp(scores - lse)
        d_probs = dot(d_out, kv_ref[block, HD:], NT)
        d_scores = (probs * (d_probs - delta)).astype(BF)
        dkv_ref[block, :HD] = dot(d_scores, q, TN).astype(BF)
        dkv_ref[block, HD:] = dot(probs.astype(BF), d_out, TN).astype(BF)
        return jnp.dot(d_scores, kv_ref[block, :HD], preferred_element_type=F32)

    dq_ref[...] = work(last, masked_scores(q, kv_ref[block_of(last), :HD], last, ctx, tokens))

    def body(index, carry):
        dq_ref[...] += work(index, dot(q, kv_ref[block_of(index), :HD], NT))
        return carry

    lax.fori_loop(0, last, body, 0)

    def clear(index, carry):
        dkv_ref[block_of(index), :] = jnp.zeros((KB, 2 * HD), BF)
        return carry

    lax.fori_loop(last + 1, kv_ref.shape[0] // KB, clear, 0)


def attend_back(q, kv, out, lse, d_out, tokens):
    return pl.pallas_call(
        functools.partial(attend_back_kernel, tokens),
        out_shape=[
            jax.ShapeDtypeStruct(q.shape, F32),
            jax.ShapeDtypeStruct(kv.shape, BF),
        ],
        compiler_params=pltpu.CompilerParams(vmem_limit_bytes=40 * 2**20),
        cost_estimate=cost(20),
        name="attend_back",
    )(q, kv, out, lse, d_out)


def scale_of(values):
    return lax.rsqrt(jnp.mean(values * values, axis=-1, keepdims=True) + EPS)


def norm_back(v, r, g, dy):
    gdy = g * dy
    dv = r * gdy - v * (r * r * r) * jnp.mean(gdy * v, axis=-1, keepdims=True)
    return dv, dy * v * r


def rope(v, cosine, sine):
    a, b = v[..., : HD // 2], v[..., HD // 2 :]
    return jnp.concatenate([a * cosine - b * sine, b * cosine + a * sine], axis=-1)


def rope_back(u, cosine, sine):
    a, b = u[..., : HD // 2], u[..., HD // 2 :]
    return jnp.concatenate([a * cosine + b * sine, b * cosine - a * sine], axis=-1)


def on_device(hidden, w_qkv, w_out, norm_gains, qk_gains, w_gate_up, w_down, cotangent):
    tokens = hidden.shape[1]
    width = hidden.shape[2]
    x = hidden[0].astype(F32)
    cot = cotangent[0].astype(F32)
    positions = lax.axis_index("ctx") * tokens + jnp.arange(tokens, dtype=jnp.int32)
    freqs = ROPE_BASE ** (-jnp.arange(0, HD, 2, dtype=F32) / HD)
    angles = positions.astype(F32)[:, None] * freqs[None, :]
    cosine, sine = jnp.cos(angles), jnp.sin(angles)

    gain_part, qk_part = norm_gains.shape[0], qk_gains.shape[0]
    packed = jnp.zeros((16, 256), BF)
    packed = packed.at[:4, :gain_part].set(norm_gains.T)
    packed = packed.at[4:6, :qk_part].set(qk_gains.T)
    all_qkv, all_packed = gather_weights(w_qkv, packed)
    full_qkv = all_qkv.reshape(-1, width)
    full_out = lax.all_gather(w_out, "wsh", axis=0, tiled=True)
    gains = all_packed[:, :4, :gain_part].transpose(1, 0, 2).reshape(4, width).astype(F32)
    qk_gain = all_packed[:, 4:6, :qk_part].transpose(1, 0, 2).reshape(2, HD).astype(F32)

    r0 = scale_of(x)
    normed = (x * r0 * gains[0]).astype(BF)
    normed_all = lax.all_gather(normed, "wsh", axis=0, tiled=True)
    mixed = dot(normed, full_qkv, NT)
    q_raw = mixed[:, : HEADS * HD].reshape(tokens, HEADS, HD).transpose(1, 0, 2)
    k_raw = mixed[:, HEADS * HD : (HEADS + 1) * HD]
    rq, rk = scale_of(q_raw), scale_of(k_raw)
    q_low = (rope(q_raw * rq * qk_gain[0], cosine, sine) * HD ** (-0.5)).astype(BF)
    q_low = q_low.reshape(HEADS * tokens, HD)
    k_low = rope(k_raw * rk * qk_gain[1], cosine, sine).astype(BF)
    local_kv = jnp.concatenate([k_low, mixed[:, (HEADS + 1) * HD :].astype(BF)], axis=1)
    whole_kv = gather_kv(local_kv).reshape(-1, 2 * HD)

    out_heads, lse = attend(q_low, whole_kv, tokens)
    attended = out_heads.reshape(HEADS, tokens, HD).transpose(1, 0, 2).reshape(tokens, HEADS * HD)
    attended = attended.astype(BF)
    branch = jnp.dot(attended, full_out, preferred_element_type=F32)
    r1 = scale_of(branch)
    resid = x + branch * r1 * gains[1]
    r2 = scale_of(resid)
    normed2 = (resid * r2 * gains[2]).astype(BF)

    (n2_all,) = exchange("wsh", 8, 3, "gather_normed2", 31, ("gather", normed2))
    n2_all = n2_all.reshape(-1, width)
    w_gate, w_up = w_gate_up[:, 0], w_gate_up[:, 1]
    gate, up = dot(n2_all, w_gate, NT), dot(n2_all, w_up, NT)
    gelu, gelu_pull = jax.vjp(functools.partial(jax.nn.gelu, approximate=True), gate)
    inner = (gelu * up).astype(BF)
    terms = jnp.dot(inner, w_down, preferred_element_type=F32).astype(BF)
    (parts,) = exchange("wsh", 8, 4, "scatter_branch2", 31, ("scatter", terms.reshape(8, tokens, width)))
    branch2 = jnp.sum(parts.astype(F32), axis=0)

    r3 = scale_of(branch2)
    output = (resid + branch2 * r3 * gains[3]).astype(BF)
    d_branch2, dg3 = norm_back(branch2, r3, gains[3], cot)
    (d2_all,) = exchange("wsh", 8, 5, "gather_d_branch2", 31, ("gather", d_branch2.astype(BF)))
    d2_all = d2_all.reshape(-1, width)
    d_inner = dot(d2_all, w_down, NT)
    d_gate = (gelu_pull(d_inner * up)[0]).astype(BF)
    d_up = (d_inner * gelu).astype(BF)
    terms = (
        jnp.dot(d_gate, w_gate, preferred_element_type=F32)
        + jnp.dot(d_up, w_up, preferred_element_type=F32)
    ).astype(BF)
    (parts,) = exchange("wsh", 8, 6, "scatter_d_normed2", 31, ("scatter", terms.reshape(8, tokens, width)))
    ff_grads = lax.psum(
        (
            dot(d_gate, n2_all, TN).astype(BF),
            dot(d_up, n2_all, TN).astype(BF),
            dot(inner, d2_all, TN).astype(BF),
        ),
        "ctx",
    )
    d_normed2 = jnp.sum(parts.astype(F32), axis=0)

    d_more, dg2 = norm_back(resid, r2, gains[2], d_normed2)
    d_resid = cot + d_more
    d_branch, dg1 = norm_back(branch, r1, gains[1], d_resid)
    branch_low = d_branch.astype(BF)
    db_all = lax.all_gather(branch_low, "wsh", axis=0, tiled=True)
    d_attended = dot(branch_low, full_out, NT).astype(BF)
    d_heads = d_attended.reshape(tokens, HEADS, HD).transpose(1, 0, 2).reshape(HEADS * tokens, HD)
    d_q, d_kv = attend_back(q_low, whole_kv, out_heads, lse, d_heads, tokens)
    (kv_parts,) = exchange("ctx", 16, 7, "scatter_d_kv", 31, ("scatter", d_kv.reshape(16, tokens, 2 * HD)))
    own_kv = jnp.sum(kv_parts.astype(F32), axis=0)

    dq_rot = rope_back(d_q.reshape(HEADS, tokens, HD) * HD ** (-0.5), cosine, sine)
    d_q_raw, dgq = norm_back(q_raw, rq, qk_gain[0], dq_rot)
    dk_rot = rope_back(own_kv[:, :HD], cosine, sine)
    d_k_raw, dgk = norm_back(k_raw, rk, qk_gain[1], dk_rot)
    d_mixed = jnp.concatenate(
        [d_q_raw.transpose(1, 0, 2).reshape(tokens, HEADS * HD), d_k_raw, own_kv[:, HD:]], axis=1
    ).astype(BF)
    d_normed = jnp.dot(d_mixed, full_qkv, preferred_element_type=F32)
    d_input, dg0 = norm_back(x, r0, gains[0], d_normed)
    grad_hidden = (d_resid + d_input).astype(BF)

    dg = jnp.stack([jnp.sum(term, axis=0) for term in (dg0, dg1, dg2, dg3)])
    dqk = jnp.stack([jnp.sum(dgq, axis=(0, 1)), jnp.sum(dgk, axis=0)])
    small = jnp.zeros((8, 8, 256), F32)
    small = small.at[:, :4, :gain_part].set(dg.reshape(4, 8, gain_part).transpose(1, 0, 2))
    small = small.at[:, 4:6, :qk_part].set(dqk.reshape(2, 8, qk_part).transpose(1, 0, 2))
    qkv_part, out_part = w_qkv.shape[0], w_out.shape[0]
    dm_all, at_all, small_all = exchange(
        "wsh", 8, 8, "columns_to_owners", 12,
        ("scatter", d_mixed.reshape(tokens, 8, qkv_part).transpose(1, 0, 2)),
        ("scatter", attended.reshape(tokens, 8, out_part).transpose(1, 0, 2)),
        ("scatter", small),
    )
    grad_qkv = dot(dm_all.reshape(-1, qkv_part), normed_all, TN)
    grad_out = dot(at_all.reshape(-1, out_part), db_all, TN)
    both = jnp.concatenate([grad_qkv, grad_out], axis=0).astype(BF)
    share = both.shape[0] // 16
    room = -(-share // 16) * 16
    both = jnp.pad(both.reshape(16, share, width), ((0, 0), (0, room - share), (0, 0)))
    grad_parts, small_parts = exchange(
        "ctx", 16, 9, "scatter_grads", 12, ("scatter", both), ("gather", jnp.sum(small_all, axis=0))
    )
    mine = jnp.sum(grad_parts.astype(F32), axis=0).astype(BF)
    (grads,) = exchange("ctx", 16, 10, "gather_grads", 12, ("gather", mine))
    grads = grads[:, :share].reshape(-1, width).astype(F32)
    small_sum = jnp.sum(small_parts, axis=0)
    return (
        output[None],
        grad_hidden[None],
        grads[:qkv_part],
        grads[qkv_part:],
        small_sum[:4, :gain_part].T,
        small_sum[4:6, :qk_part].T,
        jnp.stack([ff_grads[0].astype(F32), ff_grads[1].astype(F32)], axis=1),
        ff_grads[2].astype(F32),
    )


def solution(mesh):
    return jax.shard_map(
        on_device,
        mesh=mesh,
        in_specs=(
            P("wsh", "ctx", None),
            P("wsh", None),
            P("wsh", None),
            P("wsh", None),
            P("wsh", None),
            P("wsh", None, None),
            P("wsh", None),
            P("wsh", "ctx", None),
        ),
        out_specs=(
            P("wsh", "ctx", None),
            P("wsh", "ctx", None),
            P("wsh", None),
            P("wsh", None),
            P("wsh", None),
            P("wsh", None),
            P("wsh", None, None),
            P("wsh", None),
        ),
        check_vma=False,
    )
```

time: 1820 us -> 604 us (0.33)
  waiting for transfers between devices: 1450 us -> 128 us
  Pallas kernels: 0 us -> 318 us
  blocking collectives: 81.4 us -> 0 us
  local copies, waits for them, and re-layouts: 111 us -> 45.8 us
  matrix products: 99.2 us -> 56.8 us
  other arithmetic: 55.8 us -> 34.6 us
    unnamed x15 -> x4, waiting for transfers between devices: 631 us -> 0.73 us
    all_gather x5 -> x3, waiting for transfers between devices: 564 us -> 35 us  [the longest x1 34.9 us: on_device(): normed_all = lax.all_gather(normed, 'wsh', axis=0, tiled=True)]
    pallas_call x0 -> x12, Pallas kernels: none -> 318 us  [the longest x8 255 us: exchange(): pl.pallas_call(functools.partial(exchange_kernel, axis, n, modes), out_sh...]
    reduce_scatter x3 -> x0, waiting for transfers between devices: 147 us -> none  [the longest x1 84.7 us: on_device(): lax.psum_scatter(grad_qkv_full.astype(jnp.bfloat16), 'wsh', scatter_dimen...]
    unnamed x105 -> x123, local copies, waits for them, and re-layouts: 95.6 us -> 23 us
    all_gather x2 -> x0, blocking collectives: 53.5 us -> none  [the longest x1 29.8 us: on_device(): lax.all_gather(norm_gains, 'wsh', axis=0, tiled=True)]
    dot_general x21 -> x15, matrix products: 99.2 us -> 56.8 us  [the longest x10 42.3 us: dot(): return lax.dot_general(a, b, dims, preferred_element_type=F32)]
    concatenate x2, other arithmetic: 33 us -> 1.49 us  [the longest x1 1.43 us: on_device(): jnp.concatenate([k_low, mixed[:, (HEADS + 1) * HD:].astype(BF)], axis=1)]
  transfers between devices with their start and end apart: 12 -> 4, of which waited for: 11 -> 2; matrix products, arithmetic and copies ran while one was open for 9% -> 11% of each run, Pallas kernels for 0% -> 31%
where the time goes in v1:
time: 604 us; the launch traced here: 599 us
  Pallas kernels  318 us (53%)
  waiting for transfers between devices  128 us (21%)
  matrix products  56.8 us (9%)
  local copies, waits for them, and re-layouts  45.8 us (8%)
  other arithmetic  34.6 us (6%)
  between operations  15 us (2%)
    pallas_call x8, Pallas kernels, exchange(): pl.pallas_call(functools.partial(exchange_kernel, axis, n, modes), out_sh...  255 us
    psum x1, waiting for transfers between devices, on_device(): lax.psum((dot(d_gate, n2_all, TN).astype(BF), dot(d_up, n2_all, TN).astyp...  92.8 us
    dot_general x10, matrix products, dot(): return lax.dot_general(a, b, dims, preferred_element_type=F32)  42.3 us
    all_gather x1, waiting for transfers between devices, on_device(): normed_all = lax.all_gather(normed, 'wsh', axis=0, tiled=True)  34.9 us
    pallas_call x1, Pallas kernels, gather_weights(): pl.pallas_call(weights_kernel, out_shape=[jax.ShapeDtypeStruct((8,) + w.s...  33.9 us
    pallas_call x1, Pallas kernels, gather_kv(): pl.pallas_call(kv_kernel, out_shape=jax.ShapeDtypeStruct((16,) + x.shape,...  25.7 us
    unnamed x123, local copies, waits for them, and re-layouts  23 us
  transfers between devices with their start and end apart: 4, of which 2 were waited for; matrix products, arithmetic and copies ran while one was open for 11% of the time, Pallas kernels for 31%

profile of v1, /device:TPU:0, one launch (start us, length us, event | category | flops | bytes accessed | tf_op | source)
XLA Modules:
  0.0 598.6 jit_solution(11067091274850438451)
XLA Ops:
  8.7 1.5 scatter.15.g_ref
  10.7 33.9 %gather_weights.1 = (bf16[8,192,1152]{2,1,0:T(8,128)(2,1)}, bf16[8,16,256]{2,1,0:T(8,128)(2,1)}) custom-call(bf16[192,1152]{1,0:T(8,128)(2,1)} %w_ref.1, bf16[16,256]{1,0:T(8,128)(2,1)} %copy-done.40), custom_call_target="tpu_custom_call" | custom-call | bytes 81000000 | tf_op jit(solution)/shard_map/gather_weights/pallas_call | solution.py:143
  45.4 0.8 convert_bitcast_fusion.1
  46.1 1.1 fusion.23
  48.0 3.4 fusion.40
  54.7 0.9 fusion.54
  57.3 1.4 pad_maximum_fusion.2.x_ref
  58.7 25.7 %gather_kv.1 = bf16[16,128,512]{2,1,0:T(8,128)(2,1)} custom-call(bf16[128,512]{1,0:T(8,128)(2,1)} %pad_maximum_fusion.2.x_ref), custom_call_target="tpu_custom_call" | custom-call | bytes 51000000 | tf_op jit(solution)/shard_map/gather_kv/pallas_call | solution.py:207
  84.5 1.6 copy-done.2
  86.0 1.5 attend.1
  88.5 9.5 %fusion.60 = (bf16[864,1,1152]{2,1,0:T(2,128)(2,1)}, bf16[864,1,1152]{2,1,0:T(2,128)(2,1)}) fusion(bf16[864,2,1152]{2,1,0:T(2,128)(2,1)} %param.21), kind=kLoop, calls=%fused_computation.150 | loop fusion | bytes 7962624 | tf_op jit(solution)/shard_map/slice | solution.py:406
  98.0 2.3 multiply_reduce_fusion.6
  101.5 0.8 multiply_convert_fusion.2.refs_0_
  102.3 36.4 %gather_normed2.1 = bf16[8,128,1152]{2,1,0:T(8,128)(2,1)} custom-call(bf16[128,1152]{1,0:T(8,128)(2,1)} %multiply_convert_fusion.2.refs_0_), custom_call_target="tpu_custom_call" | custom-call | bytes 93000000 | tf_op jit(solution)/shard_map/gather_normed2/pallas_call | solution.py:71
  138.8 5.5 fusion.10
  144.3 4.8 multiply_convert_fusion.1
  149.1 4.1 convolution_convert_fusion
  153.2 34.9 %scatter_branch2.1 = bf16[8,128,1152]{2,1,0:T(8,128)(2,1)} custom-call(bf16[8,128,1152]{2,1,0:T(8,128)(2,1)} %bitcast.155), custom_call_target="tpu_custom_call" | custom-call | bytes 93000000 | tf_op jit(solution)/shard_map/scatter_branch2/pallas_call | solution.py:71
  188.2 2.1 convert_reduce_fusion.1
  191.2 1.1 fusion.21
  192.2 33.5 %gather_d_branch2.1 = bf16[8,128,1152]{2,1,0:T(8,128)(2,1)} custom-call(bf16[128,1152]{1,0:T(8,128)(2,1)} %get-tuple-element.126.refs_0_), custom_call_target="tpu_custom_call" | custom-call | bytes 93000000 | tf_op jit(solution)/shard_map/gather_d_branch2/pallas_call | solution.py:71
  225.7 7.8 %multiply_convert_fusion = (bf16[1024,864]{0,1:T(8,128)(2,1)S(1)}, bf16[1024,864]{0,1:T(8,128)(2,1)S(1)}) fusion(f32[1024,864]{0,1:T(8,128)} %copy-done.56, f32[1024,864]{0,1:T(8,128)} %get-tuple-element.153, bf16[1024,1152]{1,0:T(8,128)(2,1)} %bitcast.152, bf16[864,1152]{1,0:T(8,128)(2,1)S(1)} %copy-done), kind=kOutput, calls=%fused_computation.15 | convolution fusion | flops 2059665408 | bytes 14966784 | tf_op jit(solution)/shard_map/dot_general | solution.py:230
  233.6 2.9 fusion.9
  237.0 4.2 add_convert_fusion
  241.2 28.8 %scatter_d_normed2.1 = bf16[8,128,1152]{2,1,0:T(8,128)(2,1)} custom-call(bf16[8,128,1152]{2,1,0:T(8,128)(2,1)} %bitcast.154), custom_call_target="tpu_custom_call" | custom-call | bytes 93000000 | tf_op jit(solution)/shard_map/scatter_d_normed2/pallas_call | solution.py:71
  270.1 2.1 convert_reduce_fusion
  272.9 1.0 multiply_reduce_fusion.1
  274.0 0.8 copy-done.15
  274.8 1.6 subtract_convert_fusion
  276.5 2.7 convolution_convert_fusion.6
  279.2 0.9 copy-done.6
  280.1 1.5 attend_back.1
  281.6 1.3 copy-done.4
  282.9 51.8 %scatter_d_kv.1 = bf16[16,128,512]{2,1,0:T(8,128)(2,1)} custom-call(bf16[16,128,512]{2,1,0:T(8,128)(2,1)} %bitcast.143), custom_call_target="tpu_custom_call" | custom-call | bytes 93000000 | tf_op jit(solution)/shard_map/scatter_d_kv/pallas_call | solution.py:71
  335.0 1.3 copy-done.12
  336.8 1.0 fusion.57
  337.8 1.0 multiply_reduce_fusion.10
  338.9 1.0 multiply_subtract_fusion.3
  340.2 1.0 multiply_add_fusion
  342.3 0.9 fusion.30
  343.3 1.2 fusion.32
  344.8 6.1 %convolution_convert_fusion.1 = bf16[864,1152]{1,0:T(8,128)(2,1)} fusion(bf16[1024,864]{0,1:T(8,128)(2,1)} %copy-done.57, bf16[1024,1152]{1,0:T(8,128)(2,1)} %bitcast.153), kind=kOutput, calls=%fused_computation.17 | convolution fusion | flops 2039427072 | bytes 6119424 | tf_op jit(solution)/shard_map/dot_general | solution.py:230
  350.9 3.7 fusion.8
  354.6 3.7 fusion.7
  358.4 0.9 copy-done.26
  359.3 0.9 copy.33
  360.8 1.0 copy.32
  361.9 0.8 scatter.19.refs_2_
  363.3 19.3 %columns_to_owners.1 = (bf16[8,128,192]{2,1,0:T(8,128)(2,1)}, bf16[8,128,128]{2,1,0:T(8,128)(2,1)}, f32[8,8,256]{2,1,0:T(8,128)}) custom-call(bf16[8,128,192]{2,1,0:T(8,128)(2,1)} %bitcast.160, bf16[8,128,128]{2,1,0:T(8,128)(2,1)} %bitcast.167, f32[8,8,256]{2,1,0:T(8,128)} %copy-done.31), custom_call_target="tpu_custom_call" | custom-call | bytes 36000000 | tf_op jit(solution)/shard_map/columns_to_owners/pallas_call | solution.py:71
  382.6 1.5 reduce_sum.240.refs_1_
  384.1 2.3 convolution_convert_fusion.5
  386.4 34.9 %all-gather.6.cloned.1.call-done = bf16[1024,1152]{1,0:T(8,128)(2,1)} async-done(((bf16[128,1152]{1,0:T(8,128)(2,1)}), bf16[1024,1152]{1,0:T(8,128)(2,1)}) %all-gather.6.cloned.1.call-update) | async-done | bytes 2359312 | tf_op jit(solution)/shard_map/all_gather | solution.py:384
  421.4 2.4 convolution_convert_fusion.4
  424.0 1.1 pad.23.refs_0_
  425.1 25.1 %scatter_grads.1 = (bf16[16,32,1152]{2,1,0:T(8,128)(2,1)}, f32[16,8,256]{2,1,0:T(8,128)}) custom-call(bf16[16,32,1152]{2,1,0:T(8,128)(2,1)} %pad.23.refs_0_, f32[8,256]{1,0:T(8,128)} %reduce_sum.240.refs_1_), custom_call_target="tpu_custom_call" | custom-call | bytes 36000000 | tf_op jit(solution)/shard_map/scatter_grads/pallas_call | solution.py:71
  450.2 2.1 reduce_sum.241.refs_0_
  452.3 25.1 %gather_grads.1 = bf16[16,32,1152]{2,1,0:T(8,128)(2,1)} custom-call(bf16[32,1152]{1,0:T(8,128)(2,1)} %reduce_sum.241.refs_0_), custom_call_target="tpu_custom_call" | custom-call | bytes 36000000 | tf_op jit(solution)/shard_map/gather_grads/pallas_call | solution.py:71
  477.4 1.3 slice_convert_fusion
  478.9 0.9 slice.240
  479.8 1.0 slice.239
  481.9 92.8 %all-reduce.6.cloned.1.call-done = (bf16[864,1,1152]{2,0,1:T(8,128)(2,1)}, bf16[864,1,1152]{2,0,1:T(8,128)(2,1)}, bf16[864,1152]{1,0:T(8,128)(2,1)}) async-done(((bf16[864,1,1152]{2,0,1:T(8,128)(2,1)}, bf16[864,1,1152]{2,0,1:T(8,128)(2,1)}, bf16[864,1152]{1,0:T(8,128)(2,1)}), (bf16[864,1,1152]{2,0,1:T(8,128)(2,1)}, bf16[864,1,1152]{2,0,1:T(8,128)(2,1)}, ...) | async-done | bytes 5971984 | tf_op jit(solution)/shard_map/psum | solution.py:427
  574.7 2.7 maximum_convert_fusion
  577.4 12.0 %copy.34 = f32[864,2,1152]{2,1,0:T(2,128)} copy(f32[864,2,1152]{2,0,1:T(8,128)S(1)} %maximum_convert_fusion) | data formatting | bytes 15925248
  589.4 2.2 convert_element_type.187
  (194 shorter events, 17.9 us)
Async XLA Ops:
  7.2 141.9 %copy-start = (bf16[864,1152]{1,0:T(8,128)(2,1)S(1)}, bf16[864,1152]{1,0:T(8,128)(2,1)}, u32[]{:S(2)}) copy-start(bf16[864,1152]{1,0:T(8,128)(2,1)} %param.22) | copy-start | bytes 5971972
  7.2 90.8 %all-gather.4.cloned.1.call-start = ((), (), s32[]{:S(2)}) async-start(), calls=%async_computation | async-start | bytes 2654208 | tf_op jit(solution)/shard_map/all_gather | solution.py:378
  7.9 376.2 %all-gather.8.cloned.1.call-start = ((), (), s32[]{:S(2)}) async-start(), calls=%async_computation.2 | async-start | bytes 2654208 | tf_op jit(solution)/shard_map/all_gather | solution.py:441
  10.1 0.6 copy-start.40
  47.8 3.6 copy-start.48
  51.4 4.3 copy-start.17
  52.2 2.3 copy-start.47
  52.2 3.8 copy-start.50
  53.7 0.9 copy-start.41
  53.8 3.3 copy-start.43
  54.5 1.1 copy-start.51
  55.8 1.4 copy-start.28
  55.8 1.4 copy-start.30
  56.0 28.3 %copy-start.7 = (f32[128,1024]{0,1:T(8,128)}, f32[128,1024]{0,1:T(8,128)S(1)}, u32[]{:S(2)}) copy-start(f32[128,1024]{0,1:T(8,128)S(1)} %copy.35) | copy-start | bytes 1572868
  56.8 27.6 %copy-start.35 = (f32[4,128]{1,0:T(4,128)}, f32[4,128]{1,0:T(4,128)S(1)}, u32[]{:S(2)}) copy-start(f32[4,128]{1,0:T(4,128)S(1)} %get-tuple-element.137) | copy-start | bytes 6148
  84.4 1.6 copy-start.2
  87.5 0.7 copy-start.5
  88.5 9.6 %copy-start.25 = (bf16[4,128,256]{1,2,0:T(8,128)(2,1)}, bf16[4,128,256]{1,2,0:T(8,128)(2,1)S(1)}, u32[]{:S(2)}) copy-start(bf16[4,128,256]{1,2,0:T(8,128)(2,1)S(1)} %copy.24) | copy-start | bytes 786436
  98.0 3.5 copy-start.32
  98.0 3.2 copy-start.13
  100.4 0.8 copy-start.10
  101.0 171.9 %copy-start.46 = (f32[128]{0:T(128)}, f32[128]{0:T(128)S(1)}, u32[]{:S(2)}) copy-start(f32[128]{0:T(128)S(1)} %get-tuple-element.145) | copy-start | bytes 1540
  138.8 5.5 copy-start.18
  138.8 5.5 copy-start.23
  144.2 4.8 copy-start.56
  149.0 4.1 copy-start.57
  188.1 2.2 copy-start.21
  188.1 2.2 copy-start.34
  225.7 7.9 %copy-start.20 = (bf16[864,1,1152]{2,1,0:T(2,128)(2,1)S(1)}, bf16[864,1,1152]{2,1,0:T(2,128)(2,1)}, u32[]{:S(2)}) copy-start(bf16[864,1,1152]{2,1,0:T(2,128)(2,1)} %get-tuple-element.120) | copy-start | bytes 5971972
  233.5 3.0 copy-start.54
  233.6 3.0 copy-start.58
  233.6 3.4 copy-start.19
  270.0 2.9 copy-start.11
  270.0 2.9 copy-start.22
  272.2 2.6 copy-start.52
  273.9 0.8 copy-start.15
  274.8 4.4 copy-start.3
  276.4 144.9 %all-gather.6.cloned.1.call-start = ((), (), s32[]{:S(2)}) async-start(), calls=%async_computation.1 | async-start | bytes 2654208 | tf_op jit(solution)/shard_map/all_gather | solution.py:384
  279.2 1.0 copy-start.6
  281.6 1.3 copy-start.4
  334.8 1.6 copy-start.12
  334.8 3.0 copy-start.42
  336.3 4.9 copy-start.8
  336.3 4.9 copy-start.36
  336.6 4.6 copy-start.44
  336.7 4.8 copy-start.45
  339.9 1.7 copy-start.14
  339.9 1.7 copy-start.49
  340.2 2.1 copy-start.9
  342.3 1.1 copy-start.16
  342.3 1.1 copy-start.53
  344.5 6.4 %copy-start.24 = (bf16[8,128,1152]{2,1,0:T(8,128)(2,1)S(1)}, bf16[8,128,1152]{2,1,0:T(8,128)(2,1)}, u32[]{:S(2)}) copy-start(bf16[8,128,1152]{2,1,0:T(8,128)(2,1)} %gather_normed2.1) | copy-start | bytes 7077892
  344.5 230.1 %all-reduce.6.cloned.1.call-start = ((), (), s32[]{:S(2)}) async-start(), calls=%async_computation.3 | async-start | bytes 11943936 | tf_op jit(solution)/shard_map/psum | solution.py:427
  344.8 6.1 %copy-start.59 = (bf16[1024,864]{0,1:T(8,128)(2,1)S(1)}, bf16[1024,864]{0,1:T(8,128)(2,1)}, u32[]{:S(2)}) copy-start(bf16[1024,864]{0,1:T(8,128)(2,1)} %copy-done.58) | copy-start | bytes 5308420
  350.9 3.7 copy-start.55
  358.4 0.9 copy-start.26
  358.4 1.8 copy-start.37
  358.4 1.9 copy-start.38
  358.4 2.0 copy-start.39
  362.7 0.6 copy-start.31
  382.6 38.8 %copy-start.29 = (bf16[8,128,192]{2,1,0:T(8,128)(2,1)S(1)}, bf16[8,128,192]{2,1,0:T(8,128)(2,1)}, u32[]{:S(2)}) copy-start(bf16[8,128,192]{2,1,0:T(8,128)(2,1)} %get-tuple-element.73) | copy-start | bytes 1179652
  478.7 2.0 copy-start.33
  577.4 12.1 %copy-start.27 = (bf16[864,1152]{1,0:T(8,128)(2,1)S(1)}, bf16[864,1152]{1,0:T(8,128)(2,1)}, u32[]{:S(2)}) copy-start(bf16[864,1152]{1,0:T(8,128)(2,1)} %get-tuple-element.114) | copy-start | bytes 5971972
  589.4 2.4 copy-start.1
Sparse Core Ops, SparseCore 0:
  10.3 83.0 all-gather.3
  276.5 78.0 all-gather.7
  357.5 63.7 all-gather.5
  424.5 150.0 all-reduce.5

commit v2 on v1

v2 whole, which is shorter than its diff:
```python
import functools

import jax
import jax.numpy as jnp
from jax import lax
from jax.experimental import pallas as pl
from jax.experimental.pallas import tpu as pltpu
from jax.sharding import PartitionSpec as P

HEADS = 4
HD = 256
KB = 512
EPS = 1e-06
ROPE_BASE = 1000000.0
MASKED = -1e30
MESH = pl.DeviceIdType.MESH
BF = jnp.bfloat16
F32 = jnp.float32


def cost(us):
    return pl.CostEstimate(flops=0, bytes_accessed=int(us * 3.0e6), transcendentals=0)


class Place:
    def __init__(self):
        ctx, wsh = lax.axis_index("ctx"), lax.axis_index("wsh")
        self.ctx, self.wsh = ctx, wsh
        self.chip, self.core = lax.div(ctx, 2), lax.rem(ctx, 2)
        self.h, self.y = lax.div(wsh, 4), lax.rem(wsh, 4)
        self.yp, self.ym, self.y2 = (lax.rem(self.y + k, 4) for k in (1, 3, 2))
        self.up = {"wsh": self.h * 4 + self.yp}
        self.down = {"wsh": self.h * 4 + self.ym}
        self.across = {"wsh": (1 - self.h) * 4 + self.y}
        self.twin = {"ctx": ctx + 1 - 2 * self.core}

    def chips(self, step):
        return {"ctx": lax.rem(self.ctx + 2 * step, 16)}

    def row(self, step):
        return {"wsh": lax.rem(self.wsh + step, 8)}

    def peers(self, groups):
        found = []
        if "near" in groups and "row" not in groups:
            found += [self.up, self.down, self.across]
        if "row" in groups:
            found += [self.row(step) for step in range(1, 8)]
        if "chips" in groups:
            found += [self.chips(step) for step in range(1, 8)]
        if "twin" in groups:
            found.append(self.twin)
        if "others" in groups:
            found += [{"ctx": lax.rem(self.ctx + 2 * s + 1, 16)} for s in range(8)]
        return found


def remote(src, dst, sems, i, device):
    return pltpu.make_async_remote_copy(
        src_ref=src, dst_ref=dst, send_sem=sems.at[0, i], recv_sem=sems.at[1, i],
        device_id=device, device_id_type=MESH,
    )


def meet(place, groups):
    barrier = pltpu.get_barrier_semaphore()
    peers = place.peers(groups)
    for peer in peers:
        pl.semaphore_signal(barrier, inc=1, device_id=peer, device_id_type=MESH)
    pl.semaphore_wait(barrier, len(peers))


class GatherWsh:
    def __init__(self, array, pair=False):
        self.arrays, self.pair = [array], pair
        self.groups = {"near", "twin"} if pair else {"near"}
        self.outs = [jax.ShapeDtypeStruct((8,) + array.shape, array.dtype)]
        self.out_spaces, self.in_spaces = [pl.ANY], [pl.ANY]
        self.scratch = [pltpu.SemaphoreType.DMA((2, 18 if pair else 9)), pltpu.SemaphoreType.DMA]

    def run(self, p, ins, outs, scratch):
        (x,), (o,), (sems, own) = ins, outs, scratch
        size = x.shape[0] // (2 if self.pair else 1)
        base = pl.multiple_of(p.core * size, size) if self.pair else 0
        half = size // 2
        every, low, high = pl.ds(base, size), pl.ds(base, half), pl.ds(base + half, half)
        other = (1 - p.h) * 4
        mine = p.h * 4
        copies = {}

        def send(i, block, rows, device, source=None):
            source = o.at[block, rows] if source is None else source
            copies[i] = remote(source, o.at[block, rows], sems, i, device)
            copies[i].start()

        def arrived(i, block, rows):
            copies[i].wait_recv()
            if self.pair:
                send(9 + i, block, rows, p.twin)

        send(2, p.wsh, every, p.across, x.at[every])
        send(0, p.wsh, every, p.up, x.at[every])
        send(1, p.wsh, every, p.down, x.at[every])
        local = pltpu.make_async_copy(x, o.at[p.wsh], own)
        local.start()
        yield
        arrived(2, other + p.y, every)
        send(5, other + p.y, every, p.up)
        send(6, other + p.y, every, p.down)
        yield
        arrived(0, mine + p.ym, every)
        send(3, mine + p.ym, low, p.up)
        arrived(1, mine + p.yp, every)
        send(4, mine + p.yp, high, p.down)
        yield
        arrived(5, other + p.ym, every)
        send(7, other + p.ym, low, p.up)
        arrived(6, other + p.yp, every)
        send(8, other + p.yp, high, p.down)
        yield
        arrived(3, mine + p.y2, low)
        arrived(4, mine + p.y2, high)
        yield
        arrived(7, other + p.y2, low)
        arrived(8, other + p.y2, high)
        yield
        for i, copy in copies.items():
            copy.wait_send()
            if i >= 9:
                copy.wait_recv()
        local.wait()


class ScatterWsh:
    def __init__(self, array):
        _, rows, width = array.shape
        self.arrays, self.groups = [array], {"near"}
        self.outs = [jax.ShapeDtypeStruct((rows, width), F32)]
        self.in_spaces, self.out_spaces = [pltpu.VMEM], [pltpu.VMEM]
        half = pltpu.VMEM((2, rows // 2, width), BF)
        whole = pltpu.VMEM((2, rows, width), BF)
        self.scratch = [half, half, half, half, whole, whole, pltpu.VMEM((2, rows, width), BF)]
        self.scratch.append(pltpu.SemaphoreType.DMA((2, 13)))

    def run(self, p, ins, outs, scratch):
        (x,), (o,), (buf_a, buf_b, sum_c, sum_d, buf_c, buf_d, buf_e, sems) = ins, outs, scratch
        half = x.shape[1] // 2
        low, high = pl.ds(0, half), pl.ds(half, half)
        planes = ((1 - p.h) * 4, p.h * 4)
        copies = {}

        def send(i, source, target, device):
            copies[i] = remote(source, target, sems, i, device)
            copies[i].start()

        for k, plane in enumerate(planes):
            send(k, x.at[plane + p.y2, low], buf_a.at[k], p.up)
            send(2 + k, x.at[plane + p.y2, high], buf_b.at[k], p.down)
            send(4 + k, x.at[plane + p.yp, high], buf_c.at[k, high], p.up)
            send(6 + k, x.at[plane + p.ym, low], buf_d.at[k, low], p.down)
        for k, plane in enumerate(planes):
            yield
            copies[k].wait_recv()
            sum_c[k] = (x[plane + p.yp, :half].astype(F32) + buf_a[k].astype(F32)).astype(BF)
            send(8 + k, sum_c.at[k], buf_c.at[k, low], p.up)
            copies[2 + k].wait_recv()
            sum_d[k] = (x[plane + p.ym, half:].astype(F32) + buf_b[k].astype(F32)).astype(BF)
            send(10 + k, sum_d.at[k], buf_d.at[k, high], p.down)
        for k, plane in enumerate(planes):
            yield
            for i in (4, 6, 8, 10):
                copies[i + k].wait_recv()
            total = x[plane + p.y].astype(F32) + buf_c[k].astype(F32) + buf_d[k].astype(F32)
            if k == 0:
                buf_e[0] = total.astype(BF)
                send(12, buf_e.at[0], buf_e.at[1], p.across)
            else:
                yield
                copies[12].wait_recv()
                o[...] = total + buf_e[1].astype(F32)
        for copy in copies.values():
            copy.wait_send()


class DirectWsh:
    def __init__(self, mode, array):
        self.mode, self.arrays, self.groups = mode, [array], {"row"}
        shape = ((8,) + array.shape) if mode == "gather" else array.shape
        self.outs = [jax.ShapeDtypeStruct(shape, array.dtype)]
        self.in_spaces, self.out_spaces = [pl.ANY], [pl.ANY]
        self.scratch = [pltpu.SemaphoreType.DMA((2, 7)), pltpu.SemaphoreType.DMA]

    def run(self, p, ins, outs, scratch):
        (x,), (o,), (sems, own) = ins, outs, scratch
        pick = (lambda i: x) if self.mode == "gather" else (lambda i: x.at[i])
        copies = []
        for step in range(1, 8):
            to = p.row(step)
            copies.append(remote(pick(to["wsh"]), o.at[p.wsh], sems, step - 1, to))
            copies[-1].start()
        copies.append(pltpu.make_async_copy(pick(p.wsh), o.at[p.wsh], own))
        copies[-1].start()
        yield
        yield
        yield
        for copy in copies:
            copy.wait()


class GatherCtx:
    def __init__(self, array):
        self.arrays, self.groups = [array], {"chips", "twin"}
        self.outs = [jax.ShapeDtypeStruct((16,) + array.shape, array.dtype)]
        self.in_spaces, self.out_spaces = [pl.ANY], [pl.ANY]
        self.scratch = [pltpu.SemaphoreType.DMA((2, 15)), pltpu.SemaphoreType.DMA]

    def run(self, p, ins, outs, scratch):
        (x,), (o,), (sems, own) = ins, outs, scratch
        copies = []
        for step in range(1, 8):
            copies.append(remote(x, o.at[p.ctx], sems, step - 1, p.chips(step)))
            copies[-1].start()
        local = pltpu.make_async_copy(x, o.at[p.ctx], own)
        local.start()
        passed = [remote(x, o.at[p.ctx], sems, 7, p.twin)]
        passed[0].start()
        for step in range(1, 8):
            if step % 2 == 1:
                yield
            copies[step - 1].wait_recv()
            source = lax.rem(p.ctx + 16 - 2 * step, 16)
            passed.append(remote(o.at[source], o.at[source], sems, 7 + step, p.twin))
            passed[-1].start()
        yield
        for copy in copies:
            copy.wait_send()
        for copy in passed + [local]:
            copy.wait()


class ScatterCtx:
    def __init__(self, array):
        _, _, rows, width = array.shape
        self.arrays, self.groups = [array], {"chips", "twin"}
        self.outs = [jax.ShapeDtypeStruct((rows, width), F32)]
        self.in_spaces, self.out_spaces = [pltpu.VMEM], [pltpu.VMEM]
        self.scratch = [pltpu.VMEM((8, rows, width), BF)] * 3 + [pltpu.SemaphoreType.DMA((2, 15))]

    def run(self, p, ins, outs, scratch):
        (x,), (o,), (pair, sums, got, sems) = ins, outs, scratch
        copies = []
        order = list(range(1, 8)) + [0]
        for i, step in enumerate(order):
            chip = lax.rem(p.chip + step, 8)
            copies.append(remote(x.at[chip, 1 - p.core], pair.at[chip], sems, i, p.twin))
            copies[-1].start()
        for i, step in enumerate(order):
            if i % 3 == 0:
                yield
            chip = lax.rem(p.chip + step, 8)
            copies[i].wait_recv()
            both = x[chip, p.core].astype(F32) + pair[chip].astype(F32)
            if step > 0:
                sums[chip] = both.astype(BF)
                copies.append(remote(sums.at[chip], got.at[p.chip], sems, 7 + step, p.chips(step)))
                copies[-1].start()
            else:
                o[...] = both
        for step in range(1, 8):
            if step % 3 == 1:
                yield
            copies[7 + step].wait_recv()
            o[...] += got[lax.rem(p.chip + 8 - step, 8)].astype(F32)
        for copy in copies:
            copy.wait_send()


class SumCtx:
    def __init__(self, array):
        _, _, rows, width = array.shape
        self.arrays, self.groups = [array], {"chips", "twin"}
        self.outs = [jax.ShapeDtypeStruct(array.shape, BF)]
        self.in_spaces, self.out_spaces = [pltpu.VMEM], [pltpu.VMEM]
        self.scratch = [pltpu.VMEM((8, rows, width), BF)] * 3 + [pltpu.SemaphoreType.DMA((2, 23))]

    def run(self, p, ins, outs, scratch):
        (x,), (o,), (pair, sums, got, sems) = ins, outs, scratch
        first = remote(x.at[:, 1 - p.core], pair, sems, 0, p.twin)
        first.start()
        first.wait_recv()
        copies = [first]
        for step in range(1, 8):
            chip = lax.rem(p.chip + step, 8)
            sums[chip] = (x[chip, p.core].astype(F32) + pair[chip].astype(F32)).astype(BF)
            copies.append(remote(sums.at[chip], got.at[p.chip], sems, step, p.chips(step)))
            copies[-1].start()
        total = x[p.chip, p.core].astype(F32) + pair[p.chip].astype(F32)
        yield
        for step in range(1, 8):
            copies[step].wait_recv()
            total = total + got[lax.rem(p.chip + 8 - step, 8)].astype(F32)
        o[p.chip, p.core] = total.astype(BF)
        mine = o.at[p.chip, p.core]
        spread = []
        for step in range(1, 8):
            spread.append(remote(mine, mine, sems, 7 + step, p.chips(step)))
            spread[-1].start()
        passed = [remote(mine, mine, sems, 15, p.twin)]
        passed[0].start()
        yield
        for step in range(1, 8):
            spread[step - 1].wait_recv()
            piece = o.at[lax.rem(p.chip + 8 - step, 8), p.core]
            passed.append(remote(piece, piece, sems, 15 + step, p.twin))
            passed[-1].start()
        for copy in copies + spread:
            copy.wait_send()
        for copy in passed:
            copy.wait()


class ShareCtx:
    def __init__(self, array):
        self.arrays, self.groups = [array], {"chips", "twin", "others"}
        self.outs = [jax.ShapeDtypeStruct((16,) + array.shape, array.dtype)]
        self.in_spaces, self.out_spaces = [pl.ANY], [pl.ANY]
        self.scratch = [pltpu.SemaphoreType.DMA((2, 15)), pltpu.SemaphoreType.DMA]

    def run(self, p, ins, outs, scratch):
        (x,), (o,), (sems, own) = ins, outs, scratch
        copies = []
        for step in range(1, 16):
            to = {"ctx": lax.rem(p.ctx + step, 16)}
            copies.append(remote(x, o.at[p.ctx], sems, step - 1, to))
            copies[-1].start()
        copies.append(pltpu.make_async_copy(x, o.at[p.ctx], own))
        copies[-1].start()
        yield
        yield
        for copy in copies:
            copy.wait()


def transfer_kernel(parts, *refs):
    place = Place()
    groups = set().union(*(part.groups for part in parts))
    if "others" in groups:
        groups = groups - {"twin"}
    meet(place, groups)
    refs = list(refs)

    def take(count):
        taken = refs[:count]
        del refs[:count]
        return taken

    ins = [take(len(part.arrays)) for part in parts]
    outs = [take(len(part.outs)) for part in parts]
    scratch = [take(len(part.scratch)) for part in parts]
    active = [part.run(place, i, o, s) for part, i, o, s in zip(parts, ins, outs, scratch)]
    while active:
        active = [run for run in active if next(run, "end") != "end"]


def transfer(cid, name, us, *parts):
    spec = lambda space: pl.BlockSpec(memory_space=space)
    return pl.pallas_call(
        functools.partial(transfer_kernel, parts),
        out_shape=[out for part in parts for out in part.outs],
        in_specs=[spec(s) for part in parts for s in part.in_spaces],
        out_specs=[spec(s) for part in parts for s in part.out_spaces],
        scratch_shapes=[s for part in parts for s in part.scratch],
        compiler_params=pltpu.CompilerParams(
            collective_id=cid, has_side_effects=True, vmem_limit_bytes=40 * 2**20
        ),
        cost_estimate=cost(us),
        name=name,
    )(*[array for part in parts for array in part.arrays])


def interleave_kernel(gate_ref, up_ref, out_ref):
    out_ref[:, 0, :] = gate_ref[...].astype(F32)
    out_ref[:, 1, :] = up_ref[...].astype(F32)


def interleave(gate, up):
    rows, width = gate.shape
    step = 96
    spec = pl.BlockSpec((step, width), lambda i: (i, 0))
    return pl.pallas_call(
        interleave_kernel,
        grid=(rows // step,),
        out_shape=jax.ShapeDtypeStruct((rows, 2, width), F32),
        in_specs=[spec, spec],
        out_specs=pl.BlockSpec((step, 2, width), lambda i: (i, 0, 0)),
        cost_estimate=cost(6),
        name="interleave",
    )(gate, up)


NT = (((1,), (1,)), ((), ()))
TN = (((0,), (0,)), ((), ()))


def dot(a, b, dims):
    return lax.dot_general(a, b, dims, preferred_element_type=F32)


def masked_scores(q, keys, block, ctx, tokens):
    scores = dot(q, keys, NT)
    row = lax.rem(lax.broadcasted_iota(jnp.int32, scores.shape, 0), tokens) + ctx * tokens
    col = lax.broadcasted_iota(jnp.int32, scores.shape, 1) + block * KB
    return jnp.where(col <= row, scores, MASKED)


def attend_kernel(tokens, q_ref, kv_ref, out_ref, lse_ref, top, total, accum):
    ctx = lax.axis_index("ctx")
    last = (ctx * tokens) // KB
    q = q_ref[...]

    def block_of(index):
        return pl.ds(pl.multiple_of(index * KB, KB), KB)

    scores = masked_scores(q, kv_ref[block_of(last), :HD], last, ctx, tokens)
    start = jnp.max(scores, axis=-1, keepdims=True)
    probs = jnp.exp(scores - start)
    top[...] = jnp.broadcast_to(start, top.shape)
    total[...] = jnp.broadcast_to(jnp.sum(probs, axis=-1, keepdims=True), total.shape)
    accum[...] = jnp.dot(
        probs.astype(BF), kv_ref[block_of(last), HD:], preferred_element_type=F32
    )

    def body(index, carry):
        scores = dot(q, kv_ref[block_of(index), :HD], NT)
        old = top[:, :1]
        new = jnp.maximum(old, jnp.max(scores, axis=-1, keepdims=True))
        probs = jnp.exp(scores - new)
        keep = jnp.exp(old - new)
        top[...] = jnp.broadcast_to(new, top.shape)
        total[...] = total[...] * keep + jnp.sum(probs, axis=-1, keepdims=True)
        accum[...] = accum[...] * keep + jnp.dot(
            probs.astype(BF), kv_ref[block_of(index), HD:], preferred_element_type=F32
        )
        return carry

    lax.fori_loop(0, last, body, 0)
    out_ref[...] = accum[...] / total[:, :1]
    lse_ref[...] = top[...] + jnp.log(total[...])


def attend(q, kv, tokens):
    rows = q.shape[0]
    return pl.pallas_call(
        functools.partial(attend_kernel, tokens),
        out_shape=[
            jax.ShapeDtypeStruct((rows, HD), F32),
            jax.ShapeDtypeStruct((rows, 128), F32),
        ],
        scratch_shapes=[
            pltpu.VMEM((rows, 128), F32),
            pltpu.VMEM((rows, 128), F32),
            pltpu.VMEM((rows, HD), F32),
        ],
        compiler_params=pltpu.CompilerParams(vmem_limit_bytes=40 * 2**20),
        cost_estimate=cost(12),
        name="attend",
    )(q, kv)


def attend_back_kernel(tokens, q_ref, kv_ref, out_ref, lse_ref, d_ref, dq_ref, dkv_ref):
    ctx = lax.axis_index("ctx")
    last = (ctx * tokens) // KB
    q = q_ref[...]
    d_out = d_ref[...]
    lse = lse_ref[:, :1]
    delta = jnp.sum(d_out.astype(F32) * out_ref[...], axis=-1, keepdims=True)

    def block_of(index):
        return pl.ds(pl.multiple_of(index * KB, KB), KB)

    def work(index, scores):
        block = block_of(index)
        probs = jnp.exp(scores - lse)
        d_probs = dot(d_out, kv_ref[block, HD:], NT)
        d_scores = (probs * (d_probs - delta)).astype(BF)
        dkv_ref[block, :HD] = dot(d_scores, q, TN).astype(BF)
        dkv_ref[block, HD:] = dot(probs.astype(BF), d_out, TN).astype(BF)
        return jnp.dot(d_scores, kv_ref[block, :HD], preferred_element_type=F32)

    dq_ref[...] = work(last, masked_scores(q, kv_ref[block_of(last), :HD], last, ctx, tokens))

    def body(index, carry):
        dq_ref[...] += work(index, dot(q, kv_ref[block_of(index), :HD], NT))
        return carry

    lax.fori_loop(0, last, body, 0)

    def clear(index, carry):
        dkv_ref[block_of(index), :] = jnp.zeros((KB, 2 * HD), BF)
        return carry

    lax.fori_loop(last + 1, kv_ref.shape[0] // KB, clear, 0)


def attend_back(q, kv, out, lse, d_out, tokens):
    return pl.pallas_call(
        functools.partial(attend_back_kernel, tokens),
        out_shape=[
            jax.ShapeDtypeStruct(q.shape, F32),
            jax.ShapeDtypeStruct(kv.shape, BF),
        ],
        compiler_params=pltpu.CompilerParams(vmem_limit_bytes=40 * 2**20),
        cost_estimate=cost(20),
        name="attend_back",
    )(q, kv, out, lse, d_out)


def scale_of(values):
    return lax.rsqrt(jnp.mean(values * values, axis=-1, keepdims=True) + EPS)


def norm_back(v, r, g, dy):
    gdy = g * dy
    dv = r * gdy - v * (r * r * r) * jnp.mean(gdy * v, axis=-1, keepdims=True)
    return dv, dy * v * r


def rope(v, cosine, sine):
    a, b = v[..., : HD // 2], v[..., HD // 2 :]
    return jnp.concatenate([a * cosine - b * sine, b * cosine + a * sine], axis=-1)


def rope_back(u, cosine, sine):
    a, b = u[..., : HD // 2], u[..., HD // 2 :]
    return jnp.concatenate([a * cosine + b * sine, b * cosine - a * sine], axis=-1)


def on_device(hidden, w_qkv, w_out, norm_gains, qk_gains, w_gate_up, w_down, cotangent):
    tokens = hidden.shape[1]
    width = hidden.shape[2]
    x = hidden[0].astype(F32)
    cot = cotangent[0].astype(F32)
    positions = lax.axis_index("ctx") * tokens + jnp.arange(tokens, dtype=jnp.int32)
    freqs = ROPE_BASE ** (-jnp.arange(0, HD, 2, dtype=F32) / HD)
    angles = positions.astype(F32)[:, None] * freqs[None, :]
    cosine, sine = jnp.cos(angles), jnp.sin(angles)

    gain_part, qk_part = norm_gains.shape[0], qk_gains.shape[0]
    packed = jnp.concatenate(
        [
            jnp.pad(norm_gains.T, ((0, 0), (0, 256 - gain_part))),
            jnp.pad(qk_gains.T, ((0, 10), (0, 256 - qk_part))),
        ]
    )
    all_qkv, all_out, all_packed = transfer(
        1, "gather_weights", 30,
        GatherWsh(w_qkv, pair=True), GatherWsh(w_out, pair=True), DirectWsh("gather", packed),
    )
    full_qkv, full_out = all_qkv.reshape(-1, width), all_out.reshape(-1, width)
    gains = all_packed[:, :4, :gain_part].transpose(1, 0, 2).reshape(4, width).astype(F32)
    qk_gain = all_packed[:, 4:6, :qk_part].transpose(1, 0, 2).reshape(2, HD).astype(F32)

    r0 = scale_of(x)
    normed = (x * r0 * gains[0]).astype(BF)
    mixed = dot(normed, full_qkv, NT)
    q_raw = mixed[:, : HEADS * HD].reshape(tokens, HEADS, HD).transpose(1, 0, 2)
    k_raw = mixed[:, HEADS * HD : (HEADS + 1) * HD]
    rq, rk = scale_of(q_raw), scale_of(k_raw)
    q_low = (rope(q_raw * rq * qk_gain[0], cosine, sine) * HD ** (-0.5)).astype(BF)
    q_low = q_low.reshape(HEADS * tokens, HD)
    k_low = rope(k_raw * rk * qk_gain[1], cosine, sine).astype(BF)
    local_kv = jnp.concatenate([k_low, mixed[:, (HEADS + 1) * HD :].astype(BF)], axis=1)
    whole_kv, normed_all = transfer(2, "gather_kv", 25, GatherCtx(local_kv), GatherWsh(normed))
    whole_kv, normed_all = whole_kv.reshape(-1, 2 * HD), normed_all.reshape(-1, width)

    out_heads, lse = attend(q_low, whole_kv, tokens)
    attended = out_heads.reshape(HEADS, tokens, HD).transpose(1, 0, 2).reshape(tokens, HEADS * HD)
    attended = attended.astype(BF)
    branch = jnp.dot(attended, full_out, preferred_element_type=F32)
    r1 = scale_of(branch)
    resid = x + branch * r1 * gains[1]
    r2 = scale_of(resid)
    normed2 = (resid * r2 * gains[2]).astype(BF)

    (n2_all,) = transfer(3, "gather_normed2", 24, GatherWsh(normed2))
    n2_all = n2_all.reshape(-1, width)
    w_gate, w_up = w_gate_up[:, 0], w_gate_up[:, 1]
    gate, up = dot(n2_all, w_gate, NT), dot(n2_all, w_up, NT)
    gelu, gelu_pull = jax.vjp(functools.partial(jax.nn.gelu, approximate=True), gate)
    inner = (gelu * up).astype(BF)
    terms = jnp.dot(inner, w_down, preferred_element_type=F32).astype(BF)
    (branch2,) = transfer(4, "scatter_branch2", 24, ScatterWsh(terms.reshape(8, tokens, width)))

    r3 = scale_of(branch2)
    output = (resid + branch2 * r3 * gains[3]).astype(BF)
    d_branch2, dg3 = norm_back(branch2, r3, gains[3], cot)
    (d2_all,) = transfer(5, "gather_d_branch2", 24, GatherWsh(d_branch2.astype(BF)))
    d2_all = d2_all.reshape(-1, width)
    d_inner = dot(d2_all, w_down, NT)
    d_gate = (gelu_pull(d_inner * up)[0]).astype(BF)
    d_up = (d_inner * gelu).astype(BF)
    terms = (
        jnp.dot(d_gate, w_gate, preferred_element_type=F32)
        + jnp.dot(d_up, w_up, preferred_element_type=F32)
    ).astype(BF)
    (d_normed2,) = transfer(6, "scatter_d_normed2", 24, ScatterWsh(terms.reshape(8, tokens, width)))
    ff_grads = lax.psum(
        (
            dot(d_gate, n2_all, TN).astype(BF),
            dot(d_up, n2_all, TN).astype(BF),
            dot(inner, d2_all, TN).astype(BF),
        ),
        "ctx",
    )

    d_more, dg2 = norm_back(resid, r2, gains[2], d_normed2)
    d_resid = cot + d_more
    d_branch, dg1 = norm_back(branch, r1, gains[1], d_resid)
    branch_low = d_branch.astype(BF)
    d_attended = dot(branch_low, full_out, NT).astype(BF)
    d_heads = d_attended.reshape(tokens, HEADS, HD).transpose(1, 0, 2).reshape(HEADS * tokens, HD)
    d_q, d_kv = attend_back(q_low, whole_kv, out_heads, lse, d_heads, tokens)
    qkv_part, out_part = w_qkv.shape[0], w_out.shape[0]
    own_kv, db_all, at_all = transfer(
        7, "scatter_d_kv", 30,
        ScatterCtx(d_kv.reshape(8, 2, tokens, 2 * HD)),
        GatherWsh(branch_low),
        DirectWsh("scatter", attended.reshape(tokens, 8, out_part).transpose(1, 0, 2)),
    )
    grad_out = dot(at_all.reshape(-1, out_part), db_all.reshape(-1, width), TN)

    dq_rot = rope_back(d_q.reshape(HEADS, tokens, HD) * HD ** (-0.5), cosine, sine)
    d_q_raw, dgq = norm_back(q_raw, rq, qk_gain[0], dq_rot)
    dk_rot = rope_back(own_kv[:, :HD], cosine, sine)
    d_k_raw, dgk = norm_back(k_raw, rk, qk_gain[1], dk_rot)
    d_mixed = jnp.concatenate(
        [d_q_raw.transpose(1, 0, 2).reshape(tokens, HEADS * HD), d_k_raw, own_kv[:, HD:]], axis=1
    ).astype(BF)
    d_normed = jnp.dot(d_mixed, full_qkv, preferred_element_type=F32)
    d_input, dg0 = norm_back(x, r0, gains[0], d_normed)
    grad_hidden = (d_resid + d_input).astype(BF)

    dg = jnp.stack([jnp.sum(term, axis=0) for term in (dg0, dg1, dg2, dg3)])
    dqk = jnp.stack([jnp.sum(dgq, axis=(0, 1)), jnp.sum(dgk, axis=0)])
    dg = jnp.pad(dg.reshape(4, 8, gain_part).transpose(1, 0, 2), ((0, 0), (0, 0), (0, 256 - gain_part)))
    dqk = jnp.pad(dqk.reshape(2, 8, qk_part).transpose(1, 0, 2), ((0, 0), (0, 2), (0, 256 - qk_part)))
    dm_all, small_all = transfer(
        8, "columns_to_owners", 12,
        DirectWsh("scatter", d_mixed.reshape(tokens, 8, qkv_part).transpose(1, 0, 2)),
        DirectWsh("scatter", jnp.concatenate([dg, dqk], axis=1)),
    )
    grad_qkv = dot(dm_all.reshape(-1, qkv_part), normed_all, TN)
    both = jnp.concatenate([grad_qkv, grad_out], axis=0).astype(BF)
    share = both.shape[0] // 16
    room = -(-share // 16) * 16
    both = jnp.pad(both.reshape(8, 2, share, width), ((0, 0), (0, 0), (0, room - share), (0, 0)))
    grads, small_parts = transfer(
        9, "sum_grads", 25, SumCtx(both), ShareCtx(jnp.sum(small_all, axis=0))
    )
    grads = grads[:, :, :share].reshape(-1, width).astype(F32)
    small_sum = jnp.sum(small_parts, axis=0)
    return (
        output[None],
        grad_hidden[None],
        grads[:qkv_part],
        grads[qkv_part:],
        small_sum[:4, :gain_part].T,
        small_sum[4:6, :qk_part].T,
        interleave(ff_grads[0], ff_grads[1]),
        ff_grads[2].astype(F32),
    )


def solution(mesh):
    return jax.shard_map(
        on_device,
        mesh=mesh,
        in_specs=(
            P("wsh", "ctx", None),
            P("wsh", None),
            P("wsh", None),
            P("wsh", None),
            P("wsh", None),
            P("wsh", None, None),
            P("wsh", None),
            P("wsh", "ctx", None),
        ),
        out_specs=(
            P("wsh", "ctx", None),
            P("wsh", "ctx", None),
            P("wsh", None),
            P("wsh", None),
            P("wsh", None),
            P("wsh", None),
            P("wsh", None, None),
            P("wsh", None),
        ),
        check_vma=False,
    )
```

time: 604 us -> 404 us (0.67)
  waiting for transfers between devices: 128 us -> 2.16 us
  Pallas kernels: 318 us -> 263 us
  other arithmetic: 34.6 us -> 24.3 us
  local copies, waits for them, and re-layouts: 45.8 us -> 35.7 us
    psum x1, waiting for transfers between devices: 92.8 us -> 2.15 us  [on_device(): lax.psum((dot(d_gate, n2_all, TN).astype(BF), dot(d_up, n2_all, TN).astyp...]
    pallas_call x10, Pallas kernels: 315 us -> 260 us  [the longest x9 251 us: transfer(): pl.pallas_call(functools.partial(transfer_kernel, parts), out_shape=[out...]
    all_gather x3 -> x0, waiting for transfers between devices: 35 us -> none  [the longest x1 34.9 us: on_device(): normed_all = lax.all_gather(normed, 'wsh', axis=0, tiled=True)]
    dot_general x10, matrix products: 42.3 us -> 32.6 us  [dot(): return lax.dot_general(a, b, dims, preferred_element_type=F32)]
    unnamed x123 -> x96, local copies, waits for them, and re-layouts: 23 us -> 13.4 us
    reduce_sum x4 -> x0, other arithmetic: 6.6 us -> none  [the longest x1 2.12 us: on_device(): d_normed2 = jnp.sum(parts.astype(F32), axis=0)]
  transfers between devices with their start and end apart: 4 -> 1, of which waited for: 2 -> 1; matrix products, arithmetic and copies ran while one was open for 11% -> 11% of each run, Pallas kernels for 31% -> 28%
where the time goes in v2:
time: 404 us; the launch traced here: 397 us
  Pallas kernels  263 us (65%)
  matrix products  56.5 us (14%)
  local copies, waits for them, and re-layouts  35.7 us (9%)
  other arithmetic  24.3 us (6%)
  between operations  15.4 us (4%)
    pallas_call x9, Pallas kernels, transfer(): pl.pallas_call(functools.partial(transfer_kernel, parts), out_shape=[out...  251 us
    dot_general x10, matrix products, dot(): return lax.dot_general(a, b, dims, preferred_element_type=F32)  32.6 us
    unnamed x96, local copies, waits for them, and re-layouts  13.4 us
    pallas_call x1, Pallas kernels, interleave(): pl.pallas_call(interleave_kernel, grid=(rows // step,), out_shape=jax.Sha...  8.99 us
  transfers between devices with their start and end apart: 1, of which 1 were waited for; matrix products, arithmetic and copies ran while one was open for 11% of the time, Pallas kernels for 28%

profile of v2, /device:TPU:0, one launch (start us, length us, event | category | flops | bytes accessed | tf_op | source)
XLA Modules:
  0.0 396.9 jit_solution(6800827205031228563)
XLA Ops:
  7.3 0.8 fusion.61.refs_2_
  8.1 1.0 copy-done.10
  9.1 1.0 copy-done.11
  10.1 33.4 %gather_weights.1 = (bf16[8,192,1152]{2,1,0:T(8,128)(2,1)S(1)}, bf16[8,128,1152]{2,1,0:T(8,128)(2,1)S(1)}, bf16[8,16,256]{2,1,0:T(8,128)(2,1)S(1)}) custom-call(bf16[192,1152]{1,0:T(8,128)(2,1)S(1)} %copy-done.10, bf16[128,1152]{1,0:T(8,128)(2,1)S(1)} %copy-done.11, bf16[16,256]{1,0:T(8,128)(2,1)S(1)} %fusion.61.refs_2_), custom_call_target="tpu_custom_call" | custom-call | bytes 90000000 | tf_op jit(solution)/shard_map/gather_weights/pallas_call | solution.py:367
  43.5 1.8 copy-done.2
  45.3 1.4 copy-done.3
  46.7 1.1 fusion.23
  48.6 1.1 fusion.25.refs_1_
  49.7 3.4 fusion.40
  53.2 0.9 slice.125
  54.1 0.7 mul.703
  55.9 1.0 fusion.54
  57.1 1.2 copy.39
  59.2 0.8 multiply_subtract_fusion.2
  59.9 1.1 copy.23
  61.0 0.8 copy.24
  61.9 1.0 fusion.37.q_ref
  62.8 0.8 pad_maximum_fusion.2.refs_0_
  63.7 40.6 %gather_kv.1 = (bf16[16,128,512]{2,1,0:T(8,128)(2,1)S(1)}, bf16[8,128,1152]{2,1,0:T(8,128)(2,1)S(1)}) custom-call(bf16[128,512]{1,0:T(8,128)(2,1)S(1)} %pad_maximum_fusion.2.refs_0_, bf16[128,1152]{1,0:T(8,128)(2,1)S(1)} %fusion.25.refs_1_), custom_call_target="tpu_custom_call" | custom-call | bytes 75000000 | tf_op jit(solution)/shard_map/gather_kv/pallas_call | solution.py:367
  104.3 1.5 copy-done.7
  105.7 1.0 attend.1
  106.7 1.3 copy-done.4
  108.1 0.7 convert_element_type.152
  108.8 1.8 copy.25
  110.6 2.4 multiply_reduce_fusion.6
  113.4 22.7 %gather_normed2.1 = bf16[8,128,1152]{2,1,0:T(8,128)(2,1)S(1)} custom-call(bf16[128,1152]{1,0:T(8,128)(2,1)S(1)} %multiply_convert_fusion.2.refs_0_), custom_call_target="tpu_custom_call" | custom-call | bytes 72000000 | tf_op jit(solution)/shard_map/gather_normed2/pallas_call | solution.py:367
  136.2 5.7 %fusion.63 = (bf16[864,1,1152]{2,1,0:T(2,128)(2,1)S(1)}, bf16[864,1,1152]{2,1,0:T(2,128)(2,1)S(1)}) fusion(bf16[864,2,1152]{2,1,0:T(2,128)(2,1)S(1)} %copy-done.14), kind=kLoop, calls=%fused_computation.154 | loop fusion | bytes 7962624 | tf_op jit(solution)/shard_map/slice | solution.py:587
  141.9 2.5 fusion.10
  144.4 0.7 copy-done.21
  145.1 3.0 multiply_convert_fusion.1
  148.1 3.1 convolution_convert_fusion
  151.3 26.7 %scatter_branch2.1 = f32[128,1152]{1,0:T(8,128)S(1)} custom-call(bf16[8,128,1152]{2,1,0:T(8,128)(2,1)S(1)} %bitcast.157), custom_call_target="tpu_custom_call" | custom-call | bytes 72000000 | tf_op jit(solution)/shard_map/scatter_branch2/pallas_call | solution.py:367
  178.3 1.0 fusion.21
  179.3 19.2 %gather_d_branch2.1 = bf16[8,128,1152]{2,1,0:T(8,128)(2,1)S(1)} custom-call(bf16[128,1152]{1,0:T(8,128)(2,1)S(1)} %get-tuple-element.72.refs_0_), custom_call_target="tpu_custom_call" | custom-call | bytes 72000000 | tf_op jit(solution)/shard_map/gather_d_branch2/pallas_call | solution.py:367
  198.5 3.7 convolution_convert_fusion.1
  202.3 5.2 %multiply_convert_fusion = (bf16[1024,864]{0,1:T(8,128)(2,1)S(1)}, bf16[1024,864]{0,1:T(8,128)(2,1)S(1)}) fusion(f32[1024,864]{0,1:T(8,128)S(1)} %fusion.10, f32[1024,864]{0,1:T(8,128)S(1)} %get-tuple-element.97, bf16[1024,1152]{1,0:T(8,128)(2,1)S(1)} %bitcast.155, bf16[864,1152]{1,0:T(8,128)(2,1)S(1)} %copy-done), kind=kOutput, calls=%fused_computation.11 | convolution fusion | flops 2059665408 | bytes 14966784 | tf_op jit(solution)/shard_map/dot_general | solution.py:406
  207.5 3.8 convolution_convert_fusion.2
  211.3 3.8 convolution_convert_fusion.3
  215.2 7.8 %fusion.9 = f32[1024,1152]{1,0:T(8,128)} fusion(bf16[1024,864]{0,1:T(8,128)(2,1)} %copy-done.45, bf16[864,1,1152]{2,1,0:T(2,128)(2,1)} %copy-done.22), kind=kOutput, calls=%fused_computation.29 | convolution fusion | flops 2038431744 | bytes 8478720 | tf_op jit(solution)/shard_map/dot_general | solution.py:603
  223.2 7.0 %add_convert_fusion = bf16[1024,1152]{1,0:T(8,128)(2,1)S(1)} fusion(f32[1024,1152]{1,0:T(8,128)} %fusion.9, bf16[1024,864]{0,1:T(8,128)(2,1)} %copy-done.46, bf16[864,1,1152]{2,1,0:T(2,128)(2,1)} %copy-done.21), kind=kOutput, calls=%fused_computation.2 | convolution fusion | flops 2040791040 | bytes 10838016 | tf_op jit(solution)/shard_map/dot_general | solution.py:604
  230.2 23.4 %scatter_d_normed2.1 = f32[128,1152]{1,0:T(8,128)S(1)} custom-call(bf16[8,128,1152]{2,1,0:T(8,128)(2,1)S(1)} %bitcast.156), custom_call_target="tpu_custom_call" | custom-call | bytes 72000000 | tf_op jit(solution)/shard_map/scatter_d_normed2/pallas_call | solution.py:367
  253.9 2.3 multiply_reduce_fusion.1
  256.3 1.6 subtract_convert_fusion.refs_1_
  257.9 2.6 convolution_convert_fusion.4
  260.5 1.7 attend_back.1
  262.3 1.3 copy-done.8
  263.9 1.6 copy-done.9
  265.4 35.5 %scatter_d_kv.1 = (f32[128,512]{1,0:T(8,128)S(1)}, bf16[8,128,1152]{2,1,0:T(8,128)(2,1)S(1)}, bf16[8,128,128]{2,1,0:T(8,128)(2,1)S(1)}) custom-call(bf16[8,2,128,512]{3,2,1,0:T(8,128)(2,1)S(1)} %bitcast.159, bf16[128,1152]{1,0:T(8,128)(2,1)S(1)} %subtract_convert_fusion.refs_1_, bf16[8,128,128]{2,1,0:T(8,128)(2,1)S(1)} %bitcast.160), custom_call_target="tpu_custom_call" | custom-call | bytes 90000000 | tf_op jit(solution)/shard_map/scatter_d_kv/pallas_call | solution.py:367
  301.0 1.4 copy-done.6
  302.9 1.0 multiply_reduce_fusion.10
  304.0 1.0 multiply_subtract_fusion.3
  305.8 3.6 fusion.32
  309.9 12.2 %columns_to_owners.1 = (bf16[8,128,192]{2,1,0:T(8,128)(2,1)S(1)}, f32[8,8,256]{2,1,0:T(8,128)S(1)}) custom-call(bf16[8,128,192]{2,1,0:T(8,128)(2,1)S(1)} %bitcast.158, f32[8,8,256]{2,1,0:T(8,128)S(1)} %select_maximum_fusion.refs_1_), custom_call_target="tpu_custom_call" | custom-call | bytes 36000000 | tf_op jit(solution)/shard_map/columns_to_owners/pallas_call | solution.py:367
  322.1 2.2 fusion.8
  324.4 2.4 fusion.7
  327.1 37.4 %sum_grads.1 = (bf16[8,2,32,1152]{3,2,1,0:T(8,128)(2,1)S(1)}, f32[16,8,256]{2,1,0:T(8,128)S(1)}) custom-call(bf16[8,2,32,1152]{3,2,1,0:T(8,128)(2,1)S(1)} %pad.24.refs_0_, f32[8,256]{1,0:T(8,128)S(1)} %reduce_sum.198.refs_1_), custom_call_target="tpu_custom_call" | custom-call | bytes 75000000 | tf_op jit(solution)/shard_map/sum_grads/pallas_call | solution.py:367
  364.5 1.3 slice_convert_fusion
  365.8 2.6 reshape.317
  368.4 2.0 slice.140
  370.4 2.1 slice.139
  373.8 1.0 fusion.42
  374.7 2.1 all-reduce.8.cloned.1.call-done
  376.9 3.7 convert_element_type.178
  380.6 9.0 %interleave.1 = f32[864,2,1152]{2,1,0:T(2,128)} custom-call(bf16[864,1152]{1,0:T(8,128)(2,1)} %get-tuple-element.58.gate_ref, bf16[864,1152]{1,0:T(8,128)(2,1)} %get-tuple-element.59.up_ref), custom_call_target="tpu_custom_call" | custom-call | bytes 18000000 | tf_op jit(solution)/shard_map/interleave/pallas_call | solution.py:390
  (152 shorter events, 8.0 us)
Async XLA Ops:
  7.2 140.9 %copy-start = (bf16[864,1152]{1,0:T(8,128)(2,1)S(1)}, bf16[864,1152]{1,0:T(8,128)(2,1)}, u32[]{:S(2)}) copy-start(bf16[864,1152]{1,0:T(8,128)(2,1)} %param.14) | copy-start | bytes 5971972
  7.2 369.7 %all-reduce.8.cloned.1.call-start = ((), (), s32[]{:S(2)}) async-start(), calls=%async_computation | async-start | bytes 11943936 | tf_op jit(solution)/shard_map/psum | solution.py:607
  7.2 48.6 %copy-start.39 = (f32[128]{0:T(128)}, f32[128]{0:T(128)S(1)}, u32[]{:S(2)}) copy-start(f32[128]{0:T(128)S(1)} %multiply_power_fusion) | copy-start | bytes 1540
  8.1 1.0 copy-start.10
  9.1 1.0 copy-start.11
  43.5 1.8 copy-start.2
  45.3 1.4 copy-start.3
  48.4 4.7 %copy-start.35 = (f32[128]{0:T(128)}, f32[128]{0:T(128)S(1)}, u32[]{:S(2)}) copy-start(f32[128]{0:T(128)S(1)} %get-tuple-element.85) | copy-start | bytes 1540
  53.1 3.9 copy-start.20
  54.1 2.7 copy-start.41
  54.9 1.9 copy-start.30
  55.0 4.0 %copy-start.32 = (f32[256]{0:T(256)}, f32[256]{0:T(256)S(1)}, u32[]{:S(2)}) copy-start(f32[256]{0:T(256)S(1)} %mul.653) | copy-start | bytes 3076
  55.8 1.3 copy-start.37
  58.3 5.3 %copy-start.12 = (f32[128,1024]{0,1:T(8,128)}, f32[128,1024]{0,1:T(8,128)S(1)}, u32[]{:S(2)}) copy-start(f32[128,1024]{0,1:T(8,128)S(1)} %copy.39) | copy-start | bytes 1572868
  59.0 0.9 copy-start.28
  104.3 1.5 copy-start.7
  106.7 1.4 copy-start.4
  108.1 4.9 %copy-start.17 = (bf16[1,128,1152]{2,1,0:T(8,128)(2,1)S(1)}, bf16[1,128,1152]{2,1,0:T(8,128)(2,1)}, u32[]{:S(2)}) copy-start(bf16[1,128,1152]{2,1,0:T(8,128)(2,1)} %param.8) | copy-start | bytes 884740
  113.0 23.2 %copy-start.18 = (f32[128,1152]{1,0:T(8,128)}, f32[128,1152]{1,0:T(8,128)S(1)}, u32[]{:S(2)}) copy-start(f32[128,1152]{1,0:T(8,128)S(1)} %get-tuple-element.95) | copy-start | bytes 1769476
  113.0 23.2 %copy-start.14 = (bf16[864,2,1152]{2,1,0:T(2,128)(2,1)S(1)}, bf16[864,2,1152]{2,1,0:T(2,128)(2,1)}, u32[]{:S(2)}) copy-start(bf16[864,2,1152]{2,1,0:T(2,128)(2,1)} %param.13) | copy-start | bytes 11943940
  113.3 65.0 %copy-start.15 = (f32[128,1152]{1,0:T(8,128)}, f32[128,1152]{1,0:T(8,128)S(1)}, u32[]{:S(2)}) copy-start(f32[128,1152]{1,0:T(8,128)S(1)} %get-tuple-element.63) | copy-start | bytes 1769476
  141.9 2.5 copy-start.22
  141.9 3.2 copy-start.21
  151.2 26.9 %copy-start.23 = (bf16[1,128,1152]{2,1,0:T(8,128)(2,1)S(1)}, bf16[1,128,1152]{2,1,0:T(8,128)(2,1)}, u32[]{:S(2)}) copy-start(bf16[1,128,1152]{2,1,0:T(8,128)(2,1)} %param.15) | copy-start | bytes 884740
  151.2 26.9 %copy-start.27 = (f32[1152]{0:T(1024)S(1)}, f32[1152]{0:T(1024)}, u32[]{:S(2)}) copy-start(f32[1152]{0:T(1024)} %mul.703) | copy-start | bytes 13828
  207.5 3.8 copy-start.46
  207.5 3.8 copy-start.45
  215.1 7.8 %copy-start.26 = (bf16[4,128,256]{1,2,0:T(8,128)(2,1)S(1)}, bf16[4,128,256]{1,2,0:T(8,128)(2,1)}, u32[]{:S(2)}) copy-start(bf16[4,128,256]{1,2,0:T(8,128)(2,1)} %copy.25) | copy-start | bytes 786436
  230.2 23.5 %copy-start.16 = (f32[128,1152]{1,0:T(8,128)S(1)}, f32[128,1152]{1,0:T(8,128)}, u32[]{:S(2)}) copy-start(f32[128,1152]{1,0:T(8,128)} %copy-done.15) | copy-start | bytes 1769476
  230.2 23.8 %copy-start.24 = (bf16[1,128,1152]{2,1,0:T(8,128)(2,1)S(1)}, bf16[1,128,1152]{2,1,0:T(8,128)(2,1)}, u32[]{:S(2)}) copy-start(bf16[1,128,1152]{2,1,0:T(8,128)(2,1)} %param.15) | copy-start | bytes 884740
  256.3 4.2 %copy-start.5 = (bf16[16,128,512]{2,1,0:T(8,128)(2,1)S(1)}, bf16[16,128,512]{2,1,0:T(8,128)(2,1)}, u32[]{:S(2)}) copy-start(bf16[16,128,512]{2,1,0:T(8,128)(2,1)} %copy-done.4) | copy-start | bytes 6291460
  262.2 1.3 copy-start.8
  263.6 38.9 %copy-start.40 = (f32[128]{0:T(128)S(1)}, f32[128]{0:T(128)}, u32[]{:S(2)}) copy-start(f32[128]{0:T(128)} %copy-done.39) | copy-start | bytes 1540
  263.6 38.9 %copy-start.42 = (f32[128]{0:T(128)S(1)}, f32[128]{0:T(128)}, u32[]{:S(2)}) copy-start(f32[128]{0:T(128)} %copy-done.41) | copy-start | bytes 1540
  263.6 39.2 %copy-start.31 = (f32[256]{0:T(256)S(1)}, f32[256]{0:T(256)}, u32[]{:S(2)}) copy-start(f32[256]{0:T(256)} %copy-done.30) | copy-start | bytes 3076
  263.6 39.2 %copy-start.38 = (f32[128]{0:T(128)S(1)}, f32[128]{0:T(128)}, u32[]{:S(2)}) copy-start(f32[128]{0:T(128)} %copy-done.37) | copy-start | bytes 1540
  263.7 40.3 %copy-start.44 = (f32[128]{0:T(128)S(1)}, f32[128]{0:T(128)}, u32[]{:S(2)}) copy-start(f32[128]{0:T(128)} %get-tuple-element.86) | copy-start | bytes 1540
  263.8 1.6 copy-start.9
  265.4 40.0 %copy-start.13 = (f32[128,1024]{0,1:T(8,128)S(1)}, f32[128,1024]{0,1:T(8,128)}, u32[]{:S(2)}) copy-start(f32[128,1024]{0,1:T(8,128)} %copy-done.12) | copy-start | bytes 1572868
  265.4 40.0 %copy-start.29 = (f32[4,128]{1,0:T(4,128)S(1)}, f32[4,128]{1,0:T(4,128)}, u32[]{:S(2)}) copy-start(f32[4,128]{1,0:T(4,128)} %copy-done.28) | copy-start | bytes 6148
  265.4 40.0 %copy-start.33 = (f32[256]{0:T(256)S(1)}, f32[256]{0:T(256)}, u32[]{:S(2)}) copy-start(f32[256]{0:T(256)} %copy-done.32) | copy-start | bytes 3076
  301.0 1.4 copy-start.6
  302.4 3.2 copy-start.34
  305.0 0.8 copy-start.36
  368.4 5.4 %copy-start.19 = (f32[128,1152]{1,0:T(8,128)S(1)}, f32[128,1152]{1,0:T(8,128)}, u32[]{:S(2)}) copy-start(f32[128,1152]{1,0:T(8,128)} %get-tuple-element.61) | copy-start | bytes 1769476
  368.4 5.4 %copy-start.25 = (f32[128,1152]{1,0:T(8,128)S(1)}, f32[128,1152]{1,0:T(8,128)}, u32[]{:S(2)}) copy-start(f32[128,1152]{1,0:T(8,128)} %get-tuple-element.98) | copy-start | bytes 1769476
  368.4 5.4 %copy-start.43 = (f32[128]{0:T(128)S(1)}, f32[128]{0:T(128)}, u32[]{:S(2)}) copy-start(f32[128]{0:T(128)} %get-tuple-element.84) | copy-start | bytes 1540
  380.6 9.0 %copy-start.1 = (bf16[864,1152]{1,0:T(8,128)(2,1)S(1)}, bf16[864,1152]{1,0:T(8,128)(2,1)}, u32[]{:S(2)}) copy-start(bf16[864,1152]{1,0:T(8,128)(2,1)} %param.14) | copy-start | bytes 5971972
Sparse Core Ops, SparseCore 0:
  215.3 161.5 all-reduce.7

commit v3 on v2

v3 whole, which is shorter than its diff:
```python
import functools
import math

import jax
import jax.numpy as jnp
from jax import lax
from jax.experimental import pallas as pl
from jax.experimental.pallas import tpu as pltpu
from jax.sharding import PartitionSpec as P

HEADS = 4
HD = 256
KB = 512
EPS = 1e-06
ROPE_BASE = 1000000.0
MASKED = -1e30
MESH = pl.DeviceIdType.MESH
BF = jnp.bfloat16
F32 = jnp.float32
HBM = pltpu.HBM


def cost(us):
    return pl.CostEstimate(flops=0, bytes_accessed=int(us * 3.0e6), transcendentals=0)


class Grid:
    def __init__(self, axis, index, core):
        self.axis, self.core = axis, core
        self.h, self.y = lax.div(index, 4), lax.rem(index, 4)
        self.yp, self.ym, self.y2 = (lax.rem(self.y + k, 4) for k in (1, 3, 2))
        self.up, self.down = self.device(self.h, self.yp), self.device(self.h, self.ym)
        self.across = self.device(1 - self.h, self.y)

    def block(self, h, y):
        return h * 4 + y if self.axis == "wsh" else (h * 4 + y) * 2 + self.core

    def device(self, h, y):
        return {self.axis: self.block(h, y)}


class Place:
    def __init__(self):
        self.ctx, self.wsh = lax.axis_index("ctx"), lax.axis_index("wsh")
        self.chip, self.core = lax.div(self.ctx, 2), lax.rem(self.ctx, 2)
        self.grids = {"wsh": Grid("wsh", self.wsh, 0), "ctx": Grid("ctx", self.chip, self.core)}
        self.twin = {"ctx": self.ctx + 1 - 2 * self.core}

    def chips(self, step):
        return {"ctx": lax.rem(self.ctx + 2 * step, 16)}

    def row(self, step):
        return {"wsh": lax.rem(self.wsh + step, 8)}

    def peers(self, groups):
        found = []
        for axis, whole in (("wsh", "row"), ("ctx", "chips")):
            if axis in groups and whole not in groups:
                grid = self.grids[axis]
                found += [grid.up, grid.down, grid.across]
        if "row" in groups:
            found += [self.row(step) for step in range(1, 8)]
        if "chips" in groups:
            found += [self.chips(step) for step in range(1, 8)]
        if "others" in groups:
            found += [{"ctx": lax.rem(self.ctx + 2 * s + 1, 16)} for s in range(8)]
        elif "twin" in groups:
            found.append(self.twin)
        return found


def remote(src, dst, sems, i, device):
    return pltpu.make_async_remote_copy(
        src_ref=src, dst_ref=dst, send_sem=sems.at[0, i], recv_sem=sems.at[1, i],
        device_id=device, device_id_type=MESH,
    )


def meet(place, groups):
    barrier = pltpu.get_barrier_semaphore()
    peers = place.peers(groups)
    for peer in peers:
        pl.semaphore_signal(barrier, inc=1, device_id=peer, device_id_type=MESH)
    pl.semaphore_wait(barrier, len(peers))


def split_rows(count):
    return (count // 2 + 15) // 16 * 16


class Gather:
    def __init__(self, array, axis="wsh", pair=False):
        self.arrays, self.axis, self.pair = [array], axis, pair
        self.twins = pair or axis == "ctx"
        self.groups = {axis, "twin"} if self.twins else {axis}
        count = 16 if axis == "ctx" else 8
        self.outs = [jax.ShapeDtypeStruct((count,) + array.shape, array.dtype)]
        self.out_spaces, self.in_spaces = [HBM], [HBM]
        self.scratch = [pltpu.SemaphoreType.DMA((2, 19)), pltpu.SemaphoreType.DMA]

    def run(self, p, ins, outs, scratch):
        (x,), (o,), (sems, own) = ins, outs, scratch
        g = p.grids[self.axis]
        size = x.shape[0] // (2 if self.pair else 1)
        base = pl.multiple_of(p.core * size, size) if self.pair else 0
        half = split_rows(size)
        every, low, high = pl.ds(base, size), pl.ds(base, half), pl.ds(base + half, size - half)
        h, other = g.h, 1 - g.h
        me = g.block(h, g.y)
        copies = {}

        def send(i, block, rows, device, source=None):
            source = o.at[block, rows] if source is None else source
            copies[i] = remote(source, o.at[block, rows], sems, i, device)
            copies[i].start()

        def arrived(i, block, rows):
            copies[i].wait_recv()
            if self.twins:
                send(9 + i, block, rows, p.twin)

        send(2, me, every, g.across, x.at[every])
        send(0, me, every, g.up, x.at[every])
        send(1, me, every, g.down, x.at[every])
        if self.axis == "ctx":
            send(18, me, every, p.twin, x)
        local = pltpu.make_async_copy(x, o.at[me], own)
        local.start()
        yield
        block = g.block(other, g.y)
        arrived(2, block, every)
        send(5, block, every, g.up)
        send(6, block, every, g.down)
        yield
        block = g.block(h, g.ym)
        arrived(0, block, every)
        send(3, block, low, g.up)
        yield
        block = g.block(h, g.yp)
        arrived(1, block, every)
        send(4, block, high, g.down)
        yield
        block = g.block(other, g.ym)
        arrived(5, block, every)
        send(7, block, low, g.up)
        yield
        block = g.block(other, g.yp)
        arrived(6, block, every)
        send(8, block, high, g.down)
        yield
        block = g.block(h, g.y2)
        arrived(3, block, low)
        arrived(4, block, high)
        yield
        block = g.block(other, g.y2)
        arrived(7, block, low)
        arrived(8, block, high)
        yield
        for i, copy in copies.items():
            copy.wait_send()
            if i >= 9:
                copy.wait_recv()
        local.wait()


class Scatter:
    def __init__(self, array, axis="wsh", dtype=F32):
        _, rows, width = array.shape
        self.arrays, self.axis, self.groups = [array], axis, {axis}
        self.outs = [jax.ShapeDtypeStruct((rows, width), dtype)]
        self.in_spaces, self.out_spaces = [pltpu.VMEM], [pltpu.VMEM]
        half = split_rows(rows)
        low, high = pltpu.VMEM((2, half, width), BF), pltpu.VMEM((2, rows - half, width), BF)
        whole = pltpu.VMEM((2, rows, width), BF)
        self.scratch = [low, high, low, high, whole, whole, whole, pltpu.SemaphoreType.DMA((2, 13))]

    def run(self, p, ins, outs, scratch):
        (x,), (o,), (buf_a, buf_b, sum_c, sum_d, buf_c, buf_d, buf_e, sems) = ins, outs, scratch
        g = p.grids[self.axis]
        rows = o.shape[0]
        half = split_rows(rows)
        low, high = pl.ds(0, half), pl.ds(half, rows - half)
        planes = ((1 - g.h) * 4, g.h * 4)
        copies = {}

        def send(i, source, target, device):
            copies[i] = remote(source, target, sems, i, device)
            copies[i].start()

        for k, plane in enumerate(planes):
            send(k, x.at[plane + g.y2, low], buf_a.at[k], g.up)
            send(2 + k, x.at[plane + g.y2, high], buf_b.at[k], g.down)
            send(4 + k, x.at[plane + g.yp, high], buf_c.at[k, high], g.up)
            send(6 + k, x.at[plane + g.ym, low], buf_d.at[k, low], g.down)
        for k, plane in enumerate(planes):
            yield
            copies[k].wait_recv()
            sum_c[k] = (x[plane + g.yp, :half].astype(F32) + buf_a[k].astype(F32)).astype(BF)
            send(8 + k, sum_c.at[k], buf_c.at[k, low], g.up)
            yield
            copies[2 + k].wait_recv()
            sum_d[k] = (x[plane + g.ym, half:].astype(F32) + buf_b[k].astype(F32)).astype(BF)
            send(10 + k, sum_d.at[k], buf_d.at[k, high], g.down)
        for k, plane in enumerate(planes):
            yield
            for i in (4, 6, 8, 10):
                copies[i + k].wait_recv()
            total = x[plane + g.y].astype(F32) + buf_c[k].astype(F32) + buf_d[k].astype(F32)
            if k == 0:
                buf_e[0] = total.astype(BF)
                send(12, buf_e.at[0], buf_e.at[1], g.across)
            else:
                yield
                copies[12].wait_recv()
                o[...] = (total + buf_e[1].astype(F32)).astype(o.dtype)
        for copy in copies.values():
            copy.wait_send()


class DirectWsh:
    def __init__(self, mode, array):
        self.mode, self.arrays, self.groups = mode, [array], {"row"}
        shape = ((8,) + array.shape) if mode == "gather" else array.shape
        self.outs = [jax.ShapeDtypeStruct(shape, array.dtype)]
        self.in_spaces, self.out_spaces = [HBM], [HBM]
        self.scratch = [pltpu.SemaphoreType.DMA((2, 7)), pltpu.SemaphoreType.DMA]

    def run(self, p, ins, outs, scratch):
        (x,), (o,), (sems, own) = ins, outs, scratch
        pick = (lambda i: x) if self.mode == "gather" else (lambda i: x.at[i])
        copies = []
        for step in range(1, 8):
            to = p.row(step)
            copies.append(remote(pick(to["wsh"]), o.at[p.wsh], sems, step - 1, to))
            copies[-1].start()
        copies.append(pltpu.make_async_copy(pick(p.wsh), o.at[p.wsh], own))
        copies[-1].start()
        yield
        yield
        yield
        for copy in copies:
            copy.wait()


class ScatterCtx:
    def __init__(self, array):
        _, _, rows, width = array.shape
        self.arrays, self.groups = [array], {"chips", "twin"}
        self.outs = [jax.ShapeDtypeStruct((rows, width), F32)]
        self.in_spaces, self.out_spaces = [pltpu.VMEM], [pltpu.VMEM]
        self.scratch = [pltpu.VMEM((8, rows, width), BF)] * 3 + [pltpu.SemaphoreType.DMA((2, 15))]

    def run(self, p, ins, outs, scratch):
        (x,), (o,), (pair, sums, got, sems) = ins, outs, scratch
        copies = []
        order = list(range(1, 8)) + [0]
        for i, step in enumerate(order):
            chip = lax.rem(p.chip + step, 8)
            copies.append(remote(x.at[chip, 1 - p.core], pair.at[chip], sems, i, p.twin))
            copies[-1].start()
        for i, step in enumerate(order):
            if i % 3 == 0:
                yield
            chip = lax.rem(p.chip + step, 8)
            copies[i].wait_recv()
            both = x[chip, p.core].astype(F32) + pair[chip].astype(F32)
            if step > 0:
                sums[chip] = both.astype(BF)
                copies.append(remote(sums.at[chip], got.at[p.chip], sems, 7 + step, p.chips(step)))
                copies[-1].start()
            else:
                o[...] = both
        for step in range(1, 8):
            if step % 3 == 1:
                yield
            copies[7 + step].wait_recv()
            o[...] += got[lax.rem(p.chip + 8 - step, 8)].astype(F32)
        for copy in copies:
            copy.wait_send()


class SumCtx:
    def __init__(self, array):
        _, _, rows, width = array.shape
        self.arrays, self.groups = [array], {"chips", "twin"}
        self.outs = [jax.ShapeDtypeStruct(array.shape, BF)]
        self.in_spaces, self.out_spaces = [pltpu.VMEM], [pltpu.VMEM]
        self.scratch = [pltpu.VMEM((8, rows, width), BF)] * 3 + [pltpu.SemaphoreType.DMA((2, 23))]

    def run(self, p, ins, outs, scratch):
        (x,), (o,), (pair, sums, got, sems) = ins, outs, scratch
        first = remote(x.at[:, 1 - p.core], pair, sems, 0, p.twin)
        first.start()
        first.wait_recv()
        copies = [first]
        for step in range(1, 8):
            chip = lax.rem(p.chip + step, 8)
            sums[chip] = (x[chip, p.core].astype(F32) + pair[chip].astype(F32)).astype(BF)
            copies.append(remote(sums.at[chip], got.at[p.chip], sems, step, p.chips(step)))
            copies[-1].start()
        total = x[p.chip, p.core].astype(F32) + pair[p.chip].astype(F32)
        yield
        for step in range(1, 8):
            copies[step].wait_recv()
            total = total + got[lax.rem(p.chip + 8 - step, 8)].astype(F32)
        o[p.chip, p.core] = total.astype(BF)
        mine = o.at[p.chip, p.core]
        spread = []
        for step in range(1, 8):
            spread.append(remote(mine, mine, sems, 7 + step, p.chips(step)))
            spread[-1].start()
        passed = [remote(mine, mine, sems, 15, p.twin)]
        passed[0].start()
        yield
        for step in range(1, 8):
            spread[step - 1].wait_recv()
            piece = o.at[lax.rem(p.chip + 8 - step, 8), p.core]
            passed.append(remote(piece, piece, sems, 15 + step, p.twin))
            passed[-1].start()
        for copy in copies + spread:
            copy.wait_send()
        for copy in passed:
            copy.wait()


class ShareCtx:
    def __init__(self, array):
        self.arrays, self.groups = [array], {"chips", "twin", "others"}
        self.outs = [jax.ShapeDtypeStruct((16,) + array.shape, array.dtype)]
        self.in_spaces, self.out_spaces = [HBM], [HBM]
        self.scratch = [pltpu.SemaphoreType.DMA((2, 15)), pltpu.SemaphoreType.DMA]

    def run(self, p, ins, outs, scratch):
        (x,), (o,), (sems, own) = ins, outs, scratch
        copies = []
        for step in range(1, 16):
            to = {"ctx": lax.rem(p.ctx + step, 16)}
            copies.append(remote(x, o.at[p.ctx], sems, step - 1, to))
            copies[-1].start()
        copies.append(pltpu.make_async_copy(x, o.at[p.ctx], own))
        copies[-1].start()
        yield
        yield
        for copy in copies:
            copy.wait()


def rows_loop(count, body):
    lax.fori_loop(0, count // 16, lambda i, _: (body(pl.ds(pl.multiple_of(i * 16, 16), 16)), 0)[1], 0)


class FeedForwardGrads:
    def __init__(self, d_gate, d_up, inner, normed, d_branch):
        units, width = d_gate.shape[1], normed.shape[1]
        self.arrays, self.groups = [d_gate, d_up, inner, normed, d_branch], {"ctx", "twin"}
        granules = -(-3 * units // 256)
        early = granules * 5 // 9
        self.pieces = (early * 16, (granules - early) * 16)
        sums = [pltpu.VMEM((8, rows, width), BF) for rows in self.pieces]
        late = jax.ShapeDtypeStruct(sums[1].shape, BF)
        self.scatter = Scatter(jax.ShapeDtypeStruct(sums[0].shape, BF), "ctx", BF)
        self.outs = self.scatter.outs + [late]
        self.in_spaces, self.out_spaces = [pltpu.VMEM] * 5, [pltpu.VMEM] * 2
        self.scratch = [pltpu.VMEM((16 * rows, width), BF) for rows in self.pieces]
        self.scratch += sums + sums[:1] + [pltpu.SemaphoreType.DMA((2, 16))] + self.scatter.scratch

    def run(self, p, ins, outs, scratch):
        d_gate, d_up, inner, normed, d_branch = ins
        first, second, pair_first, pair_second, sums, sems, *rest = scratch
        units = d_gate.shape[1]
        split = first.shape[0]
        twins = []

        def put(at, value):
            end = at + value.shape[0]
            if at < split:
                first[at : min(end, split)] = value[: min(end, split) - at]
            if end > split:
                second[max(at, split) - split : end - split] = value[max(at, split) - at :]

        def swap(whole, pair, number):
            size = pair.shape[1]
            for chip in range(8):
                there = pl.ds(pl.multiple_of((2 * chip + 1 - p.core) * size, 16), size)
                twins.append(remote(whole.at[there], pair.at[chip], sems, 8 * number + chip, p.twin))
                twins[-1].start()

        def add(whole, pair, result, number):
            size = pair.shape[1]
            for chip in range(8):
                here = pl.ds(pl.multiple_of((2 * chip + p.core) * size, 16), size)
                twins[8 * number + chip].wait_recv()
                result[chip] = (whole[here].astype(F32) + pair[chip].astype(F32)).astype(BF)

        yield
        started = False
        for number, (left, right) in enumerate(((d_gate, normed), (d_up, normed), (inner, d_branch))):
            for start in range(0, units, 256):
                stop = min(start + 256, units)
                put(number * units + start, dot(left[:, start:stop], right[...], TN).astype(BF))
                if not started and number * units + stop >= split:
                    started = True
                    swap(first, pair_first, 0)
            yield
        missing = second.shape[0] - (3 * units - split)
        if missing:
            second[second.shape[0] - missing :] = jnp.zeros((missing, second.shape[1]), BF)
        swap(second, pair_second, 1)
        add(first, pair_first, sums, 0)
        middle = self.scatter.run(p, [sums], outs[:1], rest)
        next(middle)
        add(second, pair_second, outs[1], 1)
        yield
        yield from middle
        for copy in twins:
            copy.wait_send()


class Unpair:
    def __init__(self, array):
        self.arrays, self.groups = [array], set()
        self.outs = [jax.ShapeDtypeStruct((array.shape[0], array.shape[2]), BF)] * 2
        self.in_spaces, self.out_spaces, self.scratch = [pltpu.VMEM], [pltpu.VMEM] * 2, []

    def run(self, p, ins, outs, scratch):
        def step(rows):
            outs[0][rows] = ins[0][rows, 0, :]
            outs[1][rows] = ins[0][rows, 1, :]

        rows_loop(ins[0].shape[0], step)
        yield


class Tables:
    def __init__(self, tokens):
        self.tokens, self.arrays, self.groups = tokens, [], set()
        self.outs = [jax.ShapeDtypeStruct((tokens, HD // 2), F32)] * 2
        self.in_spaces, self.out_spaces, self.scratch = [], [pltpu.VMEM] * 2, []

    def run(self, p, ins, outs, scratch):
        shape = outs[0].shape
        token = lax.broadcasted_iota(jnp.int32, shape, 0) + p.ctx * self.tokens
        power = lax.broadcasted_iota(jnp.int32, shape, 1).astype(F32) * (-2.0 / HD)
        angles = token.astype(F32) * jnp.exp(power * math.log(ROPE_BASE))
        outs[0][...] = jnp.cos(angles)
        outs[1][...] = jnp.sin(angles)
        yield


def transfer_kernel(parts, *refs):
    place = Place()
    groups = set().union(*(part.groups for part in parts))
    if "others" in groups:
        groups = groups - {"twin"}
    meet(place, groups)
    refs = list(refs)

    def take(count):
        taken = refs[:count]
        del refs[:count]
        return taken

    ins = [take(len(part.arrays)) for part in parts]
    outs = [take(len(part.outs)) for part in parts]
    scratch = [take(len(part.scratch)) for part in parts]
    active = [part.run(place, i, o, s) for part, i, o, s in zip(parts, ins, outs, scratch)]
    while active:
        active = [run for run in active if next(run, "end") != "end"]


def transfer(cid, name, us, *parts):
    spec = lambda space: pl.BlockSpec(memory_space=space)
    return pl.pallas_call(
        functools.partial(transfer_kernel, parts),
        out_shape=[out for part in parts for out in part.outs],
        in_specs=[spec(s) for part in parts for s in part.in_spaces],
        out_specs=[spec(s) for part in parts for s in part.out_spaces],
        scratch_shapes=[s for part in parts for s in part.scratch],
        compiler_params=pltpu.CompilerParams(
            collective_id=cid, has_side_effects=True, vmem_limit_bytes=48 * 2**20
        ),
        cost_estimate=cost(us),
        name=name,
    )(*[array for part in parts for array in part.arrays])


NT = (((1,), (1,)), ((), ()))
TN = (((0,), (0,)), ((), ()))


def dot(a, b, dims):
    return lax.dot_general(a, b, dims, preferred_element_type=F32)


def masked_scores(q, keys, block, ctx, tokens):
    scores = dot(q, keys, NT)
    row = lax.rem(lax.broadcasted_iota(jnp.int32, scores.shape, 0), tokens) + ctx * tokens
    col = lax.broadcasted_iota(jnp.int32, scores.shape, 1) + block * KB
    return jnp.where(col <= row, scores, MASKED)


def widen_kernel(first, gate_ref, up_ref, more_ref, low_ref, both_ref, down_ref):
    both_ref[:, 0, :] = gate_ref[...].astype(F32)
    down_ref[...] = low_ref[...].astype(F32)

    @pl.when(pl.program_id(0) < first)
    def _():
        both_ref[:, 1, :] = up_ref[...].astype(F32)

    @pl.when(pl.program_id(0) >= first)
    def _():
        both_ref[:, 1, :] = more_ref[...].astype(F32)


def widen(early, late, rows):
    width = early.shape[1]
    step = 96
    count = rows // step
    first = early.shape[0] // step - count
    spec = lambda index: pl.BlockSpec((step, width), lambda i: (index(i), 0))
    return pl.pallas_call(
        functools.partial(widen_kernel, first),
        grid=(count,),
        out_shape=[
            jax.ShapeDtypeStruct((rows, 2, width), F32),
            jax.ShapeDtypeStruct((rows, width), F32),
        ],
        in_specs=[
            spec(lambda i: i),
            spec(lambda i: jnp.minimum(i, first - 1) + count),
            spec(lambda i: jnp.maximum(i - first, 0)),
            spec(lambda i: i + count - first),
        ],
        out_specs=[pl.BlockSpec((step, 2, width), lambda i: (i, 0, 0)), spec(lambda i: i)],
        cost_estimate=cost(9),
        name="widen",
    )(early, early, late, late)


def scale_of(values):
    return lax.rsqrt(jnp.mean(values * values, axis=-1, keepdims=True) + EPS)


def norm_back(v, r, g, dy):
    gdy = g * dy
    dv = r * gdy - v * (r * r * r) * jnp.mean(gdy * v, axis=-1, keepdims=True)
    return dv, dy * v * r


def rope(v, cosine, sine):
    a, b = v[..., : HD // 2], v[..., HD // 2 :]
    return jnp.concatenate([a * cosine - b * sine, b * cosine + a * sine], axis=-1)


def rope_back(u, cosine, sine):
    a, b = u[..., : HD // 2], u[..., HD // 2 :]
    return jnp.concatenate([a * cosine + b * sine, b * cosine - a * sine], axis=-1)


def compute(kernel, name, us, outs, scratch, *args):
    return pl.pallas_call(
        kernel,
        out_shape=[jax.ShapeDtypeStruct(shape, dtype) for shape, dtype in outs],
        scratch_shapes=scratch,
        compiler_params=pltpu.CompilerParams(vmem_limit_bytes=28 * 2**20),
        cost_estimate=cost(us),
        name=name,
    )(*args)


def tiled(kernel, name, us, widths, rowed, whole):
    rows, step = rowed[0].shape[0], 256
    spec = lambda width: pl.BlockSpec((step, width), lambda i: (i, 0))
    return pl.pallas_call(
        kernel,
        grid=(rows // step,),
        out_shape=[jax.ShapeDtypeStruct((rows, width), BF) for width in widths],
        in_specs=[spec(a.shape[1]) for a in rowed]
        + [pl.BlockSpec(a.shape, lambda i: (0, 0)) for a in whole],
        out_specs=[spec(width) for width in widths],
        compiler_params=pltpu.CompilerParams(vmem_limit_bytes=40 * 2**20),
        cost_estimate=cost(us),
        name=name,
    )(*rowed, *whole)


def forward_kernel(n_ref, gate_ref, up_ref, down_ref, inner_ref, gelu_ref, slope_ref, terms_ref):
    gate = dot(n_ref[...], gate_ref[...], NT)
    up = dot(n_ref[...], up_ref[...], NT)
    bend, grow = math.sqrt(2.0 / math.pi), 0.044715
    square = gate * gate
    wave = jnp.tanh(bend * gate * (1.0 + grow * square))
    rise = 0.5 * (1.0 + wave)
    gelu = gate * rise
    slope = rise + 0.5 * bend * gate * (1.0 - wave * wave) * (1.0 + 3.0 * grow * square)
    gelu_ref[...] = gelu.astype(BF)
    slope_ref[...] = (up * slope).astype(BF)
    inner_ref[...] = (gelu * up).astype(BF)
    terms_ref[...] = jnp.dot(inner_ref[...], down_ref[...], preferred_element_type=F32).astype(BF)


def backward_kernel(d_ref, gelu_ref, slope_ref, gate_ref, up_ref, down_ref, dgate_ref, dup_ref, terms_ref):
    d_inner = dot(d_ref[...], down_ref[...], NT)
    dgate_ref[...] = (d_inner * slope_ref[...].astype(F32)).astype(BF)
    dup_ref[...] = (d_inner * gelu_ref[...].astype(F32)).astype(BF)
    terms_ref[...] = (
        jnp.dot(dgate_ref[...], gate_ref[...], preferred_element_type=F32)
        + jnp.dot(dup_ref[...], up_ref[...], preferred_element_type=F32)
    ).astype(BF)


def prepare_kernel(x_ref, w_ref, g_ref, qk_ref, cos_ref, sin_ref, normed_ref, raw_ref, q_ref, kv_ref):
    x = x_ref[...].astype(F32)
    tokens = x.shape[0]
    normed = (x * scale_of(x) * g_ref[0:1]).astype(BF)
    normed_ref[...] = normed
    raw_ref[...] = dot(normed, w_ref[...], NT)
    cosine, sine = cos_ref[...], sin_ref[...]
    for head in range(HEADS + 1):
        v = raw_ref[:, head * HD : (head + 1) * HD]
        column = 0 if head < HEADS else 1
        turned = rope(v * scale_of(v) * qk_ref[column : column + 1], cosine, sine)
        if head < HEADS:
            q_ref[head * tokens : (head + 1) * tokens] = (turned * HD ** (-0.5)).astype(BF)
        else:
            kv_ref[:, :HD] = turned.astype(BF)
    kv_ref[:, HD:] = raw_ref[:, (HEADS + 1) * HD :].astype(BF)


def attend_kernel(q_ref, kv_ref, x_ref, w_ref, g_ref, out_ref, lse_ref, att_ref, branch_ref,
                  resid_ref, normed_ref, top, total, accum):
    ctx = lax.axis_index("ctx")
    tokens = x_ref.shape[0]
    last = lax.div(ctx * tokens, KB)
    q = q_ref[...]

    def block_of(index):
        return pl.ds(pl.multiple_of(index * KB, KB), KB)

    scores = masked_scores(q, kv_ref[block_of(last), :HD], last, ctx, tokens)
    start = jnp.max(scores, axis=-1, keepdims=True)
    probs = jnp.exp(scores - start)
    top[...] = jnp.broadcast_to(start, top.shape)
    total[...] = jnp.broadcast_to(jnp.sum(probs, axis=-1, keepdims=True), total.shape)
    accum[...] = jnp.dot(
        probs.astype(BF), kv_ref[block_of(last), HD:], preferred_element_type=F32
    )

    def body(index, carry):
        scores = dot(q, kv_ref[block_of(index), :HD], NT)
        old = top[:, :1]
        new = jnp.maximum(old, jnp.max(scores, axis=-1, keepdims=True))
        probs = jnp.exp(scores - new)
        keep = jnp.exp(old - new)
        top[...] = jnp.broadcast_to(new, top.shape)
        total[...] = total[...] * keep + jnp.sum(probs, axis=-1, keepdims=True)
        accum[...] = accum[...] * keep + jnp.dot(
            probs.astype(BF), kv_ref[block_of(index), HD:], preferred_element_type=F32
        )
        return carry

    lax.fori_loop(0, last, body, 0)
    out_ref[...] = accum[...] / total[:, :1]
    lse_ref[...] = top[...] + jnp.log(total[...])
    for head in range(HEADS):
        att_ref[:, head * HD : (head + 1) * HD] = out_ref[
            head * tokens : (head + 1) * tokens
        ].astype(BF)
    branch = jnp.dot(att_ref[...], w_ref[...], preferred_element_type=F32)
    branch_ref[...] = branch
    resid = x_ref[...].astype(F32) + branch * scale_of(branch) * g_ref[1:2]
    resid_ref[...] = resid
    normed_ref[...] = (resid * scale_of(resid) * g_ref[2:3]).astype(BF)


def attend_back_kernel(dn_ref, resid_ref, branch_ref, cot_ref, g_ref, w_ref, q_ref, kv_ref, out_ref,
                       lse_ref, dres_ref, low_ref, dg_ref, dq_ref, dkv_ref, d_ref):
    ctx = lax.axis_index("ctx")
    tokens = resid_ref.shape[0]
    last = lax.div(ctx * tokens, KB)
    resid = resid_ref[...]
    d_more, dg2 = norm_back(resid, scale_of(resid), g_ref[2:3], dn_ref[...])
    d_resid = cot_ref[...].astype(F32) + d_more
    dres_ref[...] = d_resid
    branch = branch_ref[...]
    d_branch, dg1 = norm_back(branch, scale_of(branch), g_ref[1:2], d_resid)
    low_ref[...] = d_branch.astype(BF)
    dg_ref[0:1] = jnp.sum(dg1, axis=0, keepdims=True)
    dg_ref[1:2] = jnp.sum(dg2, axis=0, keepdims=True)
    d_att = dot(low_ref[...], w_ref[...], NT)
    for head in range(HEADS):
        d_ref[head * tokens : (head + 1) * tokens] = d_att[:, head * HD : (head + 1) * HD].astype(BF)
    q = q_ref[...]
    d_out = d_ref[...]
    lse = lse_ref[:, :1]
    delta = jnp.sum(d_out.astype(F32) * out_ref[...], axis=-1, keepdims=True)

    def block_of(index):
        return pl.ds(pl.multiple_of(index * KB, KB), KB)

    def work(index, scores):
        block = block_of(index)
        probs = jnp.exp(scores - lse)
        d_probs = dot(d_out, kv_ref[block, HD:], NT)
        d_scores = (probs * (d_probs - delta)).astype(BF)
        dkv_ref[block, :HD] = dot(d_scores, q, TN).astype(BF)
        dkv_ref[block, HD:] = dot(probs.astype(BF), d_out, TN).astype(BF)
        return jnp.dot(d_scores, kv_ref[block, :HD], preferred_element_type=F32)

    dq_ref[...] = work(last, masked_scores(q, kv_ref[block_of(last), :HD], last, ctx, tokens))

    def body(index, carry):
        dq_ref[...] += work(index, dot(q, kv_ref[block_of(index), :HD], NT))
        return carry

    lax.fori_loop(0, last, body, 0)

    def clear(index, carry):
        dkv_ref[block_of(index), :] = jnp.zeros((KB, 2 * HD), BF)
        return carry

    lax.fori_loop(last + 1, kv_ref.shape[0] // KB, clear, 0)


def finish_kernel(own_ref, dq_ref, raw_ref, cos_ref, sin_ref, w_ref, x_ref, g_ref, qk_ref, dres_ref,
                  parts_ref, grad_ref, dg_ref, dqk_ref, mixed_ref):
    tokens = x_ref.shape[0]
    cosine, sine = cos_ref[...], sin_ref[...]
    total = jnp.zeros((1, HD), F32)
    for head in range(HEADS + 1):
        v = raw_ref[:, head * HD : (head + 1) * HD]
        if head < HEADS:
            u = dq_ref[head * tokens : (head + 1) * tokens] * HD ** (-0.5)
        else:
            u = own_ref[:, :HD]
        column = 0 if head < HEADS else 1
        dv, dg = norm_back(
            v, scale_of(v), qk_ref[column : column + 1], rope_back(u, cosine, sine)
        )
        mixed_ref[:, head * HD : (head + 1) * HD] = dv.astype(BF)
        dg = jnp.sum(dg, axis=0, keepdims=True)
        if head < HEADS:
            total = total + dg
        else:
            dqk_ref[0:1] = total
            dqk_ref[1:2] = dg
    mixed_ref[:, (HEADS + 1) * HD :] = own_ref[:, HD:].astype(BF)
    d_mixed = mixed_ref[...]
    part = parts_ref.shape[2]
    for i in range(parts_ref.shape[0]):
        parts_ref[i] = d_mixed[:, i * part : (i + 1) * part]
    d_normed = jnp.dot(d_mixed, w_ref[...], preferred_element_type=F32)
    x = x_ref[...].astype(F32)
    d_input, dg0 = norm_back(x, scale_of(x), g_ref[0:1], d_normed)
    dg_ref[...] = jnp.sum(dg0, axis=0, keepdims=True)
    grad_ref[...] = (dres_ref[...] + d_input).astype(BF)


def on_device(hidden, w_qkv, w_out, norm_gains, qk_gains, w_gate_up, w_down, cotangent):
    tokens = hidden.shape[1]
    width = hidden.shape[2]
    cot = cotangent[0].astype(F32)
    gain_part, qk_part = norm_gains.shape[0], qk_gains.shape[0]
    packed = jnp.concatenate(
        [
            jnp.pad(norm_gains.T, ((0, 0), (0, 256 - gain_part))),
            jnp.pad(qk_gains.T, ((0, 10), (0, 256 - qk_part))),
        ]
    )
    all_packed, all_qkv, all_out, cosine, sine, w_gate, w_up = transfer(
        1, "gather_weights", 30,
        DirectWsh("gather", packed), Gather(w_qkv, pair=True), Gather(w_out, pair=True), Tables(tokens),
        Unpair(w_gate_up),
    )
    full_qkv, full_out = all_qkv.reshape(-1, width), all_out.reshape(-1, width)
    gains = all_packed[:, :4, :gain_part].transpose(1, 0, 2).reshape(4, width).astype(F32)
    qk_gain = all_packed[:, 4:6, :qk_part].transpose(1, 0, 2).reshape(2, HD).astype(F32)

    heads = HEADS * tokens
    normed, raw, q_low, local_kv = compute(
        prepare_kernel, "prepare", 6,
        [((tokens, width), BF), ((tokens, (HEADS + 2) * HD), F32), ((heads, HD), BF), ((tokens, 2 * HD), BF)],
        [], hidden[0], full_qkv, gains, qk_gain, cosine, sine,
    )
    normed_all, whole_kv = transfer(2, "gather_kv", 25, Gather(normed), Gather(local_kv, "ctx"))
    whole_kv, normed_all = whole_kv.reshape(-1, 2 * HD), normed_all.reshape(-1, width)
    out_heads, lse, attended, branch, resid, normed2 = compute(
        attend_kernel, "attend", 10,
        [((heads, HD), F32), ((heads, 128), F32), ((tokens, HEADS * HD), BF), ((tokens, width), F32),
         ((tokens, width), F32), ((tokens, width), BF)],
        [pltpu.VMEM((heads, 128), F32), pltpu.VMEM((heads, 128), F32), pltpu.VMEM((heads, HD), F32)],
        q_low, whole_kv, hidden[0], full_out, gains,
    )

    (n2_all,) = transfer(3, "gather_normed2", 24, Gather(normed2))
    n2_all = n2_all.reshape(-1, width)
    units = w_down.shape[0]
    inner, gelu, slope, terms = tiled(
        forward_kernel, "feed_forward", 10, [units, units, units, width], [n2_all], [w_gate, w_up, w_down]
    )
    (branch2,) = transfer(4, "scatter_branch2", 24, Scatter(terms.reshape(8, tokens, width)))

    r3 = scale_of(branch2)
    output = (resid + branch2 * r3 * gains[3]).astype(BF)
    d_branch2, dg3 = norm_back(branch2, r3, gains[3], cot)
    (d2_all,) = transfer(5, "gather_d_branch2", 24, Gather(d_branch2.astype(BF)))
    d2_all = d2_all.reshape(-1, width)
    d_gate, d_up, terms = tiled(
        backward_kernel, "feed_forward_back", 8, [units, units, width],
        [d2_all, gelu, slope], [w_gate, w_up, w_down],
    )
    d_normed2, ff_early, ff_sums = transfer(
        6, "scatter_d_normed2", 40,
        Scatter(terms.reshape(8, tokens, width)),
        FeedForwardGrads(d_gate, d_up, inner, n2_all, d2_all),
    )

    d_resid, branch_low, dg12, d_q, d_kv = compute(
        attend_back_kernel, "attend_back", 10,
        [((tokens, width), F32), ((tokens, width), BF), ((2, width), F32), ((heads, HD), F32),
         (whole_kv.shape, BF)],
        [pltpu.VMEM((heads, HD), BF)],
        d_normed2, resid, branch, cotangent[0], gains, full_out, q_low, whole_kv, out_heads, lse,
    )
    qkv_part, out_part = w_qkv.shape[0], w_out.shape[0]
    at_all, db_all, own_kv, ff_late = transfer(
        7, "scatter_d_kv", 30,
        DirectWsh("scatter", attended.reshape(tokens, 8, out_part).transpose(1, 0, 2)),
        Gather(branch_low),
        ScatterCtx(d_kv.reshape(8, 2, tokens, 2 * HD)),
        Scatter(ff_sums, "ctx", BF),
    )
    grad_out = dot(at_all.reshape(-1, out_part), db_all.reshape(-1, width), TN)
    d_mixed, grad_hidden, dg0, dqk, _ = compute(
        finish_kernel, "finish", 6,
        [((8, tokens, qkv_part), BF), ((tokens, width), BF), ((1, width), F32), ((2, HD), F32),
         ((tokens, (HEADS + 2) * HD), BF)],
        [], own_kv, d_q, raw, cosine, sine, full_qkv, hidden[0], gains, qk_gain, d_resid,
    )

    dg = jnp.concatenate([dg0, dg12, jnp.sum(dg3, axis=0, keepdims=True)])
    dg = jnp.pad(dg.reshape(4, 8, gain_part).transpose(1, 0, 2), ((0, 0), (0, 0), (0, 256 - gain_part)))
    dqk = jnp.pad(dqk.reshape(2, 8, qk_part).transpose(1, 0, 2), ((0, 0), (0, 2), (0, 256 - qk_part)))
    dm_all, small_all, early_all = transfer(
        8, "columns_to_owners", 12,
        DirectWsh("scatter", d_mixed),
        DirectWsh("scatter", jnp.concatenate([dg, dqk], axis=1)),
        Gather(ff_early, "ctx"),
    )
    grad_qkv = dot(dm_all.reshape(-1, qkv_part), normed_all, TN)
    both = jnp.concatenate([grad_qkv, grad_out], axis=0).astype(BF)
    share = both.shape[0] // 16
    room = -(-share // 16) * 16
    both = jnp.pad(both.reshape(8, 2, share, width), ((0, 0), (0, 0), (0, room - share), (0, 0)))
    small_parts, grads, late_all = transfer(
        9, "sum_grads", 40,
        ShareCtx(jnp.sum(small_all, axis=0)), SumCtx(both), Gather(ff_late, "ctx"),
    )
    grad_gate_up, grad_down = widen(
        early_all.reshape(-1, width), late_all.reshape(-1, width), units
    )
    grads = grads[:, :, :share].reshape(-1, width).astype(F32)
    small_sum = jnp.sum(small_parts, axis=0)
    return (
        output[None],
        grad_hidden[None],
        grads[:qkv_part],
        grads[qkv_part:],
        small_sum[:4, :gain_part].T,
        small_sum[4:6, :qk_part].T,
        grad_gate_up,
        grad_down,
    )


def solution(mesh):
    return jax.shard_map(
        on_device,
        mesh=mesh,
        in_specs=(
            P("wsh", "ctx", None),
            P("wsh", None),
            P("wsh", None),
            P("wsh", None),
            P("wsh", None),
            P("wsh", None, None),
            P("wsh", None),
            P("wsh", "ctx", None),
        ),
        out_specs=(
            P("wsh", "ctx", None),
            P("wsh", "ctx", None),
            P("wsh", None),
            P("wsh", None),
            P("wsh", None),
            P("wsh", None),
            P("wsh", None, None),
            P("wsh", None),
        ),
        check_vma=False,
    )
```

time: 404 us -> 379 us (0.938); the launches traced: 397 us -> 376 us
  Pallas kernels: 263 us -> 324 us
  matrix products: 56.5 us -> 3.87 us
  other arithmetic: 24.3 us -> 6.25 us
  between operations: 15.4 us -> 1.23 us
  local copies, waits for them, and re-layouts: 35.7 us -> 40.7 us
    pallas_call x9, Pallas kernels: 251 us -> 285 us  [transfer(): pl.pallas_call(functools.partial(transfer_kernel, parts), out_shape=[out...]
    dot_general x10 -> x2, matrix products: 32.6 us -> 3.87 us  [dot(): return lax.dot_general(a, b, dims, preferred_element_type=F32)]
    pallas_call x3 -> x7, Pallas kernels: 11.7 us -> 39.5 us  [the longest x2 21.1 us: tiled(): pl.pallas_call(kernel, grid=(rows // step,), out_shape=[jax.ShapeDtypeStr...]
    dot_general x5 -> x0, matrix products: 23.8 us -> none  [the longest x1 7.77 us: on_device(): jnp.dot(d_gate, w_gate, preferred_element_type=F32)]
    unnamed x96 -> x108, local copies, waits for them, and re-layouts: 13.4 us -> 31 us
    convert_element_type x9 -> x1, other arithmetic: 9.27 us -> 2.22 us  [on_device(): d2_all, = transfer(5, 'gather_d_branch2', 24, Gather(d_branch2.astype(BF)))]
    slice x7 -> x0, local copies, waits for them, and re-layouts: 6.79 us -> none  [the longest x1 5.67 us: on_device(): w_gate, w_up = (w_gate_up[:, 0], w_gate_up[:, 1])]
  transfers between devices with their start and end apart: 1 -> 0, of which waited for: 1 -> 0; matrix products, arithmetic and copies ran while one was open for 11% -> 0% of each run, Pallas kernels for 28% -> 0%
where the time goes in v3:
time: 379 us; the launch traced here: 376 us
  Pallas kernels  324 us (85%)
  local copies, waits for them, and re-layouts  40.7 us (11%)
  other arithmetic  6.25 us (2%)
  matrix products  3.87 us (1%)
    pallas_call x9, Pallas kernels, transfer(): pl.pallas_call(functools.partial(transfer_kernel, parts), out_shape=[out...  285 us
    unnamed x108, local copies, waits for them, and re-layouts  31 us
    pallas_call x2, Pallas kernels, tiled(): pl.pallas_call(kernel, grid=(rows // step,), out_shape=[jax.ShapeDtypeStr...  21.1 us
    pallas_call x1, Pallas kernels, widen(): pl.pallas_call(functools.partial(widen_kernel, first), grid=(count,), out...  10.5 us
    pallas_call x4, Pallas kernels, compute(): pl.pallas_call(kernel, out_shape=[jax.ShapeDtypeStruct(shape, dtype) for...  7.88 us

profile of v3, /device:TPU:0, one launch (start us, length us, event | category | flops | bytes accessed | tf_op | source)
XLA Modules:
  0.0 376.3 jit_solution(14603842078799119937)
XLA Ops:
  0.6 0.7 fusion.12.refs_0_
  1.3 1.0 copy-done.41
  2.4 1.0 copy-done.42
  3.3 37.6 %gather_weights.1 = (bf16[8,16,256]{2,1,0:T(8,128)(2,1)S(1)}, bf16[8,192,1152]{2,1,0:T(8,128)(2,1)}, bf16[8,128,1152]{2,1,0:T(8,128)(2,1)}, f32[128,128]{1,0:T(8...) custom-call(bf16[16,256]{1,0:T(8,128)(2,1)S(1)} %fusion.12.refs_0_, ...), custom_call_target="tpu_custom_call" | custom-call | bytes 90000000 | tf_op jit(solution)/shard_map/gather_weights/pallas_call | solution.py:473
  40.9 1.3 copy-done.11
  42.2 1.4 copy-done.14
  43.8 0.1 convert_element_type.46.g_ref
  43.9 2.0 copy-done.3
  45.9 1.4 prepare.1
  47.4 0.9 copy-done.33
  48.2 29.3 %gather_kv.1 = (bf16[8,128,1152]{2,1,0:T(8,128)(2,1)S(1)}, bf16[16,128,512]{2,1,0:T(8,128)(2,1)S(1)}) custom-call(bf16[128,1152]{1,0:T(8,128)(2,1)S(1)} %get-tuple-element.63.refs_0_, bf16[128,512]{1,0:T(8,128)(2,1)S(1)} %get-tuple-element.64.refs_1_), custom_call_target="tpu_custom_call" | custom-call | bytes 75000000 | tf_op jit(solution)/shard_map/gather_kv/pallas_call | solution.py:473
  77.6 1.7 attend.1
  79.4 0.3 copy-done.19
  79.7 0.8 copy-done.21
  80.5 0.8 copy-done.35
  81.4 0.8 copy-done.37
  82.2 0.7 copy-done.47
  82.9 0.2 copy.22
  83.1 0.9 copy.23
  83.9 26.2 %gather_normed2.1 = bf16[8,128,1152]{2,1,0:T(8,128)(2,1)S(1)} custom-call(bf16[128,1152]{1,0:T(8,128)(2,1)S(1)} %get-tuple-element.68.refs_0_), custom_call_target="tpu_custom_call" | custom-call | bytes 72000000 | tf_op jit(solution)/shard_map/gather_normed2/pallas_call | solution.py:473
  110.1 1.4 copy-done
  111.5 1.6 copy-done.12
  113.1 1.6 copy-done.15
  114.6 10.3 %feed_forward.1 = (bf16[1024,864]{1,0:T(8,128)(2,1)S(1)}, bf16[1024,864]{1,0:T(8,128)(2,1)S(1)}, bf16[1024,864]{1,0:T(8,128)(2,1)S(1)}, bf16[1024,1152]{1,0:T(8,128)(2,1)S(1)}) custom-call(bf16[1024,1152]{1,0:T(8,128)(2,1)} %bitcast.47, bf16[864,1152]{1,0:T(8,128)(2,1)S(1)} %copy-done.12, bf16[864,1152]{1,0:T(8,128)(2,1)S(1)} %copy-done.15, ...), custom_call_target="tpu_custom_call" | custom-call | bytes 30000000 | tf_op jit(solution)/shard_map/feed_forward/pallas_call | solution.py:574
  125.0 1.2 copy-done.23
  126.2 1.3 copy-done.24
  127.5 27.4 %scatter_branch2.1 = f32[128,1152]{1,0:T(8,128)S(1)} custom-call(bf16[8,128,1152]{2,1,0:T(8,128)(2,1)S(1)} %bitcast.65), custom_call_target="tpu_custom_call" | custom-call | bytes 72000000 | tf_op jit(solution)/shard_map/scatter_branch2/pallas_call | solution.py:473
  154.9 0.1 multiply_reduce_fusion
  155.0 0.5 multiply_multiply_fusion
  155.5 0.8 fusion.8
  156.3 1.4 concatenate.23
  157.7 0.7 broadcast_multiply_fusion
  158.3 2.2 fusion.5
  160.5 21.2 %gather_d_branch2.1 = bf16[8,128,1152]{2,1,0:T(8,128)(2,1)S(1)} custom-call(bf16[128,1152]{1,0:T(8,128)(2,1)S(1)} %get-tuple-element.110.refs_0_), custom_call_target="tpu_custom_call" | custom-call | bytes 72000000 | tf_op jit(solution)/shard_map/gather_d_branch2/pallas_call | solution.py:473
  181.7 1.4 copy-done.1
  183.1 1.6 copy-done.16
  184.7 1.5 copy-done.25
  186.2 1.5 copy-done.27
  187.7 10.8 %feed_forward_back.1 = (bf16[1024,864]{1,0:T(8,128)(2,1)S(1)}, bf16[1024,864]{1,0:T(8,128)(2,1)S(1)}, bf16[1024,1152]{1,0:T(8,128)(2,1)}) custom-call(bf16[1024,1152]{1,0:T(8,128)(2,1)} %bitcast.49, bf16[1024,864]{1,0:T(8,128)(2,1)S(1)} %copy-done.25, bf16[1024,864]{1,0:T(8,128)(2,1)S(1)} %copy-done.27, bf16[864,1152]{1,0:T(8,128)(2,1)S(1)} %copy-done.13, ...), custom_call_target="tpu_custom_call" | custom-call | bytes 24000000 | tf_op jit(solution)/shard_map/feed_forward_back/pallas_call | solution.py:574
  198.5 45.8 %scatter_d_normed2.1 = (f32[128,1152]{1,0:T(8,128)S(1)}, bf16[96,1152]{1,0:T(8,128)(2,1)S(1)}, bf16[8,80,1152]{2,1,0:T(8,128)(2,1)S(1)}) custom-call(bf16[8,128,1152]{2,1,0:T(8,128)(2,1)} %bitcast.68, bf16[1024,864]{1,0:T(8,128)(2,1)S(1)} %get-tuple-element.76.refs_1_, bf16[1024,864]{1,0:T(8,128)(2,1)S(1)} %get-tuple-element.77.refs_2_, ...), custom_call_target="tpu_custom_call" | custom-call | bytes 120000000 | tf_op jit(solution)/shard_map/scatter_d_normed2/pallas_call | solution.py:473
  244.3 1.1 copy-done.28
  245.4 0.7 copy-done.49
  246.2 2.7 attend_back.1
  248.9 35.6 %scatter_d_kv.1 = (bf16[8,128,128]{2,1,0:T(8,128)(2,1)S(1)}, bf16[8,128,1152]{2,1,0:T(8,128)(2,1)}, f32[128,512]{1,0:T(8,128)S(1)}, bf16[80,1152]{1,0:T(8,128)(2,1)S(1)}) custom-call(bf16[8,128,128]{2,1,0:T(8,128)(2,1)S(1)} %bitcast.67, bf16[128,1152]{1,0:T(8,128)(2,1)S(1)} %get-tuple-element.83.refs_1_, bf16[8,2,128,512]{3,2,1,0:T(8,128)(2,1)S(1)} %bitcast.66, ...), custom_call_target="tpu_custom_call" | custom-call | bytes 90000000 | tf_op jit(solution)/shard_map/scatter_d_kv/pallas_call | solution.py:473
  284.6 1.2 copy-done.34
  285.7 2.0 finish.1
  287.8 0.1 concatenate.21
  288.2 3.2 fusion.1
  291.4 25.2 %columns_to_owners.1 = (bf16[8,128,192]{2,1,0:T(8,128)(2,1)S(1)}, f32[8,8,256]{2,1,0:T(8,128)S(1)}, bf16[16,96,1152]{2,1,0:T(8,128)(2,1)S(1)}) custom-call(bf16[8,128,192]{2,1,0:T(8,128)(2,1)S(1)} %get-tuple-element.91.refs_0_, f32[8,8,256]{2,1,0:T(8,128)S(1)} %select_maximum_fusion.refs_1_, bf16[96,1152]{1,0:T(8,128)(2,1)S(1)} %copy-done.50), custom_call_target="tpu_custom_call" | custom-call | bytes 36000000 | tf_op jit(solution)/shard_map/columns_to_owners/pallas_call | solution.py:473
  316.5 1.7 copy-done.2
  318.3 0.7 fusion
  319.0 1.0 pad_maximum_fusion
  320.1 0.1 convert_element_type.53
  320.2 0.1 pad.24.refs_1_
  320.3 0.6 copy-done.52
  321.0 36.6 %sum_grads.1 = (f32[16,8,256]{2,1,0:T(8,128)S(1)}, bf16[8,2,32,1152]{3,2,1,0:T(8,128)(2,1)S(1)}, bf16[16,80,1152]{2,1,0:T(8,128)(2,1)S(1)}) custom-call(f32[8,256]{1,0:T(8,128)S(1)} %reduce_sum.48.refs_0_, bf16[8,2,32,1152]{3,2,1,0:T(8,128)(2,1)S(1)} %pad.24.refs_1_, bf16[80,1152]{1,0:T(8,128)(2,1)S(1)} %copy-done.52), custom_call_target="tpu_custom_call" | custom-call | bytes 120000000 | tf_op jit(solution)/shard_map/sum_grads/pallas_call | solution.py:473
  357.6 1.6 copy-done.5
  359.3 0.6 slice_bitcast_fusion.1
  359.8 0.6 slice_bitcast_fusion
  360.4 0.1 slice_convert_fusion
  360.5 1.3 reshape.105
  361.8 1.9 slice.36
  363.7 2.1 slice.35
  365.8 10.5 %widen.1 = (f32[864,2,1152]{2,1,0:T(2,128)}, f32[864,1152]{1,0:T(8,128)}) custom-call(bf16[1536,1152]{1,0:T(8,128)(2,1)} %bitcast.51, bf16[1536,1152]{1,0:T(8,128)(2,1)} %bitcast.52, bf16[1280,1152]{1,0:T(8,128)(2,1)} %bitcast.55, bf16[1280,1152]{1,0:T(8,128)(2,1)} %bitcast.56), custom_call_target="tpu_custom_call" | custom-call | bytes 27000000 | tf_op jit(solution)/shard_map/widen/pallas_call | solution.py:521
  (98 shorter events, 0.7 us)
Async XLA Ops:
  1.3 1.0 copy-start.41
  2.4 1.0 copy-start.42
  3.3 40.6 %copy-start.18 = (bf16[1,128,1152]{2,1,0:T(8,128)(2,1)S(1)}, bf16[1,128,1152]{2,1,0:T(8,128)(2,1)}, u32[]{:S(2)}) copy-start(bf16[1,128,1152]{2,1,0:T(8,128)(2,1)} %param.8) | copy-start | bytes 884740
  40.9 1.3 copy-start.11
  42.2 1.4 copy-start.14
  43.6 3.8 %copy-start.43 = (f32[128,128]{1,0:T(8,128)}, f32[128,128]{1,0:T(8,128)S(1)}, u32[]{:S(2)}) copy-start(f32[128,128]{1,0:T(8,128)S(1)} %get-tuple-element.60.cos_ref) | copy-start | bytes 196612
  43.6 3.8 %copy-start.45 = (f32[128,128]{1,0:T(8,128)}, f32[128,128]{1,0:T(8,128)S(1)}, u32[]{:S(2)}) copy-start(f32[128,128]{1,0:T(8,128)S(1)} %get-tuple-element.61.sin_ref) | copy-start | bytes 196612
  43.9 2.0 copy-start.3
  45.9 31.7 %copy-start.39 = (f32[4,1152]{1,0:T(4,128)}, f32[4,1152]{1,0:T(4,128)S(1)}, u32[]{:S(2)}) copy-start(f32[4,1152]{1,0:T(4,128)S(1)} %convert_element_type.46.g_ref) | copy-start | bytes 55300
  45.9 31.7 %copy-start.6 = (bf16[8,128,1152]{2,1,0:T(8,128)(2,1)S(1)}, bf16[8,128,1152]{2,1,0:T(8,128)(2,1)}, u32[]{:S(2)}) copy-start(bf16[8,128,1152]{2,1,0:T(8,128)(2,1)} %get-tuple-element.66) | copy-start | bytes 7077892
  47.4 0.9 copy-start.33
  48.2 31.1 %copy-start.30 = (bf16[512,256]{1,0:T(8,128)(2,1)}, bf16[512,256]{1,0:T(8,128)(2,1)S(1)}, u32[]{:S(2)}) copy-start(bf16[512,256]{1,0:T(8,128)(2,1)S(1)} %get-tuple-element.62.q_ref) | copy-start | bytes 786436
  77.6 1.8 copy-start.7
  77.6 2.1 copy-start.19
  79.7 0.8 copy-start.21
  80.5 0.8 copy-start.35
  81.4 0.8 copy-start.37
  82.2 0.7 copy-start.47
  83.9 27.6 %copy-start.9 = (bf16[864,1152]{1,0:T(8,128)(2,1)S(1)}, bf16[864,1152]{1,0:T(8,128)(2,1)}, u32[]{:S(2)}) copy-start(bf16[864,1152]{1,0:T(8,128)(2,1)} %down_ref.3) | copy-start | bytes 5971972
  110.1 1.4 copy-start
  111.5 1.6 copy-start.12
  113.1 1.6 copy-start.15
  125.0 1.3 copy-start.23
  126.2 1.3 copy-start.24
  127.5 28.8 %copy-start.26 = (bf16[1024,864]{1,0:T(8,128)(2,1)}, bf16[1024,864]{1,0:T(8,128)(2,1)S(1)}, u32[]{:S(2)}) copy-start(bf16[1024,864]{1,0:T(8,128)(2,1)S(1)} %get-tuple-element.74.slope_ref) | copy-start | bytes 5308420
  127.5 28.0 %copy-start.17 = (bf16[1,128,1152]{2,1,0:T(8,128)(2,1)S(1)}, bf16[1,128,1152]{2,1,0:T(8,128)(2,1)}, u32[]{:S(2)}) copy-start(bf16[1,128,1152]{2,1,0:T(8,128)(2,1)} %param.15) | copy-start | bytes 884740
  158.3 24.8 %copy-start.10 = (bf16[864,1152]{1,0:T(8,128)(2,1)S(1)}, bf16[864,1152]{1,0:T(8,128)(2,1)}, u32[]{:S(2)}) copy-start(bf16[864,1152]{1,0:T(8,128)(2,1)} %down_ref.3) | copy-start | bytes 5971972
  158.3 24.8 %copy-start.13 = (bf16[864,1152]{1,0:T(8,128)(2,1)S(1)}, bf16[864,1152]{1,0:T(8,128)(2,1)}, u32[]{:S(2)}) copy-start(bf16[864,1152]{1,0:T(8,128)(2,1)} %copy-done.11) | copy-start | bytes 5971972
  181.7 1.4 copy-start.1
  183.1 1.6 copy-start.16
  184.7 1.5 copy-start.25
  186.2 1.5 copy-start.27
  198.5 47.6 %copy-start.8 = (bf16[16,128,512]{2,1,0:T(8,128)(2,1)S(1)}, bf16[16,128,512]{2,1,0:T(8,128)(2,1)}, u32[]{:S(2)}) copy-start(bf16[16,128,512]{2,1,0:T(8,128)(2,1)} %copy-done.7) | copy-start | bytes 6291460
  198.5 47.6 %copy-start.22 = (f32[128,1152]{1,0:T(8,128)S(1)}, f32[128,1152]{1,0:T(8,128)}, u32[]{:S(2)}) copy-start(f32[128,1152]{1,0:T(8,128)} %copy-done.21) | copy-start | bytes 1769476
  198.5 47.6 %copy-start.31 = (bf16[512,256]{1,0:T(8,128)(2,1)S(1)}, bf16[512,256]{1,0:T(8,128)(2,1)}, u32[]{:S(2)}) copy-start(bf16[512,256]{1,0:T(8,128)(2,1)} %copy-done.30) | copy-start | bytes 786436
  198.5 47.6 %copy-start.36 = (f32[128,1152]{1,0:T(8,128)S(1)}, f32[128,1152]{1,0:T(8,128)}, u32[]{:S(2)}) copy-start(f32[128,1152]{1,0:T(8,128)} %copy-done.35) | copy-start | bytes 1769476
  198.5 47.6 %copy-start.38 = (f32[512,256]{1,0:T(8,128)S(1)}, f32[512,256]{1,0:T(8,128)}, u32[]{:S(2)}) copy-start(f32[512,256]{1,0:T(8,128)} %copy-done.37) | copy-start | bytes 1572868
  198.5 47.6 %copy-start.40 = (f32[4,1152]{1,0:T(4,128)S(1)}, f32[4,1152]{1,0:T(4,128)}, u32[]{:S(2)}) copy-start(f32[4,1152]{1,0:T(4,128)} %copy-done.39) | copy-start | bytes 55300
  198.5 47.6 %copy-start.48 = (f32[512,128]{1,0:T(8,128)S(1)}, f32[512,128]{1,0:T(8,128)}, u32[]{:S(2)}) copy-start(f32[512,128]{1,0:T(8,128)} %copy-done.47) | copy-start | bytes 786436
  244.3 1.1 copy-start.28
  245.4 0.7 copy-start.49
  246.1 2.8 copy-start.29
  246.2 2.8 copy-start.32
  248.9 35.7 %copy-start.4 = (bf16[8,192,1152]{2,1,0:T(8,128)(2,1)S(1)}, bf16[8,192,1152]{2,1,0:T(8,128)(2,1)}, u32[]{:S(2)}) copy-start(bf16[8,192,1152]{2,1,0:T(8,128)(2,1)} %get-tuple-element.58) | copy-start | bytes 10616836
  248.9 35.7 %copy-start.44 = (f32[128,128]{1,0:T(8,128)S(1)}, f32[128,128]{1,0:T(8,128)}, u32[]{:S(2)}) copy-start(f32[128,128]{1,0:T(8,128)} %copy-done.43) | copy-start | bytes 196612
  248.9 35.7 %copy-start.46 = (f32[128,128]{1,0:T(8,128)S(1)}, f32[128,128]{1,0:T(8,128)}, u32[]{:S(2)}) copy-start(f32[128,128]{1,0:T(8,128)} %copy-done.45) | copy-start | bytes 196612
  284.5 3.3 copy-start.51
  284.6 1.2 copy-start.34
  285.7 2.4 copy-start.53
  287.8 3.6 copy-start.50
  287.8 30.5 %copy-start.20 = (bf16[8,128,1152]{2,1,0:T(8,128)(2,1)S(1)}, bf16[8,128,1152]{2,1,0:T(8,128)(2,1)}, u32[]{:S(2)}) copy-start(bf16[8,128,1152]{2,1,0:T(8,128)(2,1)} %copy-done.19) | copy-start | bytes 7077892
  316.5 1.8 copy-start.2
  320.0 0.9 copy-start.52
  357.6 1.6 copy-start.5

commit v4 on v3

--- a/solution.py
+++ b/solution.py
@@ -18,6 +18,7 @@
 BF = jnp.bfloat16
 F32 = jnp.float32
 HBM = pltpu.HBM
+ROOM = 60 * 2**20
 
 
 def cost(us):
@@ -218,8 +219,8 @@
 
 
 class DirectWsh:
-    def __init__(self, mode, array):
-        self.mode, self.arrays, self.groups = mode, [array], {"row"}
+    def __init__(self, mode, array, turns=9):
+        self.mode, self.arrays, self.groups, self.turns = mode, [array], {"row"}, turns
         shape = ((8,) + array.shape) if mode == "gather" else array.shape
         self.outs = [jax.ShapeDtypeStruct(shape, array.dtype)]
         self.in_spaces, self.out_spaces = [HBM], [HBM]
@@ -235,9 +236,8 @@
             copies[-1].start()
         copies.append(pltpu.make_async_copy(pick(p.wsh), o.at[p.wsh], own))
         copies[-1].start()
-        yield
-        yield
-        yield
+        for _ in range(self.turns):
+            yield
         for copy in copies:
             copy.wait()
 
@@ -256,14 +256,14 @@
         order = list(range(1, 8)) + [0]
         for i, step in enumerate(order):
             chip = lax.rem(p.chip + step, 8)
-            copies.append(remote(x.at[chip, 1 - p.core], pair.at[chip], sems, i, p.twin))
+            copies.append(remote(x.at[2 * chip + 1 - p.core], pair.at[chip], sems, i, p.twin))
             copies[-1].start()
         for i, step in enumerate(order):
             if i % 3 == 0:
                 yield
             chip = lax.rem(p.chip + step, 8)
             copies[i].wait_recv()
-            both = x[chip, p.core].astype(F32) + pair[chip].astype(F32)
+            both = x[2 * chip + p.core].astype(F32) + pair[chip].astype(F32)
             if step > 0:
                 sums[chip] = both.astype(BF)
                 copies.append(remote(sums.at[chip], got.at[p.chip], sems, 7 + step, p.chips(step)))
@@ -280,15 +280,30 @@
 
 
 class SumCtx:
-    def __init__(self, array):
-        _, _, rows, width = array.shape
-        self.arrays, self.groups = [array], {"chips", "twin"}
-        self.outs = [jax.ShapeDtypeStruct(array.shape, BF)]
-        self.in_spaces, self.out_spaces = [pltpu.VMEM], [pltpu.VMEM]
-        self.scratch = [pltpu.VMEM((8, rows, width), BF)] * 3 + [pltpu.SemaphoreType.DMA((2, 23))]
+    def __init__(self, d_mixed, normed, attended, d_branch):
+        width = normed.shape[-1]
+        self.share = (d_mixed.shape[-1] + attended.shape[-1]) // 16
+        rows = -(-self.share // 16) * 16
+        self.arrays, self.groups = [d_mixed, normed, attended, d_branch], {"chips", "twin"}
+        self.outs = [jax.ShapeDtypeStruct((8, 2, rows, width), BF)]
+        self.in_spaces, self.out_spaces = [pltpu.VMEM] * 4, [pltpu.VMEM]
+        self.scratch = [pltpu.VMEM((8, 2, rows, width), BF)]
+        self.scratch += [pltpu.VMEM((8, rows, width), BF)] * 3 + [pltpu.SemaphoreType.DMA((2, 23))]
+
+    def product(self, ins, x):
+        d_mixed, normed, attended, d_branch = ins
+        width = normed.shape[-1]
+        flat = lambda ref: ref[...].reshape(-1, ref.shape[-1])
+        parts = (dot(flat(d_mixed), flat(normed), TN), dot(flat(attended), flat(d_branch), TN))
+        both = jnp.concatenate(parts, axis=0)
+        blank = jnp.zeros((x.shape[2] - self.share, width), F32)
+        for i in range(16):
+            rows = both[i * self.share : (i + 1) * self.share]
+            x[i // 2, i % 2] = jnp.concatenate([rows, blank], axis=0).astype(BF)
 
     def run(self, p, ins, outs, scratch):
-        (x,), (o,), (pair, sums, got, sems) = ins, outs, scratch
+        (o,), (x, pair, sums, got, sems) = outs, scratch
+        self.product(ins, x)
         first = remote(x.at[:, 1 - p.core], pair, sems, 0, p.twin)
         first.start()
         first.wait_recv()
@@ -339,8 +354,8 @@
             copies[-1].start()
         copies.append(pltpu.make_async_copy(x, o.at[p.ctx], own))
         copies[-1].start()
-        yield
-        yield
+        for _ in range(9):
+            yield
         for copy in copies:
             copy.wait()
 
@@ -357,16 +372,17 @@
         early = granules * 5 // 9
         self.pieces = (early * 16, (granules - early) * 16)
         sums = [pltpu.VMEM((8, rows, width), BF) for rows in self.pieces]
-        late = jax.ShapeDtypeStruct(sums[1].shape, BF)
-        self.scatter = Scatter(jax.ShapeDtypeStruct(sums[0].shape, BF), "ctx", BF)
-        self.outs = self.scatter.outs + [late]
+        self.scatters = [Scatter(jax.ShapeDtypeStruct(b.shape, BF), "ctx", BF) for b in sums]
+        self.outs = self.scatters[0].outs + self.scatters[1].outs
         self.in_spaces, self.out_spaces = [pltpu.VMEM] * 5, [pltpu.VMEM] * 2
         self.scratch = [pltpu.VMEM((16 * rows, width), BF) for rows in self.pieces]
-        self.scratch += sums + sums[:1] + [pltpu.SemaphoreType.DMA((2, 16))] + self.scatter.scratch
+        self.scratch += sums + sums + [pltpu.SemaphoreType.DMA((2, 16))]
+        self.scratch += self.scatters[0].scratch + self.scatters[1].scratch
 
     def run(self, p, ins, outs, scratch):
         d_gate, d_up, inner, normed, d_branch = ins
-        first, second, pair_first, pair_second, sums, sems, *rest = scratch
+        first, second, pair_first, pair_second, sums, sums_second, sems, *rest = scratch
+        count = len(self.scatters[0].scratch)
         units = d_gate.shape[1]
         split = first.shape[0]
         twins = []
@@ -407,28 +423,213 @@
             second[second.shape[0] - missing :] = jnp.zeros((missing, second.shape[1]), BF)
         swap(second, pair_second, 1)
         add(first, pair_first, sums, 0)
-        middle = self.scatter.run(p, [sums], outs[:1], rest)
-        next(middle)
-        add(second, pair_second, outs[1], 1)
-        yield
-        yield from middle
+        turns = [self.scatters[0].run(p, [sums], outs[:1], rest[:count])]
+        next(turns[0])
+        add(second, pair_second, sums_second, 1)
+        turns.append(self.scatters[1].run(p, [sums_second], outs[1:], rest[count:]))
+        while turns:
+            turns = [turn for turn in turns if next(turn, "end") != "end"]
+            yield
         for copy in twins:
             copy.wait_send()
 
 
-class Unpair:
-    def __init__(self, array):
-        self.arrays, self.groups = [array], set()
-        self.outs = [jax.ShapeDtypeStruct((array.shape[0], array.shape[2]), BF)] * 2
-        self.in_spaces, self.out_spaces, self.scratch = [pltpu.VMEM], [pltpu.VMEM] * 2, []
+def unpair(both, gate, up):
+    step = 96
+    for start in range(0, gate.shape[0], step):
+        def move(rows):
+            here = pl.ds(pl.multiple_of(rows.start + start, 16), 16)
+            gate[here] = both[here, 0, :]
+            up[here] = both[here, 1, :]
+
+        rows_loop(step, move)
+        yield
+
+
+def ring_blocks(g, x, o, sems):
+    rows = x.shape[0]
+    half = rows // 2
+    low, high = (0, half), (half, half)
+    copies = {}
+
+    def at(slot, part=(0, rows)):
+        return o.at[pl.ds(slot * rows + part[0], part[1])]
+
+    def send(i, source, target, device):
+        copies[i] = remote(source, target, sems, i, device)
+        copies[i].start()
+
+    send(2, x, at(1), g.across)
+    send(0, x, at(2), g.up)
+    send(1, x, at(3), g.down)
+    o[:rows] = x[...]
+    copies[2].wait_recv()
+    send(5, at(1), at(4), g.up)
+    send(6, at(1), at(5), g.down)
+    yield 0
+    copies[0].wait_recv()
+    send(3, at(2, low), at(6, low), g.up)
+    copies[1].wait_recv()
+    send(4, at(3, high), at(6, high), g.down)
+    yield 1
+    copies[5].wait_recv()
+    send(7, at(4, low), at(7, low), g.up)
+    copies[6].wait_recv()
+    send(8, at(5, high), at(7, high), g.down)
+    yield 2
+    for i in (3, 4, 7, 8):
+        copies[i].wait_recv()
+    yield 3
+    for copy in copies.values():
+        copy.wait_send()
+
+
+class RingSum:
+    slots = {"opposite": (7, 6), "up": (5, 3), "down": (4, 2), "own": (1, 0)}
+
+    def __init__(self, g, x, o, scratch):
+        self.g, self.x, self.o = g, x, o
+        self.buf_a, self.buf_b, self.sum_c, self.sum_d, self.buf_c, self.buf_d, self.buf_e, self.sems = scratch
+        self.rows = o.shape[0]
+        self.half = self.rows // 2
+        self.copies = {}
+
+    @staticmethod
+    def scratch(rows, width):
+        half, whole = pltpu.VMEM((2, rows // 2, width), BF), pltpu.VMEM((2, rows, width), BF)
+        return [half, half, half, half, whole, whole, whole, pltpu.SemaphoreType.DMA((2, 13))]
+
+    def at(self, place, k, part):
+        return pl.ds(self.slots[place][k] * self.rows + part * self.half, self.half * (1 if part < 2 else 2))
+
+    def send(self, i, source, target, device):
+        self.copies[i] = remote(source, target, self.sems, i, device)
+        self.copies[i].start()
+
+    def near(self, k):
+        low, high = pl.ds(0, self.half), pl.ds(self.half, self.half)
+        self.send(4 + k, self.x.at[self.at("up", k, 1)], self.buf_c.at[k, high], self.g.up)
+        self.send(6 + k, self.x.at[self.at("down", k, 0)], self.buf_d.at[k, low], self.g.down)
+
+    def far(self, k):
+        self.send(k, self.x.at[self.at("opposite", k, 0)], self.buf_a.at[k], self.g.up)
+        self.send(2 + k, self.x.at[self.at("opposite", k, 1)], self.buf_b.at[k], self.g.down)
+
+    def rest(self):
+        x, copies = self.x, self.copies
+        low, high = pl.ds(0, self.half), pl.ds(self.half, self.half)
+        for k in range(2):
+            yield
+            copies[k].wait_recv()
+            self.sum_c[k] = (x[self.at("up", k, 0)].astype(F32) + self.buf_a[k].astype(F32)).astype(BF)
+            self.send(8 + k, self.sum_c.at[k], self.buf_c.at[k, low], self.g.up)
+            copies[2 + k].wait_recv()
+            self.sum_d[k] = (x[self.at("down", k, 1)].astype(F32) + self.buf_b[k].astype(F32)).astype(BF)
+            self.send(10 + k, self.sum_d.at[k], self.buf_d.at[k, high], self.g.down)
+        for k in range(2):
+            yield
+            for i in (4, 6, 8, 10):
+                copies[i + k].wait_recv()
+            slot = self.slots["own"][k] * self.rows
+            total = x[slot : slot + self.rows].astype(F32) + self.buf_c[k].astype(F32) + self.buf_d[k].astype(F32)
+            if k == 0:
+                self.buf_e[0] = total.astype(BF)
+                self.send(12, self.buf_e.at[0], self.buf_e.at[1], self.g.across)
+            else:
+                yield
+                copies[12].wait_recv()
+                self.o[...] = total + self.buf_e[1].astype(F32)
+        for copy in copies.values():
+            copy.wait_send()
+
+
+def forward_block(n, w_gate, w_up, w_down, inner_ref, gelu_ref, slope_ref, terms_ref, rows):
+    gate = dot(n, w_gate[...], NT)
+    up = dot(n, w_up[...], NT)
+    bend, grow = math.sqrt(2.0 / math.pi), 0.044715
+    square = gate * gate
+    wave = jnp.tanh(bend * gate * (1.0 + grow * square))
+    rise = 0.5 * (1.0 + wave)
+    gelu = gate * rise
+    slope = rise + 0.5 * bend * gate * (1.0 - wave * wave) * (1.0 + 3.0 * grow * square)
+    gelu_ref[rows] = gelu.astype(BF)
+    slope_ref[rows] = (up * slope).astype(BF)
+    inner_ref[rows] = (gelu * up).astype(BF)
+    terms_ref[rows] = jnp.dot(inner_ref[rows], w_down[...], preferred_element_type=F32).astype(BF)
+
+
+class FeedForward:
+    def __init__(self, normed, resid, cot, gains, w_gate, w_up, w_down, first_normed):
+        (rows, width), units = normed.shape, w_down.shape[0]
+        self.arrays = [normed, resid, cot, gains, w_gate, w_up, w_down, first_normed]
+        self.gather = Gather(first_normed)
+        tokens = jax.ShapeDtypeStruct((8 * rows, width), BF)
+        hidden = jax.ShapeDtypeStruct((8 * rows, units), BF)
+        self.grads = FeedForwardGrads(hidden, hidden, hidden, tokens, tokens)
+        self.groups = {"wsh"} | self.grads.groups
+        shapes = [((rows, width), BF), ((1, width), F32), ((rows, width), F32)]
+        self.outs = [jax.ShapeDtypeStruct(*shape) for shape in shapes] + self.grads.outs
+        self.outs += self.gather.outs
+        self.in_spaces, self.out_spaces = [pltpu.VMEM] * 7 + [HBM], [pltpu.VMEM] * 5 + [HBM]
+        wide, narrow = pltpu.VMEM(tokens.shape, BF), pltpu.VMEM(hidden.shape, BF)
+        self.scratch = [wide] * 3 + [narrow] * 5 + [pltpu.VMEM((rows, width), F32), pltpu.VMEM((rows, width), BF)]
+        self.scratch += [pltpu.SemaphoreType.DMA((2, 9))] * 2
+        self.scratch += RingSum.scratch(rows, width) * 2 + self.grads.scratch + self.gather.scratch
 
     def run(self, p, ins, outs, scratch):
-        def step(rows):
-            outs[0][rows] = ins[0][rows, 0, :]
-            outs[1][rows] = ins[0][rows, 1, :]
-
-        rows_loop(ins[0].shape[0], step)
-        yield
+        x, resid, cot, gains, w_gate, w_up, w_down, first_normed = ins
+        out, dg, d_normed, *grads, first_all = outs
+        tokens, terms, d_all, inner, gelu, slope, d_gate, d_up, branch, low, sems, back_sems, *rest = scratch
+        g = p.grids["wsh"]
+        count = len(RingSum.scratch(*x.shape))
+        there = RingSum(g, terms, branch, rest[:count])
+        back = RingSum(g, terms, d_normed, rest[count : 2 * count])
+        pair = 2 * x.shape[0]
+
+        def sends(ring, i):
+            if i in (1, 2):
+                ring.near(2 - i)
+            if i == 3:
+                ring.far(0)
+                ring.far(1)
+
+        p.ready(0)
+        for i in ring_blocks(g, x, tokens, sems):
+            if i == 0:
+                p.ready()
+            rows = slice(i * pair, (i + 1) * pair)
+            forward_block(tokens[rows], w_gate, w_up, w_down, inner, gelu, slope, terms, rows)
+            sends(there, i)
+        yield from there.rest()
+        total, gain, c = branch[...], gains[3:4], cot[...].astype(F32)
+        scale = scale_of(total)
+        d_branch, dg_terms = norm_back(total, scale, gain, c)
+        low[...] = d_branch.astype(BF)
+        out[...] = (resid[...] + total * scale * gain).astype(BF)
+        dg[...] = jnp.sum(dg_terms, axis=0, keepdims=True)
+        for i in ring_blocks(g, low, d_all, back_sems):
+            rows = slice(i * pair, (i + 1) * pair)
+            d_inner = dot(d_all[rows], w_down[...], NT)
+            d_gate[rows] = (d_inner * slope[rows].astype(F32)).astype(BF)
+            d_up[rows] = (d_inner * gelu[rows].astype(F32)).astype(BF)
+            terms[rows] = (
+                jnp.dot(d_gate[rows], w_gate[...], preferred_element_type=F32)
+                + jnp.dot(d_up[rows], w_up[...], preferred_element_type=F32)
+            ).astype(BF)
+            sends(back, i)
+        last = len(self.gather.scratch)
+
+        def others():
+            yield from back.rest()
+            yield from self.gather.run(p, [first_normed], [first_all], rest[-last:])
+
+        turns = [
+            self.grads.run(p, [d_gate, d_up, inner, tokens, d_all], grads, rest[2 * count : -last]),
+            others(),
+        ]
+        while turns:
+            turns = [turn for turn in turns if next(turn, "end") != "end"]
+            yield
 
 
 class Tables:
@@ -447,41 +648,83 @@
         yield
 
 
-def transfer_kernel(parts, *refs):
+def transfer_kernel(parts, ins, outs, scratch, ready, store):
     place = Place()
-    groups = set().union(*(part.groups for part in parts))
-    if "others" in groups:
-        groups = groups - {"twin"}
-    meet(place, groups)
-    refs = list(refs)
-
-    def take(count):
-        taken = refs[:count]
-        del refs[:count]
-        return taken
-
-    ins = [take(len(part.arrays)) for part in parts]
-    outs = [take(len(part.outs)) for part in parts]
-    scratch = [take(len(part.scratch)) for part in parts]
+    place.ready, place.store = ready, store
+    meet(place, set().union(*(part.groups for part in parts)))
+
+    def take(refs, counts):
+        refs = list(refs)
+        return [[refs.pop(0) for _ in range(count)] for count in counts]
+
+    ins = take(ins, [len(part.arrays) for part in parts])
+    outs = take(outs, [len(part.outs) for part in parts])
+    scratch = take(scratch, [len(part.scratch) for part in parts])
     active = [part.run(place, i, o, s) for part, i, o, s in zip(parts, ins, outs, scratch)]
     while active:
         active = [run for run in active if next(run, "end") != "end"]
 
 
-def transfer(cid, name, us, *parts):
-    spec = lambda space: pl.BlockSpec(memory_space=space)
+def staged(body, name, us, arrays, in_spaces, outs, out_spaces, scratch, cid=None):
+    picked_in = [i for i, space in enumerate(in_spaces) if space == pltpu.VMEM]
+    picked_out = [i for i, space in enumerate(out_spaces) if space == pltpu.VMEM]
+    held = [pltpu.VMEM(arrays[i].shape, arrays[i].dtype) for i in picked_in]
+    held += [pltpu.VMEM(outs[i].shape, outs[i].dtype) for i in picked_out]
+    counts = (len(arrays), len(outs), len(picked_in), len(picked_out))
+
+    def kernel(*refs):
+        ends = [sum(counts[:k]) for k in range(5)]
+        far_in, far_out, near_in, near_out = (refs[ends[k] : ends[k + 1]] for k in range(4))
+        in_sems, out_sems, *rest = refs[ends[4] :]
+        ins, results = list(far_in), list(far_out)
+        loads = []
+        for k, i in enumerate(picked_in):
+            loads.append(pltpu.make_async_copy(far_in[i], near_in[k], in_sems.at[k]))
+            loads[-1].start()
+            ins[i] = near_in[k]
+        for k, i in enumerate(picked_out):
+            results[i] = near_out[k]
+
+        waiting = dict(zip(picked_in, loads))
+
+        def ready(*indices):
+            for i in indices or tuple(waiting):
+                waiting.pop(i).wait()
+
+        stores = {}
+
+        def store(i):
+            k = picked_out.index(i)
+            stores[i] = pltpu.make_async_copy(near_out[k], far_out[i], out_sems.at[k])
+            stores[i].start()
+
+        body(ins, results, rest, ready, store)
+        for i in picked_out:
+            if i not in stores:
+                store(i)
+        for copy in stores.values():
+            copy.wait()
+
+    sems = [pltpu.SemaphoreType.DMA((max(len(picked), 1),)) for picked in (picked_in, picked_out)]
+    extra = {} if cid is None else {"collective_id": cid, "has_side_effects": True}
     return pl.pallas_call(
-        functools.partial(transfer_kernel, parts),
-        out_shape=[out for part in parts for out in part.outs],
-        in_specs=[spec(s) for part in parts for s in part.in_spaces],
-        out_specs=[spec(s) for part in parts for s in part.out_spaces],
-        scratch_shapes=[s for part in parts for s in part.scratch],
-        compiler_params=pltpu.CompilerParams(
-            collective_id=cid, has_side_effects=True, vmem_limit_bytes=48 * 2**20
-        ),
+        kernel,
+        out_shape=list(outs),
+        in_specs=[pl.BlockSpec(memory_space=HBM)] * counts[0],
+        out_specs=[pl.BlockSpec(memory_space=HBM)] * counts[1],
+        scratch_shapes=held + sems + list(scratch),
+        compiler_params=pltpu.CompilerParams(vmem_limit_bytes=ROOM, **extra),
         cost_estimate=cost(us),
         name=name,
-    )(*[array for part in parts for array in part.arrays])
+    )(*arrays)
+
+
+def transfer(cid, name, us, *parts):
+    every = lambda field: [item for part in parts for item in getattr(part, field)]
+    return staged(
+        functools.partial(transfer_kernel, parts), name, us, every("arrays"), every("in_spaces"),
+        every("outs"), every("out_spaces"), every("scratch"), cid,
+    )
 
 
 NT = (((1,), (1,)), ((), ()))
@@ -499,7 +742,21 @@
     return jnp.where(col <= row, scores, MASKED)
 
 
-def widen_kernel(first, gate_ref, up_ref, more_ref, low_ref, both_ref, down_ref):
+def widen_kernel(first, gate_ref, up_ref, more_ref, low_ref, grads_ref, small_ref, both_ref, down_ref, qkv_ref, out_ref,
+                 sum_ref):
+    @pl.when(pl.program_id(0) == 0)
+    def _():
+        share, split = (qkv_ref.shape[0] + out_ref.shape[0]) // 16, qkv_ref.shape[0]
+        for i in range(16):
+            value = grads_ref[i // 2, i % 2].astype(F32)
+            start, stop = i * share, (i + 1) * share
+            middle = min(max(split, start), stop)
+            if middle > start:
+                qkv_ref[start:middle] = value[: middle - start]
+            if stop > middle:
+                out_ref[middle - split : stop - split] = value[middle - start : share]
+        sum_ref[...] = jnp.sum(small_ref[...], axis=0)
+
     both_ref[:, 0, :] = gate_ref[...].astype(F32)
     down_ref[...] = low_ref[...].astype(F32)
 
@@ -512,29 +769,41 @@
         both_ref[:, 1, :] = more_ref[...].astype(F32)
 
 
-def widen(early, late, rows):
+def widen(early, late, rows, grads, small, parts):
     width = early.shape[1]
     step = 96
     count = rows // step
     first = early.shape[0] // step - count
     spec = lambda index: pl.BlockSpec((step, width), lambda i: (index(i), 0))
+    whole = lambda shape: pl.BlockSpec(shape, lambda i: (0,) * len(shape))
     return pl.pallas_call(
         functools.partial(widen_kernel, first),
         grid=(count,),
         out_shape=[
             jax.ShapeDtypeStruct((rows, 2, width), F32),
             jax.ShapeDtypeStruct((rows, width), F32),
+            jax.ShapeDtypeStruct((parts[0], width), F32),
+            jax.ShapeDtypeStruct((parts[1], width), F32),
+            jax.ShapeDtypeStruct(small.shape[1:], F32),
         ],
         in_specs=[
             spec(lambda i: i),
             spec(lambda i: jnp.minimum(i, first - 1) + count),
             spec(lambda i: jnp.maximum(i - first, 0)),
             spec(lambda i: i + count - first),
+            whole(grads.shape),
+            whole(small.shape),
         ],
-        out_specs=[pl.BlockSpec((step, 2, width), lambda i: (i, 0, 0)), spec(lambda i: i)],
+        out_specs=[
+            pl.BlockSpec((step, 2, width), lambda i: (i, 0, 0)),
+            spec(lambda i: i),
+            whole((parts[0], width)),
+            whole((parts[1], width)),
+            whole(small.shape[1:]),
+        ],
         cost_estimate=cost(9),
         name="widen",
-    )(early, early, late, late)
+    )(early, early, late, late, grads, small)
 
 
 def scale_of(values):
@@ -558,63 +827,29 @@
 
 
 def compute(kernel, name, us, outs, scratch, *args):
-    return pl.pallas_call(
-        kernel,
-        out_shape=[jax.ShapeDtypeStruct(shape, dtype) for shape, dtype in outs],
-        scratch_shapes=scratch,
-        compiler_params=pltpu.CompilerParams(vmem_limit_bytes=28 * 2**20),
-        cost_estimate=cost(us),
-        name=name,
-    )(*args)
-
-
-def tiled(kernel, name, us, widths, rowed, whole):
-    rows, step = rowed[0].shape[0], 256
-    spec = lambda width: pl.BlockSpec((step, width), lambda i: (i, 0))
-    return pl.pallas_call(
-        kernel,
-        grid=(rows // step,),
-        out_shape=[jax.ShapeDtypeStruct((rows, width), BF) for width in widths],
-        in_specs=[spec(a.shape[1]) for a in rowed]
-        + [pl.BlockSpec(a.shape, lambda i: (0, 0)) for a in whole],
-        out_specs=[spec(width) for width in widths],
-        compiler_params=pltpu.CompilerParams(vmem_limit_bytes=40 * 2**20),
-        cost_estimate=cost(us),
-        name=name,
-    )(*rowed, *whole)
-
-
-def forward_kernel(n_ref, gate_ref, up_ref, down_ref, inner_ref, gelu_ref, slope_ref, terms_ref):
-    gate = dot(n_ref[...], gate_ref[...], NT)
-    up = dot(n_ref[...], up_ref[...], NT)
-    bend, grow = math.sqrt(2.0 / math.pi), 0.044715
-    square = gate * gate
-    wave = jnp.tanh(bend * gate * (1.0 + grow * square))
-    rise = 0.5 * (1.0 + wave)
-    gelu = gate * rise
-    slope = rise + 0.5 * bend * gate * (1.0 - wave * wave) * (1.0 + 3.0 * grow * square)
-    gelu_ref[...] = gelu.astype(BF)
-    slope_ref[...] = (up * slope).astype(BF)
-    inner_ref[...] = (gelu * up).astype(BF)
-    terms_ref[...] = jnp.dot(inner_ref[...], down_ref[...], preferred_element_type=F32).astype(BF)
-
-
-def backward_kernel(d_ref, gelu_ref, slope_ref, gate_ref, up_ref, down_ref, dgate_ref, dup_ref, terms_ref):
-    d_inner = dot(d_ref[...], down_ref[...], NT)
-    dgate_ref[...] = (d_inner * slope_ref[...].astype(F32)).astype(BF)
-    dup_ref[...] = (d_inner * gelu_ref[...].astype(F32)).astype(BF)
-    terms_ref[...] = (
-        jnp.dot(dgate_ref[...], gate_ref[...], preferred_element_type=F32)
-        + jnp.dot(dup_ref[...], up_ref[...], preferred_element_type=F32)
-    ).astype(BF)
-
-
-def prepare_kernel(x_ref, w_ref, g_ref, qk_ref, cos_ref, sin_ref, normed_ref, raw_ref, q_ref, kv_ref):
+    def body(ins, results, rest, ready, store):
+        ready()
+        kernel(*ins, *results, *rest)
+
+    outs = [jax.ShapeDtypeStruct(shape, dtype) for shape, dtype in outs]
+    return staged(
+        body, name, us, args, [pltpu.VMEM] * len(args), outs, [pltpu.VMEM] * len(outs), scratch
+    )
+
+
+def prepare_kernel(parts, x_ref, w_ref, packed_ref, cos_ref, sin_ref, g_ref, qk_ref, normed_ref, raw_ref, q_ref, kv_ref):
+    gain_part, qk_part = parts
+    g_ref[...] = jnp.zeros_like(g_ref)
+    qk_ref[...] = jnp.zeros_like(qk_ref)
+    for i in range(packed_ref.shape[0]):
+        values = packed_ref[i].astype(F32)
+        g_ref[0:4, i * gain_part : (i + 1) * gain_part] = values[0:4, :gain_part]
+        qk_ref[0:2, i * qk_part : (i + 1) * qk_part] = values[4:6, :qk_part]
     x = x_ref[...].astype(F32)
     tokens = x.shape[0]
     normed = (x * scale_of(x) * g_ref[0:1]).astype(BF)
     normed_ref[...] = normed
-    raw_ref[...] = dot(normed, w_ref[...], NT)
+    raw_ref[...] = dot(normed, w_ref[...].reshape(-1, w_ref.shape[-1]), NT)
     cosine, sine = cos_ref[...], sin_ref[...]
     for head in range(HEADS + 1):
         v = raw_ref[:, head * HD : (head + 1) * HD]
@@ -627,27 +862,27 @@
     kv_ref[:, HD:] = raw_ref[:, (HEADS + 1) * HD :].astype(BF)
 
 
-def attend_kernel(q_ref, kv_ref, x_ref, w_ref, g_ref, out_ref, lse_ref, att_ref, branch_ref,
-                  resid_ref, normed_ref, top, total, accum):
-    ctx = lax.axis_index("ctx")
+def attend_kernel(q_ref, kv_ref, x_ref, w_ref, g_ref, out_ref, lse_ref, parts_ref, branch_ref,
+                  resid_ref, normed_ref, top, total, accum, att_ref, ctx):
     tokens = x_ref.shape[0]
     last = lax.div(ctx * tokens, KB)
     q = q_ref[...]
 
-    def block_of(index):
-        return pl.ds(pl.multiple_of(index * KB, KB), KB)
-
-    scores = masked_scores(q, kv_ref[block_of(last), :HD], last, ctx, tokens)
+    def block_of(index, half):
+        per = KB // tokens
+        return kv_ref[pl.ds(index * per, per), :, half * HD : (half + 1) * HD].reshape(KB, HD)
+
+    scores = masked_scores(q, block_of(last, 0), last, ctx, tokens)
     start = jnp.max(scores, axis=-1, keepdims=True)
     probs = jnp.exp(scores - start)
     top[...] = jnp.broadcast_to(start, top.shape)
     total[...] = jnp.broadcast_to(jnp.sum(probs, axis=-1, keepdims=True), total.shape)
     accum[...] = jnp.dot(
-        probs.astype(BF), kv_ref[block_of(last), HD:], preferred_element_type=F32
+        probs.astype(BF), block_of(last, 1), preferred_element_type=F32
     )
 
     def body(index, carry):
-        scores = dot(q, kv_ref[block_of(index), :HD], NT)
+        scores = dot(q, block_of(index, 0), NT)
         old = top[:, :1]
         new = jnp.maximum(old, jnp.max(scores, axis=-1, keepdims=True))
         probs = jnp.exp(scores - new)
@@ -655,7 +890,7 @@
         top[...] = jnp.broadcast_to(new, top.shape)
         total[...] = total[...] * keep + jnp.sum(probs, axis=-1, keepdims=True)
         accum[...] = accum[...] * keep + jnp.dot(
-            probs.astype(BF), kv_ref[block_of(index), HD:], preferred_element_type=F32
+            probs.astype(BF), block_of(index, 1), preferred_element_type=F32
         )
         return carry
 
@@ -666,7 +901,10 @@
         att_ref[:, head * HD : (head + 1) * HD] = out_ref[
             head * tokens : (head + 1) * tokens
         ].astype(BF)
-    branch = jnp.dot(att_ref[...], w_ref[...], preferred_element_type=F32)
+    part = parts_ref.shape[2]
+    for i in range(parts_ref.shape[0]):
+        parts_ref[i] = att_ref[:, i * part : (i + 1) * part]
+    branch = jnp.dot(att_ref[...], w_ref[...].reshape(-1, w_ref.shape[-1]), preferred_element_type=F32)
     branch_ref[...] = branch
     resid = x_ref[...].astype(F32) + branch * scale_of(branch) * g_ref[1:2]
     resid_ref[...] = resid
@@ -674,8 +912,7 @@
 
 
 def attend_back_kernel(dn_ref, resid_ref, branch_ref, cot_ref, g_ref, w_ref, q_ref, kv_ref, out_ref,
-                       lse_ref, dres_ref, low_ref, dg_ref, dq_ref, dkv_ref, d_ref):
-    ctx = lax.axis_index("ctx")
+                       lse_ref, dres_ref, low_ref, dg_ref, dq_ref, dkv_ref, d_ref, ctx):
     tokens = resid_ref.shape[0]
     last = lax.div(ctx * tokens, KB)
     resid = resid_ref[...]
@@ -703,8 +940,12 @@
         probs = jnp.exp(scores - lse)
         d_probs = dot(d_out, kv_ref[block, HD:], NT)
         d_scores = (probs * (d_probs - delta)).astype(BF)
-        dkv_ref[block, :HD] = dot(d_scores, q, TN).astype(BF)
-        dkv_ref[block, HD:] = dot(probs.astype(BF), d_out, TN).astype(BF)
+        d_keys = dot(d_scores, q, TN).astype(BF)
+        d_values = dot(probs.astype(BF), d_out, TN).astype(BF)
+        for i in range(KB // tokens):
+            part = slice(i * tokens, (i + 1) * tokens)
+            dkv_ref[index * (KB // tokens) + i, :, :HD] = d_keys[part]
+            dkv_ref[index * (KB // tokens) + i, :, HD:] = d_values[part]
         return jnp.dot(d_scores, kv_ref[block, :HD], preferred_element_type=F32)
 
     dq_ref[...] = work(last, masked_scores(q, kv_ref[block_of(last), :HD], last, ctx, tokens))
@@ -716,14 +957,14 @@
     lax.fori_loop(0, last, body, 0)
 
     def clear(index, carry):
-        dkv_ref[block_of(index), :] = jnp.zeros((KB, 2 * HD), BF)
+        dkv_ref[index] = jnp.zeros(dkv_ref.shape[1:], BF)
         return carry
 
-    lax.fori_loop(last + 1, kv_ref.shape[0] // KB, clear, 0)
-
-
-def finish_kernel(own_ref, dq_ref, raw_ref, cos_ref, sin_ref, w_ref, x_ref, g_ref, qk_ref, dres_ref,
-                  parts_ref, grad_ref, dg_ref, dqk_ref, mixed_ref):
+    lax.fori_loop((last + 1) * (KB // tokens), dkv_ref.shape[0], clear, 0)
+
+
+def finish_kernel(sizes, own_ref, dq_ref, raw_ref, cos_ref, sin_ref, w_ref, x_ref, g_ref, qk_ref, dres_ref, dg12_ref,
+                  dg3_ref, parts_ref, grad_ref, small_ref, mixed_ref, dqk_ref):
     tokens = x_ref.shape[0]
     cosine, sine = cos_ref[...], sin_ref[...]
     total = jnp.zeros((1, HD), F32)
@@ -752,14 +993,184 @@
     d_normed = jnp.dot(d_mixed, w_ref[...], preferred_element_type=F32)
     x = x_ref[...].astype(F32)
     d_input, dg0 = norm_back(x, scale_of(x), g_ref[0:1], d_normed)
-    dg_ref[...] = jnp.sum(dg0, axis=0, keepdims=True)
+    dg = (jnp.sum(dg0, axis=0, keepdims=True), dg12_ref[0:1], dg12_ref[1:2], dg3_ref[...])
+    small_ref[...] = jnp.zeros_like(small_ref)
+    for i in range(small_ref.shape[0]):
+        for row in range(4):
+            small_ref[i, row : row + 1, : sizes[0]] = dg[row][:, i * sizes[0] : (i + 1) * sizes[0]]
+        small_ref[i, 4:6, : sizes[1]] = dqk_ref[:, i * sizes[1] : (i + 1) * sizes[1]]
     grad_ref[...] = (dres_ref[...] + d_input).astype(BF)
+
+
+class Front:
+    def __init__(self, parts, x, packed, w_qkv, w_out, w_gate_up):
+        self.parts = parts
+        self.arrays = [x, packed, w_qkv, w_out, w_gate_up]
+        like = lambda shape, dtype=BF: jax.ShapeDtypeStruct(shape, dtype)
+        (rows, width), units = x.shape, w_gate_up.shape[0]
+        heads = HEADS * rows
+        self.subs = {
+            "packed": DirectWsh("gather", packed),
+            "qkv": Gather(w_qkv, pair=True),
+            "out": Gather(w_out, pair=True),
+            "kv": Gather(like((rows, 2 * HD)), "ctx"),
+        }
+        self.tables = Tables(rows)
+        self.groups = set().union(*(sub.groups for sub in self.subs.values()))
+        self.outs = [
+            like((8, width), F32), like((8, HD), F32), like((rows, width)), like((rows, (HEADS + 2) * HD), F32),
+            like((heads, HD)), self.subs["kv"].outs[0], self.subs["qkv"].outs[0], self.subs["out"].outs[0],
+            *self.tables.outs, like((units, width)), like((units, width)),
+            like((heads, HD), F32), like((heads, 128), F32), like((8, rows, w_out.shape[0])), like((rows, width), F32),
+            like((rows, width), F32), like((rows, width)),
+        ]
+        self.in_spaces, self.out_spaces = [pltpu.VMEM] * 5, [pltpu.VMEM] * len(self.outs)
+        self.scratch = [
+            pltpu.VMEM((8,) + packed.shape, BF), pltpu.VMEM((rows, 2 * HD), BF), pltpu.VMEM((heads, 128), F32),
+            pltpu.VMEM((heads, 128), F32), pltpu.VMEM((heads, HD), F32), pltpu.VMEM((rows, HEADS * HD), BF),
+        ]
+        self.own = len(self.scratch)
+        for sub in self.subs.values():
+            self.scratch += sub.scratch
+
+    def run(self, p, ins, outs, scratch):
+        x, packed, w_qkv, w_out, w_gate_up = ins
+        (gains, qk_gain, normed, raw, q, kv_all, qkv_all, out_all, cosine, sine, w_gate, w_up, heads, lse, parts,
+         branch, resid, normed2) = outs
+        packed_all, kv, top, total, accum, att = scratch[: self.own]
+        rest = list(scratch[self.own :])
+        held = {name: [rest.pop(0) for _ in sub.scratch] for name, sub in self.subs.items()}
+
+        def begin(name, source, result):
+            return self.subs[name].run(p, [source], [result], held[name])
+
+        p.ready(1, 2)
+        small = begin("packed", packed, packed_all)
+        first = begin("qkv", w_qkv, qkv_all)
+        next(small)
+        next(first)
+        for _ in self.tables.run(p, [], [cosine, sine], []):
+            pass
+        p.ready()
+        split = unpair(w_gate_up, w_gate, w_up)
+        second = begin("out", w_out, out_all)
+        for i, _ in enumerate(first):
+            next(split, None)
+            if i >= 2:
+                next(second, None)
+        for _ in small:
+            pass
+        prepare_kernel(
+            self.parts, x, qkv_all, packed_all, cosine, sine, gains, qk_gain, normed, raw, q, kv
+        )
+        p.store(2)
+        p.store(6)
+        turns = [begin("kv", kv, kv_all), second, split]
+        while turns:
+            turns = [turn for turn in turns if next(turn, "end") != "end"]
+            yield
+        for i in (3, 4, 5, 7, 10, 11):
+            p.store(i)
+        attend_kernel(
+            q, kv_all, x, out_all, gains, heads, lse, parts, branch, resid, normed2, top, total, accum,
+            att, p.ctx,
+        )
+
+
+class Back:
+    attention = ("d_normed", "resid", "branch", "cot", "gains", "w_out", "q", "kv", "out", "lse")
+    names = attention + (
+        "raw", "cosine", "sine", "w_qkv", "x", "qk_gain", "dg3", "attended", "normed", "early", "late"
+    )
+
+    def __init__(self, parts, **arrays):
+        self.parts = parts
+        self.arrays = [arrays[name] for name in self.names]
+        like = lambda shape, dtype=BF: jax.ShapeDtypeStruct(shape, dtype)
+        (rows, width), heads = arrays["resid"].shape, arrays["q"].shape[0]
+        qkv = arrays["w_qkv"].shape[0] // 8
+        out = arrays["attended"].shape[2]
+        mixed, small = like((8, rows, qkv)), like((8, 8, 256), F32)
+        every = like((8, rows, width))
+        self.subs = {
+            "early": Gather(arrays["early"], "ctx"),
+            "late": Gather(arrays["late"], "ctx"),
+            "kv": ScatterCtx(like((8, 2, rows, 2 * HD))),
+            "d_branch": Gather(like((rows, width))),
+            "attended": DirectWsh("scatter", arrays["attended"]),
+            "mixed": DirectWsh("scatter", mixed, 3),
+            "small": DirectWsh("scatter", small, 3),
+            "sum": SumCtx(mixed, every, like((8, rows, out)), every),
+            "share": ShareCtx(like((8, 256), F32)),
+        }
+        self.groups = set().union(*(sub.groups for sub in self.subs.values()))
+        self.outs = [like((rows, width))]
+        self.outs += [self.subs[name].outs[0] for name in ("sum", "share", "early", "late")]
+        self.in_spaces = [pltpu.VMEM] * (len(self.names) - 2) + [HBM] * 2
+        self.out_spaces = [pltpu.VMEM, pltpu.VMEM, HBM, HBM, HBM]
+        shapes = [
+            ((rows, width), F32), ((rows, width), BF), ((2, width), F32), ((heads, HD), F32), ((8 * 2, rows, 2 * HD), BF),
+            ((heads, HD), BF), ((rows, 2 * HD), F32), ((8, rows, width), BF), ((8, rows, out), BF), ((8, rows, qkv), BF),
+            ((8, 8, 256), F32), ((8, rows, qkv), BF), ((8, 8, 256), F32), ((8, 256), F32),
+            ((rows, (HEADS + 2) * HD), BF), ((2, HD), F32),
+        ]
+        self.own = len(shapes)
+        self.scratch = [pltpu.VMEM(*shape) for shape in shapes]
+        for sub in self.subs.values():
+            self.scratch += sub.scratch
+
+    def run(self, p, ins, outs, scratch):
+        a = dict(zip(self.names, ins))
+        grad, grads, small_parts, early_all, late_all = outs
+        (d_resid, low, dg12, d_q, d_kv, d_heads, own_kv, db_all, at_all, d_mixed, small, dm_all, small_all, small_sum,
+         mixed, dqk) = scratch[: self.own]
+        rest = list(scratch[self.own :])
+        held = {}
+        for name, sub in self.subs.items():
+            held[name] = [rest.pop(0) for _ in sub.scratch]
+
+        def begin(name, sources, result):
+            return self.subs[name].run(p, sources, [result], held[name])
+
+        early = begin("early", [a["early"]], early_all)
+        late = begin("late", [a["late"]], late_all)
+        attended = begin("attended", [a["attended"]], at_all)
+        next(early)
+        p.ready()
+        next(attended)
+        attend_back_kernel(
+            *(a[name] for name in self.attention),
+            d_resid, low, dg12, d_q, d_kv, d_heads, p.ctx,
+        )
+        kv = begin("kv", [d_kv], own_kv)
+        turns = [kv, begin("d_branch", [low], db_all), early]
+        while kv in turns:
+            turns = [turn for turn in turns if next(turn, "end") != "end"]
+        finish_kernel(
+            self.parts, own_kv, d_q, a["raw"], a["cosine"], a["sine"], a["w_qkv"], a["x"], a["gains"], a["qk_gain"],
+            d_resid, dg12, a["dg3"], d_mixed, grad, small, mixed, dqk,
+        )
+        columns = [begin("mixed", [d_mixed], dm_all), begin("small", [small], small_all)]
+        turns = columns + turns + [late]
+        while any(turn in turns for turn in columns):
+            turns = [turn for turn in turns if next(turn, "end") != "end"]
+        for turn in turns[:-1] if late in turns else turns:
+            for _ in turn:
+                pass
+        for _ in attended:
+            pass
+        small_sum[...] = jnp.sum(small_all[...], axis=0)
+        share = begin("share", [small_sum], small_parts)
+        total = begin("sum", [dm_all, a["normed"], at_all, db_all], grads)
+        turns = [share, total] + ([late] if late in turns else [])
+        while turns:
+            turns = [turn for turn in turns if next(turn, "end") != "end"]
+            yield
 
 
 def on_device(hidden, w_qkv, w_out, norm_gains, qk_gains, w_gate_up, w_down, cotangent):
     tokens = hidden.shape[1]
     width = hidden.shape[2]
-    cot = cotangent[0].astype(F32)
     gain_part, qk_part = norm_gains.shape[0], qk_gains.shape[0]
     packed = jnp.concatenate(
         [
@@ -767,105 +1178,34 @@
             jnp.pad(qk_gains.T, ((0, 10), (0, 256 - qk_part))),
         ]
     )
-    all_packed, all_qkv, all_out, cosine, sine, w_gate, w_up = transfer(
-        1, "gather_weights", 30,
-        DirectWsh("gather", packed), Gather(w_qkv, pair=True), Gather(w_out, pair=True), Tables(tokens),
-        Unpair(w_gate_up),
+    (gains, qk_gain, normed, raw, q_low, whole_kv, full_qkv, full_out, cosine, sine, w_gate, w_up, out_heads, lse,
+     attended, branch, resid, normed2) = transfer(
+        1, "front", 70, Front((gain_part, qk_part), hidden[0], packed, w_qkv, w_out, w_gate_up)
     )
-    full_qkv, full_out = all_qkv.reshape(-1, width), all_out.reshape(-1, width)
-    gains = all_packed[:, :4, :gain_part].transpose(1, 0, 2).reshape(4, width).astype(F32)
-    qk_gain = all_packed[:, 4:6, :qk_part].transpose(1, 0, 2).reshape(2, HD).astype(F32)
-
-    heads = HEADS * tokens
-    normed, raw, q_low, local_kv = compute(
-        prepare_kernel, "prepare", 6,
-        [((tokens, width), BF), ((tokens, (HEADS + 2) * HD), F32), ((heads, HD), BF), ((tokens, 2 * HD), BF)],
-        [], hidden[0], full_qkv, gains, qk_gain, cosine, sine,
+    full_qkv, full_out = full_qkv.reshape(-1, width), full_out.reshape(-1, width)
+    whole_kv = whole_kv.reshape(-1, 2 * HD)
+
+    output, dg3, d_normed2, ff_early, ff_late, normed_all = transfer(
+        3, "feed_forward", 100, FeedForward(normed2, resid, cotangent[0], gains, w_gate, w_up, w_down, normed)
     )
-    normed_all, whole_kv = transfer(2, "gather_kv", 25, Gather(normed), Gather(local_kv, "ctx"))
-    whole_kv, normed_all = whole_kv.reshape(-1, 2 * HD), normed_all.reshape(-1, width)
-    out_heads, lse, attended, branch, resid, normed2 = compute(
-        attend_kernel, "attend", 10,
-        [((heads, HD), F32), ((heads, 128), F32), ((tokens, HEADS * HD), BF), ((tokens, width), F32),
-         ((tokens, width), F32), ((tokens, width), BF)],
-        [pltpu.VMEM((heads, 128), F32), pltpu.VMEM((heads, 128), F32), pltpu.VMEM((heads, HD), F32)],
-        q_low, whole_kv, hidden[0], full_out, gains,
+    grad_hidden, grads, small_parts, early_all, late_all = transfer(
+        7, "backward", 80,
+        Back(
+            (gain_part, qk_part), d_normed=d_normed2, resid=resid, branch=branch, cot=cotangent[0], gains=gains,
+            w_out=full_out, q=q_low, kv=whole_kv, out=out_heads, lse=lse, raw=raw, cosine=cosine, sine=sine,
+            w_qkv=full_qkv, x=hidden[0], qk_gain=qk_gain, dg3=dg3, attended=attended, normed=normed_all,
+            early=ff_early, late=ff_late,
+        ),
     )
-
-    (n2_all,) = transfer(3, "gather_normed2", 24, Gather(normed2))
-    n2_all = n2_all.reshape(-1, width)
-    units = w_down.shape[0]
-    inner, gelu, slope, terms = tiled(
-        forward_kernel, "feed_forward", 10, [units, units, units, width], [n2_all], [w_gate, w_up, w_down]
+    grad_gate_up, grad_down, grad_qkv, grad_out, small_sum = widen(
+        early_all.reshape(-1, width), late_all.reshape(-1, width), w_down.shape[0], grads, small_parts,
+        (w_qkv.shape[0], w_out.shape[0]),
     )
-    (branch2,) = transfer(4, "scatter_branch2", 24, Scatter(terms.reshape(8, tokens, width)))
-
-    r3 = scale_of(branch2)
-    output = (resid + branch2 * r3 * gains[3]).astype(BF)
-    d_branch2, dg3 = norm_back(branch2, r3, gains[3], cot)
-    (d2_all,) = transfer(5, "gather_d_branch2", 24, Gather(d_branch2.astype(BF)))
-    d2_all = d2_all.reshape(-1, width)
-    d_gate, d_up, terms = tiled(
-        backward_kernel, "feed_forward_back", 8, [units, units, width],
-        [d2_all, gelu, slope], [w_gate, w_up, w_down],
-    )
-    d_normed2, ff_early, ff_sums = transfer(
-        6, "scatter_d_normed2", 40,
-        Scatter(terms.reshape(8, tokens, width)),
-        FeedForwardGrads(d_gate, d_up, inner, n2_all, d2_all),
-    )
-
-    d_resid, branch_low, dg12, d_q, d_kv = compute(
-        attend_back_kernel, "attend_back", 10,
-        [((tokens, width), F32), ((tokens, width), BF), ((2, width), F32), ((heads, HD), F32),
-         (whole_kv.shape, BF)],
-        [pltpu.VMEM((heads, HD), BF)],
-        d_normed2, resid, branch, cotangent[0], gains, full_out, q_low, whole_kv, out_heads, lse,
-    )
-    qkv_part, out_part = w_qkv.shape[0], w_out.shape[0]
-    at_all, db_all, own_kv, ff_late = transfer(
-        7, "scatter_d_kv", 30,
-        DirectWsh("scatter", attended.reshape(tokens, 8, out_part).transpose(1, 0, 2)),
-        Gather(branch_low),
-        ScatterCtx(d_kv.reshape(8, 2, tokens, 2 * HD)),
-        Scatter(ff_sums, "ctx", BF),
-    )
-    grad_out = dot(at_all.reshape(-1, out_part), db_all.reshape(-1, width), TN)
-    d_mixed, grad_hidden, dg0, dqk, _ = compute(
-        finish_kernel, "finish", 6,
-        [((8, tokens, qkv_part), BF), ((tokens, width), BF), ((1, width), F32), ((2, HD), F32),
-         ((tokens, (HEADS + 2) * HD), BF)],
-        [], own_kv, d_q, raw, cosine, sine, full_qkv, hidden[0], gains, qk_gain, d_resid,
-    )
-
-    dg = jnp.concatenate([dg0, dg12, jnp.sum(dg3, axis=0, keepdims=True)])
-    dg = jnp.pad(dg.reshape(4, 8, gain_part).transpose(1, 0, 2), ((0, 0), (0, 0), (0, 256 - gain_part)))
-    dqk = jnp.pad(dqk.reshape(2, 8, qk_part).transpose(1, 0, 2), ((0, 0), (0, 2), (0, 256 - qk_part)))
-    dm_all, small_all, early_all = transfer(
-        8, "columns_to_owners", 12,
-        DirectWsh("scatter", d_mixed),
-        DirectWsh("scatter", jnp.concatenate([dg, dqk], axis=1)),
-        Gather(ff_early, "ctx"),
-    )
-    grad_qkv = dot(dm_all.reshape(-1, qkv_part), normed_all, TN)
-    both = jnp.concatenate([grad_qkv, grad_out], axis=0).astype(BF)
-    share = both.shape[0] // 16
-    room = -(-share // 16) * 16
-    both = jnp.pad(both.reshape(8, 2, share, width), ((0, 0), (0, 0), (0, room - share), (0, 0)))
-    small_parts, grads, late_all = transfer(
-        9, "sum_grads", 40,
-        ShareCtx(jnp.sum(small_all, axis=0)), SumCtx(both), Gather(ff_late, "ctx"),
-    )
-    grad_gate_up, grad_down = widen(
-        early_all.reshape(-1, width), late_all.reshape(-1, width), units
-    )
-    grads = grads[:, :, :share].reshape(-1, width).astype(F32)
-    small_sum = jnp.sum(small_parts, axis=0)
     return (
         output[None],
         grad_hidden[None],
-        grads[:qkv_part],
-        grads[qkv_part:],
+        grad_qkv,
+        grad_out,
         small_sum[:4, :gain_part].T,
         small_sum[4:6, :qk_part].T,
         grad_gate_up,

time: 379 us -> 298 us (0.79)
  the two profiles are of different devices: /device:TPU:0 before, /device:TPU:105 now
where the time goes in v4:
time: 298 us; the launch traced here: 293 us
  Pallas kernels  287 us (96%)
  local copies, waits for them, and re-layouts  3.98 us (1%)
    pallas_call x3, Pallas kernels, staged(): pl.pallas_call(kernel, out_shape=list(outs), in_specs=[pl.BlockSpec(memor...  275 us
    pallas_call x1, Pallas kernels, widen(): pl.pallas_call(functools.partial(widen_kernel, first), grid=(count,), out...  11.7 us

profile of v4, /device:TPU:105, one launch (start us, length us, event | category | flops | bytes accessed | tf_op | source)
XLA Modules:
  0.0 293.3 jit_solution(266538945801713344)
XLA Ops:
  0.6 1.3 fusion.2.refs_1_
  1.9 53.1 %front.1 = (f32[8,1152]{1,0:T(8,128)}, f32[8,256]{1,0:T(8,128)}, bf16[128,1152]{1,0:T(8,128)(2,1)}, f32[128,1536]{1,0:T(8,128)}, bf16[512,256]{1,0:T(8,128)(2,1)...) custom-call(bf16[128,1152]{1,0:T(8,128)(2,1)} %bitcast.22, ...), custom_call_target="tpu_custom_call" | custom-call | bytes 210000000 | tf_op jit(solution)/shard_map/front/pallas_call | solution.py:710
  55.0 130.9 %feed_forward.1 = (bf16[128,1152]{1,0:T(8,128)(2,1)}, f32[1,1152]{1,0:T(1,128)}, f32[128,1152]{1,0:T(8,128)}, bf16[96,1152]{1,0:T(8,128)(2,1)}, bf16[80,1152]{1,0:T(8,128)(2,1)}, /*index=5*/bf16[8,128,1152]{2,1,0:T(8,128)(2,1)}) custom-call(bf16[128,1152]{1,0:T(8,128)(2,1)} %get-tuple-element.42.refs_0_, f32[128,1152]{1,0:T(8,128)} %get-tuple-element.43.refs_1_, ...), custom_call_target="tpu_custom_call" | custom-call | bytes 300000000 | tf_op jit(solution)/shard_map/feed_forward/pallas_call | solution.py:710
  185.9 91.2 %backward.1 = (bf16[128,1152]{1,0:T(8,128)(2,1)}, bf16[8,2,32,1152]{3,2,1,0:T(8,128)(2,1)}, f32[16,8,256]{2,1,0:T(8,128)}, bf16[16,96,1152]{2,1,0:T(8,128)(2,1)}, bf16[16,80,1152]{2,1,0:T(8,128)(2,1)}) custom-call(f32[128,1152]{1,0:T(8,128)} %get-tuple-element.49.refs_0_, f32[128,1152]{1,0:T(8,128)} %get-tuple-element.43.refs_1_, ...), custom_call_target="tpu_custom_call" | custom-call | bytes 240000000 | tf_op jit(solution)/shard_map/backward/pallas_call | solution.py:710
  277.2 0.0 copy-start
  277.2 0.0 copy-start.1
  277.2 11.7 %widen.1 = (f32[864,2,1152]{2,1,0:T(2,128)}, f32[864,1152]{1,0:T(8,128)}, f32[192,1152]{1,0:T(8,128)}, f32[128,1152]{1,0:T(8,128)}, f32[8,256]{1,0:T(8,128)}) custom-call(bf16[1536,1152]{1,0:T(8,128)(2,1)} %bitcast.15, bf16[1536,1152]{1,0:T(8,128)(2,1)} %bitcast.16, bf16[1280,1152]{1,0:T(8,128)(2,1)} %bitcast.17, bf16[1280,1152]{1,0:T(8,128)(2,1)} %bitcast.18, ...), custom_call_target="tpu_custom_call" | custom-call | bytes 27000000 | tf_op jit(solution)/shard_map/widen/pallas_call | solution.py:779
  288.9 1.3 slice_bitcast_fusion
  290.2 1.2 slice_bitcast_fusion.1
  291.4 0.0 copy-done
  291.4 0.7 copy.18
  292.2 0.0 copy-done.1
  292.2 0.7 copy.19
Async XLA Ops:
  277.2 14.3 %copy-start = (bf16[128,1152]{1,0:T(8,128)(2,1)S(1)}, bf16[128,1152]{1,0:T(8,128)(2,1)}, u32[]{:S(2)}) copy-start(bf16[128,1152]{1,0:T(8,128)(2,1)} %get-tuple-element.48) | copy-start | bytes 884740
  277.2 15.0 %copy-start.1 = (bf16[128,1152]{1,0:T(8,128)(2,1)S(1)}, bf16[128,1152]{1,0:T(8,128)(2,1)}, u32[]{:S(2)}) copy-start(bf16[128,1152]{1,0:T(8,128)(2,1)} %get-tuple-element.66) | copy-start | bytes 884740

commit v5 on v4

--- a/solution.py
+++ b/solution.py
@@ -90,8 +90,8 @@
 
 
 class Gather:
-    def __init__(self, array, axis="wsh", pair=False):
-        self.arrays, self.axis, self.pair = [array], axis, pair
+    def __init__(self, array, axis="wsh", pair=False, ring=False):
+        self.arrays, self.axis, self.pair, self.ring = [array], axis, pair, ring
         self.twins = pair or axis == "ctx"
         self.groups = {axis, "twin"} if self.twins else {axis}
         count = 16 if axis == "ctx" else 8
@@ -128,6 +128,36 @@
         local = pltpu.make_async_copy(x, o.at[me], own)
         local.start()
         yield
+        if self.ring:
+            across = lambda i, place, rows: send(i, g.block(h, place), rows, g.across)
+            arrived(0, g.block(h, g.ym), every)
+            send(3, g.block(h, g.ym), low, g.up)
+            across(5, g.ym, every)
+            yield
+            arrived(1, g.block(h, g.yp), every)
+            send(4, g.block(h, g.yp), high, g.down)
+            across(6, g.yp, every)
+            yield
+            arrived(2, g.block(other, g.y), every)
+            arrived(3, g.block(h, g.y2), low)
+            across(7, g.y2, low)
+            yield
+            arrived(4, g.block(h, g.y2), high)
+            across(8, g.y2, high)
+            yield
+            arrived(5, g.block(other, g.ym), every)
+            yield
+            arrived(6, g.block(other, g.yp), every)
+            yield
+            arrived(7, g.block(other, g.y2), low)
+            arrived(8, g.block(other, g.y2), high)
+            yield
+            for i, copy in copies.items():
+                copy.wait_send()
+                if i >= 9:
+                    copy.wait_recv()
+            local.wait()
+            return
         block = g.block(other, g.y)
         arrived(2, block, every)
         send(5, block, every, g.up)
@@ -259,7 +289,7 @@
             copies.append(remote(x.at[2 * chip + 1 - p.core], pair.at[chip], sems, i, p.twin))
             copies[-1].start()
         for i, step in enumerate(order):
-            if i % 3 == 0:
+            if i == 0:
                 yield
             chip = lax.rem(p.chip + step, 8)
             copies[i].wait_recv()
@@ -372,7 +402,8 @@
         early = granules * 5 // 9
         self.pieces = (early * 16, (granules - early) * 16)
         sums = [pltpu.VMEM((8, rows, width), BF) for rows in self.pieces]
-        self.scatters = [Scatter(jax.ShapeDtypeStruct(b.shape, BF), "ctx", BF) for b in sums]
+        pieces = [jax.ShapeDtypeStruct(b.shape, BF) for b in sums]
+        self.scatters = [Scatter(piece, "ctx", BF) for piece in pieces]
         self.outs = self.scatters[0].outs + self.scatters[1].outs
         self.in_spaces, self.out_spaces = [pltpu.VMEM] * 5, [pltpu.VMEM] * 2
         self.scratch = [pltpu.VMEM((16 * rows, width), BF) for rows in self.pieces]
@@ -408,7 +439,6 @@
                 twins[8 * number + chip].wait_recv()
                 result[chip] = (whole[here].astype(F32) + pair[chip].astype(F32)).astype(BF)
 
-        yield
         started = False
         for number, (left, right) in enumerate(((d_gate, normed), (d_up, normed), (inner, d_branch))):
             for start in range(0, units, 256):
@@ -417,7 +447,8 @@
                 if not started and number * units + stop >= split:
                     started = True
                     swap(first, pair_first, 0)
-            yield
+            if started:
+                yield
         missing = second.shape[0] - (3 * units - split)
         if missing:
             second[second.shape[0] - missing :] = jnp.zeros((missing, second.shape[1]), BF)
@@ -559,26 +590,24 @@
 
 
 class FeedForward:
-    def __init__(self, normed, resid, cot, gains, w_gate, w_up, w_down, first_normed):
+    def __init__(self, normed, resid, cot, gains, w_gate, w_up, w_down):
         (rows, width), units = normed.shape, w_down.shape[0]
-        self.arrays = [normed, resid, cot, gains, w_gate, w_up, w_down, first_normed]
-        self.gather = Gather(first_normed)
+        self.arrays = [normed, resid, cot, gains, w_gate, w_up, w_down]
         tokens = jax.ShapeDtypeStruct((8 * rows, width), BF)
         hidden = jax.ShapeDtypeStruct((8 * rows, units), BF)
         self.grads = FeedForwardGrads(hidden, hidden, hidden, tokens, tokens)
         self.groups = {"wsh"} | self.grads.groups
         shapes = [((rows, width), BF), ((1, width), F32), ((rows, width), F32)]
         self.outs = [jax.ShapeDtypeStruct(*shape) for shape in shapes] + self.grads.outs
-        self.outs += self.gather.outs
-        self.in_spaces, self.out_spaces = [pltpu.VMEM] * 7 + [HBM], [pltpu.VMEM] * 5 + [HBM]
+        self.in_spaces, self.out_spaces = [pltpu.VMEM] * 7, [pltpu.VMEM] * 5
         wide, narrow = pltpu.VMEM(tokens.shape, BF), pltpu.VMEM(hidden.shape, BF)
         self.scratch = [wide] * 3 + [narrow] * 5 + [pltpu.VMEM((rows, width), F32), pltpu.VMEM((rows, width), BF)]
         self.scratch += [pltpu.SemaphoreType.DMA((2, 9))] * 2
-        self.scratch += RingSum.scratch(rows, width) * 2 + self.grads.scratch + self.gather.scratch
+        self.scratch += RingSum.scratch(rows, width) * 2 + self.grads.scratch
 
     def run(self, p, ins, outs, scratch):
-        x, resid, cot, gains, w_gate, w_up, w_down, first_normed = ins
-        out, dg, d_normed, *grads, first_all = outs
+        x, resid, cot, gains, w_gate, w_up, w_down = ins
+        out, dg, d_normed, *grads = outs
         tokens, terms, d_all, inner, gelu, slope, d_gate, d_up, branch, low, sems, back_sems, *rest = scratch
         g = p.grids["wsh"]
         count = len(RingSum.scratch(*x.shape))
@@ -617,15 +646,9 @@
                 + jnp.dot(d_up[rows], w_up[...], preferred_element_type=F32)
             ).astype(BF)
             sends(back, i)
-        last = len(self.gather.scratch)
-
-        def others():
-            yield from back.rest()
-            yield from self.gather.run(p, [first_normed], [first_all], rest[-last:])
-
         turns = [
-            self.grads.run(p, [d_gate, d_up, inner, tokens, d_all], grads, rest[2 * count : -last]),
-            others(),
+            self.grads.run(p, [d_gate, d_up, inner, tokens, d_all], grads, rest[2 * count :]),
+            back.rest(),
         ]
         while turns:
             turns = [turn for turn in turns if next(turn, "end") != "end"]
@@ -742,9 +765,23 @@
     return jnp.where(col <= row, scores, MASKED)
 
 
-def widen_kernel(first, gate_ref, up_ref, more_ref, low_ref, grads_ref, small_ref, both_ref, down_ref, qkv_ref, out_ref,
-                 sum_ref):
-    @pl.when(pl.program_id(0) == 0)
+def widen_kernel(first, sizes, gate_ref, *refs):
+    ups, mores, lows = refs[:3], refs[3:6], refs[6:9]
+    grads_ref, small_ref, both_ref, down_ref, qkv_ref, out_ref, gains_ref, qk_ref = refs[9:]
+    step = ups[0].shape[0]
+    place = pl.program_id(0)
+    both_ref[:, 0, :] = gate_ref[...].astype(F32)
+    for k in range(3):
+        rows = slice(k * step, (k + 1) * step)
+        down_ref[rows] = lows[k][...].astype(F32)
+
+        def put(value, rows=rows):
+            both_ref[rows, 1, :] = value[...].astype(F32)
+
+        pl.when(3 * place + k < first)(functools.partial(put, ups[k]))
+        pl.when(3 * place + k >= first)(functools.partial(put, mores[k]))
+
+    @pl.when(place == 0)
     def _():
         share, split = (qkv_ref.shape[0] + out_ref.shape[0]) // 16, qkv_ref.shape[0]
         for i in range(16):
@@ -755,55 +792,35 @@
                 qkv_ref[start:middle] = value[: middle - start]
             if stop > middle:
                 out_ref[middle - split : stop - split] = value[middle - start : share]
-        sum_ref[...] = jnp.sum(small_ref[...], axis=0)
-
-    both_ref[:, 0, :] = gate_ref[...].astype(F32)
-    down_ref[...] = low_ref[...].astype(F32)
-
-    @pl.when(pl.program_id(0) < first)
-    def _():
-        both_ref[:, 1, :] = up_ref[...].astype(F32)
-
-    @pl.when(pl.program_id(0) >= first)
-    def _():
-        both_ref[:, 1, :] = more_ref[...].astype(F32)
-
-
-def widen(early, late, rows, grads, small, parts):
+        total = jnp.sum(small_ref[...], axis=0)
+        gains_ref[...] = total[0:4, : sizes[0]]
+        qk_ref[...] = total[4:6, : sizes[1]]
+
+
+def widen(early, late, rows, grads, small, parts, sizes):
     width = early.shape[1]
     step = 96
     count = rows // step
     first = early.shape[0] // step - count
     spec = lambda index: pl.BlockSpec((step, width), lambda i: (index(i), 0))
+    large = pl.BlockSpec((3 * step, width), lambda i: (i, 0))
     whole = lambda shape: pl.BlockSpec(shape, lambda i: (0,) * len(shape))
+    outs = [(rows, 2, width), (rows, width), (parts[0], width), (parts[1], width), (4, sizes[0]), (2, sizes[1])]
     return pl.pallas_call(
-        functools.partial(widen_kernel, first),
-        grid=(count,),
-        out_shape=[
-            jax.ShapeDtypeStruct((rows, 2, width), F32),
-            jax.ShapeDtypeStruct((rows, width), F32),
-            jax.ShapeDtypeStruct((parts[0], width), F32),
-            jax.ShapeDtypeStruct((parts[1], width), F32),
-            jax.ShapeDtypeStruct(small.shape[1:], F32),
-        ],
-        in_specs=[
-            spec(lambda i: i),
-            spec(lambda i: jnp.minimum(i, first - 1) + count),
-            spec(lambda i: jnp.maximum(i - first, 0)),
-            spec(lambda i: i + count - first),
-            whole(grads.shape),
-            whole(small.shape),
-        ],
-        out_specs=[
-            pl.BlockSpec((step, 2, width), lambda i: (i, 0, 0)),
-            spec(lambda i: i),
-            whole((parts[0], width)),
-            whole((parts[1], width)),
-            whole(small.shape[1:]),
-        ],
+        functools.partial(widen_kernel, first, sizes),
+        grid=(count // 3,),
+        out_shape=[jax.ShapeDtypeStruct(shape, F32) for shape in outs],
+        in_specs=[large]
+        + [spec(lambda i, k=k: jnp.minimum(3 * i + k, first - 1) + count) for k in range(3)]
+        + [spec(lambda i, k=k: jnp.maximum(3 * i + k - first, 0)) for k in range(3)]
+        + [spec(lambda i, k=k: 3 * i + k + count - first) for k in range(3)]
+        + [whole(grads.shape), whole(small.shape)],
+        out_specs=[pl.BlockSpec((3 * step, 2, width), lambda i: (i, 0, 0)), large]
+        + [whole(shape) for shape in outs[2:]],
+        compiler_params=pltpu.CompilerParams(vmem_limit_bytes=ROOM),
         cost_estimate=cost(9),
         name="widen",
-    )(early, early, late, late, grads, small)
+    )(early, *[early] * 3, *[late] * 6, grads, small)
 
 
 def scale_of(values):
@@ -1094,9 +1111,10 @@
         every = like((8, rows, width))
         self.subs = {
             "early": Gather(arrays["early"], "ctx"),
-            "late": Gather(arrays["late"], "ctx"),
+            "late": Gather(arrays["late"], "ctx", ring=True),
             "kv": ScatterCtx(like((8, 2, rows, 2 * HD))),
             "d_branch": Gather(like((rows, width))),
+            "normed": Gather(like((rows, width))),
             "attended": DirectWsh("scatter", arrays["attended"]),
             "mixed": DirectWsh("scatter", mixed, 3),
             "small": DirectWsh("scatter", small, 3),
@@ -1106,13 +1124,14 @@
         self.groups = set().union(*(sub.groups for sub in self.subs.values()))
         self.outs = [like((rows, width))]
         self.outs += [self.subs[name].outs[0] for name in ("sum", "share", "early", "late")]
-        self.in_spaces = [pltpu.VMEM] * (len(self.names) - 2) + [HBM] * 2
+        self.in_spaces = [pltpu.VMEM] * (len(self.names) - 3) + [HBM] * 3
         self.out_spaces = [pltpu.VMEM, pltpu.VMEM, HBM, HBM, HBM]
         shapes = [
             ((rows, width), F32), ((rows, width), BF), ((2, width), F32), ((heads, HD), F32), ((8 * 2, rows, 2 * HD), BF),
             ((heads, HD), BF), ((rows, 2 * HD), F32), ((8, rows, width), BF), ((8, rows, out), BF), ((8, rows, qkv), BF),
             ((8, 8, 256), F32), ((8, rows, qkv), BF), ((8, 8, 256), F32), ((8, 256), F32),
             ((rows, (HEADS + 2) * HD), BF), ((2, HD), F32),
+            ((8, rows, width), BF),
         ]
         self.own = len(shapes)
         self.scratch = [pltpu.VMEM(*shape) for shape in shapes]
@@ -1123,7 +1142,7 @@
         a = dict(zip(self.names, ins))
         grad, grads, small_parts, early_all, late_all = outs
         (d_resid, low, dg12, d_q, d_kv, d_heads, own_kv, db_all, at_all, d_mixed, small, dm_all, small_all, small_sum,
-         mixed, dqk) = scratch[: self.own]
+         mixed, dqk, normed_all) = scratch[: self.own]
         rest = list(scratch[self.own :])
         held = {}
         for name, sub in self.subs.items():
@@ -1135,6 +1154,8 @@
         early = begin("early", [a["early"]], early_all)
         late = begin("late", [a["late"]], late_all)
         attended = begin("attended", [a["attended"]], at_all)
+        normed = begin("normed", [a["normed"]], normed_all)
+        next(normed)
         next(early)
         p.ready()
         next(attended)
@@ -1143,9 +1164,10 @@
             d_resid, low, dg12, d_q, d_kv, d_heads, p.ctx,
         )
         kv = begin("kv", [d_kv], own_kv)
-        turns = [kv, begin("d_branch", [low], db_all), early]
+        turns = [kv, normed, begin("d_branch", [low], db_all), early]
         while kv in turns:
             turns = [turn for turn in turns if next(turn, "end") != "end"]
+        next(late)
         finish_kernel(
             self.parts, own_kv, d_q, a["raw"], a["cosine"], a["sine"], a["w_qkv"], a["x"], a["gains"], a["qk_gain"],
             d_resid, dg12, a["dg3"], d_mixed, grad, small, mixed, dqk,
@@ -1161,7 +1183,7 @@
             pass
         small_sum[...] = jnp.sum(small_all[...], axis=0)
         share = begin("share", [small_sum], small_parts)
-        total = begin("sum", [dm_all, a["normed"], at_all, db_all], grads)
+        total = begin("sum", [dm_all, normed_all, at_all, db_all], grads)
         turns = [share, total] + ([late] if late in turns else [])
         while turns:
             turns = [turn for turn in turns if next(turn, "end") != "end"]
@@ -1185,29 +1207,29 @@
     full_qkv, full_out = full_qkv.reshape(-1, width), full_out.reshape(-1, width)
     whole_kv = whole_kv.reshape(-1, 2 * HD)
 
-    output, dg3, d_normed2, ff_early, ff_late, normed_all = transfer(
-        3, "feed_forward", 100, FeedForward(normed2, resid, cotangent[0], gains, w_gate, w_up, w_down, normed)
+    output, dg3, d_normed2, ff_early, ff_late = transfer(
+        3, "feed_forward", 100, FeedForward(normed2, resid, cotangent[0], gains, w_gate, w_up, w_down)
     )
     grad_hidden, grads, small_parts, early_all, late_all = transfer(
         7, "backward", 80,
         Back(
             (gain_part, qk_part), d_normed=d_normed2, resid=resid, branch=branch, cot=cotangent[0], gains=gains,
             w_out=full_out, q=q_low, kv=whole_kv, out=out_heads, lse=lse, raw=raw, cosine=cosine, sine=sine,
-            w_qkv=full_qkv, x=hidden[0], qk_gain=qk_gain, dg3=dg3, attended=attended, normed=normed_all,
+            w_qkv=full_qkv, x=hidden[0], qk_gain=qk_gain, dg3=dg3, attended=attended, normed=normed,
             early=ff_early, late=ff_late,
         ),
     )
-    grad_gate_up, grad_down, grad_qkv, grad_out, small_sum = widen(
+    grad_gate_up, grad_down, grad_qkv, grad_out, grad_gains, grad_qk = widen(
         early_all.reshape(-1, width), late_all.reshape(-1, width), w_down.shape[0], grads, small_parts,
-        (w_qkv.shape[0], w_out.shape[0]),
+        (w_qkv.shape[0], w_out.shape[0]), (gain_part, qk_part),
     )
     return (
         output[None],
         grad_hidden[None],
         grad_qkv,
         grad_out,
-        small_sum[:4, :gain_part].T,
-        small_sum[4:6, :qk_part].T,
+        grad_gains.T,
+        grad_qk.T,
         grad_gate_up,
         grad_down,
     )

time: 298 us -> 288 us (0.966)
  the two profiles are of different devices: /device:TPU:105 before, /device:TPU:0 now
where the time goes in v5:
time: 288 us; the launch traced here: 282 us
  Pallas kernels  279 us (97%)
    pallas_call x3, Pallas kernels, staged(): pl.pallas_call(kernel, out_shape=list(outs), in_specs=[pl.BlockSpec(memor...  269 us
    pallas_call x1, Pallas kernels, widen(): pl.pallas_call(functools.partial(widen_kernel, first, sizes), grid=(count...  9.52 us

profile of v5, /device:TPU:0, one launch (start us, length us, event | category | flops | bytes accessed | tf_op | source)
XLA Modules:
  0.0 282.5 jit_solution(11541716966175376527)
XLA Ops:
  0.6 1.3 fusion.2.refs_1_
  1.9 54.9 %front.1 = (f32[8,1152]{1,0:T(8,128)}, f32[8,256]{1,0:T(8,128)}, bf16[128,1152]{1,0:T(8,128)(2,1)}, f32[128,1536]{1,0:T(8,128)}, bf16[512,256]{1,0:T(8,128)(2,1)...) custom-call(bf16[128,1152]{1,0:T(8,128)(2,1)} %bitcast.26, ...), custom_call_target="tpu_custom_call" | custom-call | bytes 210000000 | tf_op jit(solution)/shard_map/front/pallas_call | solution.py:733
  56.8 128.9 %feed_forward.1 = (bf16[128,1152]{1,0:T(8,128)(2,1)}, f32[1,1152]{1,0:T(1,128)}, f32[128,1152]{1,0:T(8,128)}, bf16[96,1152]{1,0:T(8,128)(2,1)}, bf16[80,1152]{1,0:T(8,128)(2,1)}) custom-call(bf16[128,1152]{1,0:T(8,128)(2,1)} %get-tuple-element.42.refs_0_, f32[128,1152]{1,0:T(8,128)} %get-tuple-element.43.refs_1_, bf16[128,1152]{1,0:T(8,128)(2,1)} %bitcast.28, ...), custom_call_target="tpu_custom_call" | custom-call | bytes 300000000 | tf_op jit(solution)/shard_map/feed_forward/pallas_call | solution.py:733
  185.8 85.3 %backward.1 = (bf16[128,1152]{1,0:T(8,128)(2,1)}, bf16[8,2,32,1152]{3,2,1,0:T(8,128)(2,1)}, f32[16,8,256]{2,1,0:T(8,128)}, bf16[16,96,1152]{2,1,0:T(8,128)(2,1)}, bf16[16,80,1152]{2,1,0:T(8,128)(2,1)}) custom-call(f32[128,1152]{1,0:T(8,128)} %get-tuple-element.48.refs_0_, f32[128,1152]{1,0:T(8,128)} %get-tuple-element.43.refs_1_, ...), custom_call_target="tpu_custom_call" | custom-call | bytes 240000000 | tf_op jit(solution)/shard_map/backward/pallas_call | solution.py:733
  271.0 0.0 copy-start
  271.1 0.0 copy-start.1
  271.1 9.5 %widen.1 = (f32[864,2,1152]{2,1,0:T(2,128)}, f32[864,1152]{1,0:T(8,128)}, f32[192,1152]{1,0:T(8,128)}, f32[128,1152]{1,0:T(8,128)}, f32[4,144]{1,0:T(4,128)}, /*index=5*/f32[2,32]{1,0:T(2,128)}) custom-call(bf16[1536,1152]{1,0:T(8,128)(2,1)} %bitcast.19, bf16[1536,1152]{1,0:T(8,128)(2,1)} %bitcast.20, bf16[1536,1152]{1,0:T(8,128)(2,1)} %bitcast.21, ...), custom_call_target="tpu_custom_call" | custom-call | bytes 27000000 | tf_op jit(solution)/shard_map/widen/pallas_call | solution.py:809
  280.6 0.0 copy-done
  280.6 0.7 copy.18
  281.3 0.0 copy-done.1
  281.3 0.7 copy.19
Async XLA Ops:
  271.0 9.5 %copy-start = (bf16[128,1152]{1,0:T(8,128)(2,1)S(1)}, bf16[128,1152]{1,0:T(8,128)(2,1)}, u32[]{:S(2)}) copy-start(bf16[128,1152]{1,0:T(8,128)(2,1)} %get-tuple-element.47) | copy-start | bytes 884740
  271.1 10.3 %copy-start.1 = (bf16[128,1152]{1,0:T(8,128)(2,1)S(1)}, bf16[128,1152]{1,0:T(8,128)(2,1)}, u32[]{:S(2)}) copy-start(bf16[128,1152]{1,0:T(8,128)(2,1)} %get-tuple-element.65) | copy-start | bytes 884740
